TPU v7x, 32 devices: a whole 2x2x4 slice. The times are simulated.
32 devices in a mesh: seq: 8 (over z, x), rep: 4 (over y, core).
Axes of the slice: x: 2, y: 2, z: 4, core: 2. Of those that a mesh axis runs over, the one named last changes fastest.
Arguments:
- tokens: bfloat16 [4096, 1024], P(('seq', 'rep')), may hold values from -40 to 40
- cotangent: bfloat16 [4096, 1024], P(('seq', 'rep')), may hold values from -6 to 6
- lengths: int32 [2], replicated, may hold values from 256 to 2048, as said below
- in_weight: bfloat16 [1, 1024, 3, 1024], P(None, 'seq', None, 'rep'), may hold values from -0.1875 to 0.1875
- in_bias: float32 [1, 3, 1024], replicated, may hold values from -2 to 2
- short_taps: float32 [1, 3, 3, 1024], replicated, may hold values from -1 to 1
- short_bias: float32 [1, 3, 1024], replicated, may hold values from -1.5 to 1.5
- feat_weight: float32 [1, 33, 64], replicated, may hold values from -1 to 1
- feat_bias: float32 [1, 64], replicated, may hold values from -4 to 4
- inner_weight: float32 [1, 64, 64], replicated, may hold values from -0.75 to 0.75
- inner_bias: float32 [1, 64], replicated, may hold values from -3 to 3
- deep_weight: float32 [1, 64, 64], replicated, may hold values from -0.75 to 0.75
- deep_bias: float32 [1, 64], replicated, may hold values from -3 to 3
- sine_freq: float32 [1, 64], replicated, may hold values from 0.5 to 1.5
- kernel_weight: float32 [1, 64, 1024], replicated, may hold values from -0.078125 to 0.078125
- skip_gain: float32 [1, 1024], replicated, may hold values from -4 to 4
- out_weight: bfloat16 [1, 1024, 1024], P(None, 'seq', 'rep'), may hold values from -0.1875 to 0.1875
- out_bias: float32 [1, 1024], replicated, may hold values from -1.5 to 1.5
- norm1_gain: float32 [1, 1024], replicated, may hold values from 0.5 to 1.5
- norm1_shift: float32 [1, 1024], replicated, may hold values from -1.5 to 1.5
- norm2_gain: float32 [1, 1024], replicated, may hold values from 0.5 to 1.5
- norm2_shift: float32 [1, 1024], replicated, may hold values from -1.5 to 1.5
- up_weight: bfloat16 [1, 1024, 4096], P(None, 'seq', 'rep'), may hold values from -0.1875 to 0.1875
- up_bias: float32 [1, 4096], replicated, may hold values from -2 to 2
- down_weight: bfloat16 [1, 1024, 4096], P(None, 'seq', 'rep'), may hold values from -0.125 to 0.125
- down_bias: float32 [1, 1024], replicated, may hold values from -1.5 to 1.5
Outputs:
- layer_out: bfloat16 [4096, 1024], P(('seq', 'rep'))
- grad_tokens: float32 [4096, 1024], P(('seq', 'rep'))
- grad_in_weight: float32 [1, 1024, 3, 1024], P(None, 'seq', None, 'rep')
- grad_in_bias: float32 [1, 3, 1024], replicated
- grad_short_taps: float32 [1, 3, 3, 1024], replicated
- grad_short_bias: float32 [1, 3, 1024], replicated
- grad_feat_weight: float32 [1, 33, 64], replicated
- grad_feat_bias: float32 [1, 64], replicated
- grad_inner_weight: float32 [1, 64, 64], replicated
- grad_inner_bias: float32 [1, 64], replicated
- grad_deep_weight: float32 [1, 64, 64], replicated
- grad_deep_bias: float32 [1, 64], replicated
- grad_sine_freq: float32 [1, 64], replicated
- grad_kernel_weight: float32 [1, 64, 1024], replicated
- grad_skip_gain: float32 [1, 1024], replicated
- grad_out_weight: float32 [1, 1024, 1024], P(None, 'seq', 'rep')
- grad_out_bias: float32 [1, 1024], replicated
- grad_norm1_gain: float32 [1, 1024], replicated
- grad_norm1_shift: float32 [1, 1024], replicated
- grad_norm2_gain: float32 [1, 1024], replicated
- grad_norm2_shift: float32 [1, 1024], replicated
- grad_up_weight: float32 [1, 1024, 4096], P(None, 'seq', 'rep')
- grad_up_bias: float32 [1, 4096], replicated
- grad_down_weight: float32 [1, 1024, 4096], P(None, 'seq', 'rep')
- grad_down_bias: float32 [1, 1024], replicated
Inputs may be any that keep to these rules, and one draw needn't show every extreme that they name: lengths[0] is 2048; lengths[1] lies between 256 and 512.
All inputs are finite; a program needn't handle non-finite values.
Results may differ from a plain program's by a relative error of at most 0.017.
Values may be sent and summed in bfloat16 or wider, within the bound.
No kernel may reach another device: no remote copies, remote signals or barrier semaphores. Data moves between devices by JAX's collectives and lax.ppermute only.
A program may use at most 192 MiB of HBM per device.

v0:
```python
from functools import partial
import math

import jax
import jax.numpy as jnp
from jax import lax
from jax.sharding import PartitionSpec as P

EPS = 1e-05
HIGH = lax.Precision.HIGHEST
F32 = jnp.float32
B16 = jnp.bfloat16


def gather_rows(values):
    return lax.all_gather(values, "rep", axis=0, tiled=True)


def sum_rows(partial_rows):
    return lax.psum_scatter(
        partial_rows.astype(jnp.bfloat16), "rep", scatter_dimension=0, tiled=True
    ).astype(jnp.float32)


def gather_weights(in_shard, out_shard, up_shard, down_shard):
    return (
        lax.all_gather(in_shard, "seq", axis=0, tiled=True),
        lax.all_gather(out_shard, "seq", axis=0, tiled=True),
        lax.all_gather(up_shard, "seq", axis=0, tiled=True),
        lax.all_gather(down_shard, "seq", axis=0, tiled=True),
    )


def layer_norm(rows, gain, shift):
    row_mean = jnp.mean(rows, axis=-1, keepdims=True)
    centred = rows - row_mean
    variance = jnp.mean(centred * centred, axis=-1, keepdims=True)
    inverse = lax.rsqrt(variance + EPS)
    normed = centred * inverse
    return (normed * gain + shift, normed, inverse)


def norm_back(grad_rows, normed, inverse, gain):
    scaled = grad_rows * gain
    mean_one = jnp.mean(scaled, axis=-1, keepdims=True)
    mean_two = jnp.mean(scaled * normed, axis=-1, keepdims=True)
    grad_in = inverse * (scaled - mean_one - normed * mean_two)
    return (grad_in, jnp.sum(grad_rows * normed, axis=0), jnp.sum(grad_rows, axis=0))


def features(length, feat_count):
    ramp_unit = jnp.linspace(0.0, 1.0, length, dtype=F32)
    angles = jnp.arange(length, dtype=F32)[:, None] * (2.0 * math.pi / length)
    band_freqs = jnp.linspace(
        0.0001, (feat_count - 1) // 2 - 1.0, (feat_count - 1) // 2, dtype=F32
    )[None, :]
    phase_grid = band_freqs * angles
    grid_out = jnp.concatenate(
        [ramp_unit[:, None], jnp.cos(phase_grid), -jnp.sin(phase_grid)], axis=1
    )
    return (grid_out, ramp_unit)


def filter_columns(
    feature_grid,
    ramp_unit,
    start_chan,
    chan_count,
    model_width,
    feat_weight,
    feat_bias,
    inner_weight,
    inner_bias,
    deep_weight,
    deep_bias,
    sine_freq,
    columns,
):
    hidden = jnp.sin(sine_freq * (jnp.dot(feature_grid, feat_weight, precision=HIGH) + feat_bias))
    hidden = jnp.sin(sine_freq * (jnp.dot(hidden, inner_weight, precision=HIGH) + inner_bias))
    hidden = jnp.sin(sine_freq * (jnp.dot(hidden, deep_weight, precision=HIGH) + deep_bias))
    deltas = jnp.abs(
        jnp.linspace(math.log(0.01) / 0.3, math.log(0.01) / 1.5, model_width, dtype=F32)
    )
    local_rates = lax.dynamic_slice_in_dim(deltas, start_chan, chan_count)
    return jnp.dot(hidden, columns, precision=HIGH).T * jnp.exp(
        -ramp_unit[None, :] * local_rates[:, None]
    )


def split_size(size_total):
    outer_size = 2
    for candidate in range(2, math.isqrt(size_total) + 1, 2):
        if size_total % candidate == 0:
            outer_size = candidate
    return (outer_size, size_total // outer_size)


def angle_table(row_count, col_count, period):
    product = (
        jnp.arange(row_count, dtype=jnp.int32)[:, None]
        * jnp.arange(col_count, dtype=jnp.int32)[None, :]
        % period
    )
    angles = product.astype(F32) * (-2.0 * math.pi / period)
    return (jnp.cos(angles), jnp.sin(angles))


def dft_tables(size_total):
    outer_size, inner_size = split_size(size_total)
    outer_cos, outer_sin = angle_table(outer_size, outer_size, outer_size)
    twist_cos, twist_sin = angle_table(outer_size, inner_size, size_total)
    inner_cos, inner_sin = angle_table(inner_size, inner_size, inner_size)
    return (outer_cos, outer_sin, twist_cos, twist_sin, inner_cos, inner_sin)


def forward_dft(signal, tables):
    outer_cos, outer_sin, twist_cos, twist_sin, inner_cos, inner_sin = tables
    outer_size, inner_size = twist_cos.shape
    half_rows = outer_size // 2
    shaped = signal.reshape(signal.shape[:-1] + (half_rows, inner_size))
    real_part = jnp.einsum("kn,...nb->...kb", outer_cos[:, :half_rows], shaped, precision=HIGH)
    imag_part = jnp.einsum("kn,...nb->...kb", outer_sin[:, :half_rows], shaped, precision=HIGH)
    real_turn = real_part * twist_cos - imag_part * twist_sin
    imag_turn = real_part * twist_sin + imag_part * twist_cos
    out_real = jnp.matmul(real_turn, inner_cos, precision=HIGH) - jnp.matmul(
        imag_turn, inner_sin, precision=HIGH
    )
    out_imag = jnp.matmul(real_turn, inner_sin, precision=HIGH) + jnp.matmul(
        imag_turn, inner_cos, precision=HIGH
    )
    return (out_real, out_imag)


def inverse_dft(real_in, imag_in, tables):
    outer_cos, outer_sin, twist_cos, twist_sin, inner_cos, inner_sin = tables
    outer_size, inner_size = twist_cos.shape
    half_rows = outer_size // 2
    real_mid = jnp.matmul(real_in, inner_cos, precision=HIGH) + jnp.matmul(
        imag_in, inner_sin, precision=HIGH
    )
    imag_mid = jnp.matmul(imag_in, inner_cos, precision=HIGH) - jnp.matmul(
        real_in, inner_sin, precision=HIGH
    )
    real_turn = real_mid * twist_cos + imag_mid * twist_sin
    imag_turn = imag_mid * twist_cos - real_mid * twist_sin
    result = (
        jnp.einsum("nk,...kb->...nb", outer_cos[:half_rows], real_turn, precision=HIGH)
        + jnp.einsum("nk,...kb->...nb", outer_sin[:half_rows], imag_turn, precision=HIGH)
    ) / (outer_size * inner_size)
    return result.reshape(result.shape[:-2] + (half_rows * inner_size,))


def mixer_forward(received, tap_weights, tap_bias, skip_local, kernel, item_mask, tables):
    chan_count = received.shape[1]
    seq_len = received.shape[2] // 2
    signal = received.astype(F32).reshape(3, chan_count, 2, seq_len)
    padded = jnp.pad(signal, ((0, 0), (0, 0), (0, 0), (2, 0)))
    shorted = (
        tap_weights[0][:, :, None, None] * padded[..., :seq_len]
        + tap_weights[1][:, :, None, None] * padded[..., 1 : seq_len + 1]
        + tap_weights[2][:, :, None, None] * signal
        + tap_bias[:, :, None, None]
    )
    gated_in = shorted[2] * shorted[1] * item_mask
    gated_real, gated_imag = forward_dft(gated_in, tables)
    kernel_real, kernel_imag = forward_dft(kernel, tables)
    kernel_real = kernel_real[:, None]
    kernel_imag = kernel_imag[:, None]
    convolved = inverse_dft(
        gated_real * kernel_real - gated_imag * kernel_imag,
        gated_real * kernel_imag + gated_imag * kernel_real,
        tables,
    )
    mixed_sum = convolved + skip_local[:, None, None] * gated_in
    output = shorted[0] * mixed_sum
    return (
        output,
        (
            signal,
            padded,
            shorted,
            gated_in,
            gated_real,
            gated_imag,
            kernel_real,
            kernel_imag,
            mixed_sum,
        ),
    )


def mixer_backward(grad_out, kept_mix, tap_weights, skip_local, item_mask, tables):
    (
        signal,
        padded,
        shorted,
        gated_in,
        gated_real,
        gated_imag,
        kernel_real,
        kernel_imag,
        mixed_sum,
    ) = kept_mix
    seq_len = signal.shape[3]
    grad_mixed = grad_out * shorted[0]
    grad_gate_out = grad_out * mixed_sum
    grad_real, grad_imag = forward_dft(grad_mixed, tables)
    grad_gated = (
        inverse_dft(
            grad_real * kernel_real + grad_imag * kernel_imag,
            grad_imag * kernel_real - grad_real * kernel_imag,
            tables,
        )
        + skip_local[:, None, None] * grad_mixed
    )
    grad_skip = jnp.sum(grad_mixed * gated_in, axis=(1, 2))
    cross_real = jnp.sum(grad_real * gated_real + grad_imag * gated_imag, axis=1)
    cross_imag = jnp.sum(grad_imag * gated_real - grad_real * gated_imag, axis=1)
    grad_kernel = inverse_dft(cross_real, cross_imag, tables)
    masked = grad_gated * item_mask
    grad_short = jnp.stack([grad_gate_out, masked * shorted[2], masked * shorted[1]])
    next_one = jnp.pad(grad_short[..., 1:], ((0, 0), (0, 0), (0, 0), (0, 1)))
    next_two = jnp.pad(grad_short[..., 2:], ((0, 0), (0, 0), (0, 0), (0, 2)))
    grad_signal = (
        tap_weights[2][:, :, None, None] * grad_short
        + tap_weights[1][:, :, None, None] * next_one
        + tap_weights[0][:, :, None, None] * next_two
    )
    grad_taps = jnp.stack(
        [
            jnp.sum(grad_short * padded[..., :seq_len], axis=(2, 3)),
            jnp.sum(grad_short * padded[..., 1 : seq_len + 1], axis=(2, 3)),
            jnp.sum(grad_short * signal, axis=(2, 3)),
        ]
    )
    grad_tap_bias = jnp.sum(grad_short, axis=(2, 3))
    return (grad_signal, grad_taps, grad_tap_bias, grad_skip, grad_kernel)


def place_block(block_values, full_shape, start_at, axis_pos):
    return lax.dynamic_update_slice_in_dim(
        jnp.zeros(full_shape, F32), block_values, start_at, axis_pos
    )


def per_device(
    tokens,
    cotangent,
    lengths,
    in_weight,
    in_bias,
    short_taps,
    short_bias,
    feat_weight,
    feat_bias,
    inner_weight,
    inner_bias,
    deep_weight,
    deep_bias,
    sine_freq,
    kernel_weight,
    skip_gain,
    out_weight,
    out_bias,
    norm1_gain,
    norm1_shift,
    norm2_gain,
    norm2_shift,
    up_weight,
    up_bias,
    down_weight,
    down_bias,
):
    seq_count = lax.axis_size("seq")
    rep_count = lax.axis_size("rep")
    seq_index = lax.axis_index("seq")
    rep_index = lax.axis_index("rep")
    tok_rows, model_width = tokens.shape
    layer_count = in_weight.shape[0]
    device_count = seq_count * rep_count
    whole_count = tok_rows * device_count
    seq_len = whole_count // 2
    chan_count = model_width // device_count
    block_width = model_width // rep_count
    hidden_block = up_weight.shape[2]
    hidden_full = hidden_block * rep_count
    block_start = rep_index * block_width
    chan_start = block_start + seq_index * chan_count
    hidden_start = rep_index * hidden_block
    tables = dft_tables(2 * seq_len)
    feature_grid, ramp_unit = features(seq_len, feat_weight.shape[1])
    row_ids = (seq_index * rep_count + rep_index) * tok_rows + jnp.arange(tok_rows, dtype=jnp.int32)
    limits = jnp.where(row_ids // seq_len == 0, lengths[0], lengths[1])
    row_mask = (row_ids % seq_len < limits).astype(F32)[:, None]
    item_mask = (jnp.arange(seq_len, dtype=jnp.int32)[None, :] < lengths[:, None]).astype(F32)
    gelu_exact = partial(jax.nn.gelu, approximate=False)
    residual = tokens.astype(F32)
    layer_idx = 0
    full_in, full_out, full_up, full_down = gather_weights(
        in_weight[layer_idx], out_weight[layer_idx], up_weight[layer_idx], down_weight[layer_idx]
    )
    normed_one, unit_one, scale_one = layer_norm(
        residual, norm1_gain[layer_idx], norm1_shift[layer_idx]
    )
    rows_one = gather_rows(normed_one.astype(B16))
    proj_bias = lax.dynamic_slice_in_dim(in_bias[layer_idx], block_start, block_width, 1)
    projected = (
        jnp.einsum("td,dpc->pct", rows_one, full_in, preferred_element_type=F32)
        + proj_bias[:, :, None]
    )
    received = lax.all_to_all(projected.astype(B16), "seq", split_axis=1, concat_axis=2, tiled=True)
    tap_weights = lax.dynamic_slice_in_dim(short_taps[layer_idx], chan_start, chan_count, 2)
    tap_bias = lax.dynamic_slice_in_dim(short_bias[layer_idx], chan_start, chan_count, 1)
    skip_local = lax.dynamic_slice_in_dim(skip_gain[layer_idx], chan_start, chan_count, 0)
    columns = lax.dynamic_slice_in_dim(kernel_weight[layer_idx], chan_start, chan_count, 1)
    kernel_fn = partial(
        filter_columns, feature_grid, ramp_unit, chan_start, chan_count, model_width
    )
    kernel, kernel_pull = jax.vjp(
        kernel_fn,
        feat_weight[layer_idx],
        feat_bias[layer_idx],
        inner_weight[layer_idx],
        inner_bias[layer_idx],
        deep_weight[layer_idx],
        deep_bias[layer_idx],
        sine_freq[layer_idx],
        columns,
    )
    mixed_out, kept_mix = mixer_forward(
        received, tap_weights, tap_bias, skip_local, kernel, item_mask, tables
    )
    rows_mixed = lax.all_to_all(
        mixed_out.reshape(chan_count, whole_count).astype(B16),
        "seq",
        split_axis=1,
        concat_axis=0,
        tiled=True,
    )
    mixed_part = jnp.einsum("ct,oc->to", rows_mixed, full_out, preferred_element_type=F32)
    middle = residual + (sum_rows(mixed_part) + out_bias[layer_idx])
    normed_two, unit_two, scale_two = layer_norm(
        middle, norm2_gain[layer_idx], norm2_shift[layer_idx]
    )
    rows_two = gather_rows(normed_two.astype(B16))
    up_block = lax.dynamic_slice_in_dim(up_bias[layer_idx], hidden_start, hidden_block, 0)
    pre_act = jnp.dot(rows_two, full_up, preferred_element_type=F32) + up_block
    activated, gelu_pull = jax.vjp(gelu_exact, pre_act)
    act_rows = activated.astype(B16)
    mlp_part = jnp.einsum("tf,of->to", act_rows, full_down, preferred_element_type=F32)
    residual = middle + (sum_rows(mlp_part) + down_bias[layer_idx])
    saved_layers = [
        (
            (full_in, full_out, full_up, full_down),
            unit_one,
            scale_one,
            rows_one,
            kept_mix,
            kernel_pull,
            tap_weights,
            skip_local,
            rows_mixed,
            unit_two,
            scale_two,
            rows_two,
            gelu_pull,
            act_rows,
        )
    ]
    layer_out = residual.astype(B16)
    grad_resid = cotangent.astype(F32) * row_mask
    small_terms = [None] * layer_count
    large_terms = [None] * layer_count
    for layer_idx in reversed(range(layer_count)):
        (
            kept_weights,
            unit_one,
            scale_one,
            rows_one,
            kept_mix,
            kernel_pull,
            tap_weights,
            skip_local,
            rows_mixed,
            unit_two,
            scale_two,
            rows_two,
            gelu_pull,
            act_rows,
        ) = saved_layers[layer_idx]
        full_in, full_out, full_up, full_down = (
            lax.all_gather(in_weight[layer_idx], "seq", axis=0, tiled=True),
            lax.all_gather(out_weight[layer_idx], "seq", axis=0, tiled=True),
            lax.all_gather(up_weight[layer_idx], "seq", axis=0, tiled=True),
            lax.all_gather(down_weight[layer_idx], "seq", axis=0, tiled=True),
        )
        grad_mlp = grad_resid.astype(B16)
        grad_down_bias = jnp.sum(grad_mlp.astype(F32), axis=0)
        mlp_rows = gather_rows(grad_mlp)
        grad_act = jnp.dot(mlp_rows, full_down, preferred_element_type=F32)
        term_down = jnp.einsum("to,tf->of", mlp_rows, act_rows, preferred_element_type=F32)
        grad_pre = gelu_pull(grad_act)[0].astype(B16)
        grad_up_block = jnp.sum(grad_pre.astype(F32), axis=0)
        term_up = jnp.einsum("td,tf->df", rows_two, grad_pre, preferred_element_type=F32)
        grad_two = sum_rows(jnp.einsum("tf,df->td", grad_pre, full_up, preferred_element_type=F32))
        grad_unit_two, grad_gain_two, grad_shift_two = norm_back(
            grad_two, unit_two, scale_two, norm2_gain[layer_idx]
        )
        grad_middle = grad_resid + grad_unit_two
        grad_mix = grad_middle.astype(B16)
        grad_out_bias = jnp.sum(grad_mix.astype(F32), axis=0)
        mix_rows = gather_rows(grad_mix)
        grad_mixed = jnp.einsum("to,oc->ct", mix_rows, full_out, preferred_element_type=F32).astype(
            B16
        )
        term_out = jnp.einsum("to,ct->oc", mix_rows, rows_mixed, preferred_element_type=F32)
        grad_chan = lax.all_to_all(grad_mixed, "seq", split_axis=0, concat_axis=1, tiled=True)
        grad_signal, grad_taps, grad_tap_bias, grad_skip, grad_kernel = mixer_backward(
            grad_chan.astype(F32).reshape(chan_count, 2, seq_len),
            kept_mix,
            tap_weights,
            skip_local,
            item_mask,
            tables,
        )
        kernel_grads = kernel_pull(grad_kernel)
        grad_proj = lax.all_to_all(
            grad_signal.reshape(3, chan_count, whole_count).astype(B16),
            "seq",
            split_axis=2,
            concat_axis=1,
            tiled=True,
        )
        grad_proj_bias = jnp.sum(grad_proj.astype(F32), axis=2)
        term_in = jnp.einsum("td,pct->dpc", rows_one, grad_proj, preferred_element_type=F32)
        grad_one = sum_rows(
            jnp.einsum("pct,dpc->td", grad_proj, full_in, preferred_element_type=F32)
        )
        grad_unit_one, grad_gain_one, grad_shift_one = norm_back(
            grad_one, unit_one, scale_one, norm1_gain[layer_idx]
        )
        grad_resid = grad_middle + grad_unit_one
        large_terms[layer_idx] = (term_in, term_out, term_up, term_down)
        small_terms[layer_idx] = (
            place_block(grad_proj_bias, (3, model_width), block_start, 1),
            place_block(grad_taps, (3, 3, model_width), chan_start, 2),
            place_block(grad_tap_bias, (3, model_width), chan_start, 1),
            kernel_grads[0],
            kernel_grads[1],
            kernel_grads[2],
            kernel_grads[3],
            kernel_grads[4],
            kernel_grads[5],
            kernel_grads[6],
            place_block(kernel_grads[7], (kernel_grads[7].shape[0], model_width), chan_start, 1),
            place_block(grad_skip, (model_width,), chan_start, 0),
            grad_out_bias,
            grad_gain_one,
            grad_shift_one,
            grad_gain_two,
            grad_shift_two,
            place_block(grad_up_block, (hidden_full,), hidden_start, 0),
            grad_down_bias,
        )
    stacked = [jnp.stack([small_terms[0][pos]]) for pos in range(19)]
    summed = lax.psum(
        (
            stacked[0],
            stacked[1],
            stacked[2],
            stacked[3],
            stacked[4],
            stacked[5],
            stacked[6],
            stacked[7],
            stacked[8],
            stacked[9],
            stacked[10],
            stacked[11],
            stacked[12],
            stacked[13],
            stacked[14],
            stacked[15],
            stacked[16],
            stacked[17],
            stacked[18],
        ),
        ("seq", "rep"),
    )
    large_stacked = [jnp.stack([large_terms[0][pos]]) for pos in range(4)]
    large_stacked = list(
        (
            lax.psum_scatter(large_stacked[0], "seq", scatter_dimension=1, tiled=True),
            lax.psum_scatter(large_stacked[1], "seq", scatter_dimension=1, tiled=True),
            lax.psum_scatter(large_stacked[2], "seq", scatter_dimension=1, tiled=True),
            lax.psum_scatter(large_stacked[3], "seq", scatter_dimension=1, tiled=True),
        )
    )
    return (
        layer_out,
        grad_resid,
        large_stacked[0],
        summed[0],
        summed[1],
        summed[2],
        summed[3],
        summed[4],
        summed[5],
        summed[6],
        summed[7],
        summed[8],
        summed[9],
        summed[10],
        summed[11],
        large_stacked[1],
        summed[12],
        summed[13],
        summed[14],
        summed[15],
        summed[16],
        large_stacked[2],
        summed[17],
        large_stacked[3],
        summed[18],
    )


def solution(mesh):
    return jax.shard_map(
        per_device,
        mesh=mesh,
        in_specs=(
            P(("seq", "rep"), None),
            P(("seq", "rep"), None),
            P(),
            P(None, "seq", None, "rep"),
            P(),
            P(),
            P(),
            P(),
            P(),
            P(),
            P(),
            P(),
            P(),
            P(),
            P(),
            P(),
            P(None, "seq", "rep"),
            P(),
            P(),
            P(),
            P(),
            P(),
            P(None, "seq", "rep"),
            P(),
            P(None, "seq", "rep"),
            P(),
        ),
        out_specs=(
            P(("seq", "rep"), None),
            P(("seq", "rep"), None),
            P(None, "seq", None, "rep"),
            P(),
            P(),
            P(),
            P(),
            P(),
            P(),
            P(),
            P(),
            P(),
            P(),
            P(),
            P(),
            P(None, "seq", "rep"),
            P(),
            P(),
            P(),
            P(),
            P(),
            P(None, "seq", "rep"),
            P(),
            P(None, "seq", "rep"),
            P(),
        ),
        check_vma=False,
    )
```

profile of v0, /device:TPU:0, one launch (start us, length us, event | category | flops | bytes accessed | tf_op | source)
XLA Modules:
  0.0 1359.7 jit_solution(17252552228061522835)
XLA Ops:
  33.4 44.1 %all-gather.20.cloned.1.call-done = bf16[1,1024,3,256]{3,1,2,0:T(8,128)(2,1)} async-done(((bf16[1,128,3,256]{3,1,2,0:T(8,128)(2,1)}), bf16[1,1024,3,256]{3,1,2,0:T(8,128)(2,1)}) %all-gather.20.cloned.1.call-update) | async-done | bytes 1572880 | tf_op jit(solution)/shard_map/all_gather | solution.py:27
  96.3 15.5 %all-to-all-done = bf16[3,256,512]{2,0,1:T(4,128)(2,1)} async-done(((bf16[3,256,512]{2,0,1:T(4,128)(2,1)}), bf16[3,256,512]{2,0,1:T(4,128)(2,1)}, u32[]{:S(2)}, u32[]{:S(2)}) %all-to-all-start) | async-done | bytes 786464 | tf_op jit(solution)/shard_map/all_to_all | solution.py:312
  119.8 16.3 %add_add_fusion = f32[3,32,2,2048]{3,2,1,0:T(2,128)S(1)} fusion(f32[3,32,2,2048]{3,2,1,0:T(2,128)} %reshape.454, f32[3,32]{1,0:T(4,128)S(1)} %bitcast.409, f32[3,32]{1,0:T(4,128)S(1)} %copy-done.62, f32[3,32]{1,0:T(4,128)S(1)} %copy-done.64, f32[3,32]{1,0:T(4,128)S(1)} %bitcast.398), kind=kLoop, calls=%fused_computation.90 | loop fusion | flops 2359296 | bytes 3147264 | tf_op jit(solution)/shard_map/add | solution.py:160
  164.7 7.8 fusion.205
  172.4 7.6 fusion.207
  182.3 9.2 convolution_subtract_fusion.2
  191.5 6.4 convolution_add_fusion.5
  203.7 6.8 fusion.63
  219.4 36.4 %all-gather.1 = bf16[1,1024,256]{2,1,0:T(8,128)(2,1)} all-gather(bf16[1,128,256]{2,1,0:T(8,128)(2,1)} %param.42), channel_id=3, replica_groups=mesh['seq'=8,'rep'=4] {'seq'}, dimensions={1}, use_global_device_ids=true | all-gather | bytes 589824 | tf_op jit(solution)/shard_map/all_gather | solution.py:28
  259.1 22.9 %reduce-scatter.9.cloned.1.call-done = bf16[128,1024]{1,0:T(8,128)(2,1)} async-done(((bf16[512,1024]{1,0:T(8,128)(2,1)}), bf16[128,1024]{1,0:T(8,128)(2,1)}) %reduce-scatter.9.cloned.1.call-update) | async-done | bytes 262160 | tf_op jit(solution)/shard_map/reduce_scatter | solution.py:20
  292.5 41.1 %all-gather.22.cloned.1.call-done = bf16[1,1024,1024]{2,1,0:T(8,128)(2,1)} async-done(((bf16[1,128,1024]{2,1,0:T(8,128)(2,1)}), bf16[1,1024,1024]{2,1,0:T(8,128)(2,1)}) %all-gather.22.cloned.1.call-update) | async-done | bytes 2097168 | tf_op jit(solution)/shard_map/all_gather | solution.py:29
  333.6 17.3 %all-gather.14.cloned.1.call-done = bf16[512,1024]{1,0:T(8,128)(2,1)} async-done(((bf16[128,1024]{1,0:T(8,128)(2,1)}), bf16[512,1024]{1,0:T(8,128)(2,1)}) %all-gather.14.cloned.1.call-update) | async-done | bytes 1048592 | tf_op jit(solution)/shard_map/all_gather | solution.py:16
  351.0 9.2 multiply_convert_fusion
  360.1 9.7 all-gather.16.cloned.1.call-done
  369.8 51.7 %all-gather.24.cloned.1.call-done = bf16[1,1024,1024]{2,1,0:T(8,128)(2,1)} async-done(((bf16[1,128,1024]{2,1,0:T(8,128)(2,1)}), bf16[1,1024,1024]{2,1,0:T(8,128)(2,1)}) %all-gather.24.cloned.1.call-update) | async-done | bytes 2097168 | tf_op jit(solution)/shard_map/all_gather | solution.py:30
  434.9 19.2 %reduce-scatter.13.cloned.1.call-done = bf16[128,1024]{1,0:T(8,128)(2,1)} async-done(((bf16[512,1024]{1,0:T(8,128)(2,1)}), bf16[128,1024]{1,0:T(8,128)(2,1)}) %reduce-scatter.13.cloned.1.call-update) | async-done | bytes 262160 | tf_op jit(solution)/shard_map/reduce_scatter | solution.py:20
  457.0 24.5 %reduce-scatter.11.cloned.1.call-done = bf16[128,1024]{1,0:T(8,128)(2,1)} async-done(((bf16[512,1024]{1,0:T(8,128)(2,1)}), bf16[128,1024]{1,0:T(8,128)(2,1)}) %reduce-scatter.11.cloned.1.call-update) | async-done | bytes 262160 | tf_op jit(solution)/shard_map/reduce_scatter | solution.py:20
  485.4 16.1 %all-gather.18.cloned.1.call-done = bf16[512,1024]{1,0:T(8,128)(2,1)} async-done(((bf16[128,1024]{1,0:T(8,128)(2,1)}), bf16[512,1024]{1,0:T(8,128)(2,1)}) %all-gather.18.cloned.1.call-update) | async-done | bytes 1048592 | tf_op jit(solution)/shard_map/all_gather | solution.py:16
  552.7 6.3 fusion.199
  565.2 6.3 convolution_subtract_fusion
  571.4 6.4 convolution_add_fusion.3
  583.7 6.8 fusion.57
  601.5 9.2 multiply_reduce_fusion.1
  622.8 7.1 copy.451
  629.9 7.3 reshape.508
  664.4 6.8 reshape.509
  729.6 138.6 %all-reduce.9.cloned.1.call-done = (f32[1,3,1024]{2,0,1:T(1,128)}, f32[1,3,3,1024]{3,0,2,1:T(1,128)}, f32[1,3,1024]{2,0,1:T(1,128)}, f32[1,33,64]{2,1,0:T(8,128)...) async-done(((f32[1,3,1024]{2,0,1:T(1,128)}, ...) | async-done | bytes 148752 | tf_op jit(solution)/shard_map/psum | solution.py:467
  869.5 131.4 %all-reduce.7.cloned.1.call-done = f32[1,64,1024]{2,1,0:T(8,128)} async-done(((f32[1,64,1024]{2,1,0:T(8,128)}), f32[1,64,1024]{2,1,0:T(8,128)}) %all-reduce.7.cloned.1.call-update) | async-done | bytes 262160 | tf_op jit(solution)/shard_map/psum | solution.py:467
  1000.9 66.3 %reduce-scatter.19.cloned.1.call-done = f32[1,128,256]{2,1,0:T(8,128)} async-done(((f32[1,1024,256]{2,1,0:T(8,128)}), f32[1,128,256]{2,1,0:T(8,128)}) %reduce-scatter.19.cloned.1.call-update) | async-done | bytes 131088 | tf_op jit(solution)/shard_map/reduce_scatter | solution.py:495
  1067.2 91.4 %reduce-scatter.23.cloned.1.call-done = f32[1,128,1024]{2,1,0:T(8,128)} async-done(((f32[1,1024,1024]{2,1,0:T(8,128)}), f32[1,128,1024]{2,1,0:T(8,128)}) %reduce-scatter.23.cloned.1.call-update) | async-done | bytes 524304 | tf_op jit(solution)/shard_map/reduce_scatter | solution.py:497
  1158.6 91.9 %reduce-scatter.21.cloned.1.call-done = f32[1,128,1024]{2,1,0:T(8,128)} async-done(((f32[1,1024,1024]{2,1,0:T(8,128)}), f32[1,128,1024]{2,1,0:T(8,128)}) %reduce-scatter.21.cloned.1.call-update) | async-done | bytes 524304 | tf_op jit(solution)/shard_map/reduce_scatter | solution.py:496
  1250.6 79.1 %reduce-scatter.17.cloned.1.call-done = f32[1,128,3,256]{3,1,2,0:T(8,128)} async-done(((f32[1,1024,3,256]{3,1,2,0:T(8,128)}), f32[1,128,3,256]{3,1,2,0:T(8,128)}) %reduce-scatter.17.cloned.1.call-update) | async-done | bytes 393232 | tf_op jit(solution)/shard_map/reduce_scatter | solution.py:494
  (404 shorter events, 327.5 us)
Async XLA Ops:
  7.2 18.1 %copy-start = (f32[1,64,1024]{2,1,0:T(8,128)S(1)}, f32[1,64,1024]{2,1,0:T(8,128)}, u32[]{:S(2)}) copy-start(f32[1,64,1024]{2,1,0:T(8,128)} %param.40) | copy-start | bytes 786436
  7.3 14.9 %copy-start.46 = (f32[1,64,64]{2,1,0:T(8,128)S(1)}, f32[1,64,64]{2,1,0:T(8,128)}, u32[]{:S(2)}) copy-start(f32[1,64,64]{2,1,0:T(8,128)} %param.37) | copy-start | bytes 49156
  7.3 26.1 %all-gather.12.cloned.1.call-start = ((), (), s32[]{:S(2)}) async-start(), calls=%async_computation.12 | async-start | bytes 1310720 | tf_op jit(solution)/shard_map/all_gather | solution.py:16
  11.6 66.0 %all-gather.20.cloned.1.call-start = ((), (), s32[]{:S(2)}) async-start(), calls=%async_computation.25 | async-start | bytes 1769472 | tf_op jit(solution)/shard_map/all_gather | solution.py:27
  33.4 57.9 %copy-start.7 = (f32[32,64,64]{1,2,0:T(8,128)}, f32[32,64,64]{1,2,0:T(8,128)S(1)}, u32[]{:S(2)}) copy-start(f32[32,64,64]{1,2,0:T(8,128)S(1)} %convolution_bitcast_fusion.4) | copy-start | bytes 1572868
  82.0 29.9 %all-to-all-start = ((bf16[3,256,512]{2,0,1:T(4,128)(2,1)}), bf16[3,256,512]{2,0,1:T(4,128)(2,1)}, u32[]{:S(2)}, u32[]{:S(2)}) async-start(bf16[3,256,512]{2,0,1:T(4,128)(2,1)} %copy.280), calls=%async_computation | async-start | bytes 2097152 | tf_op jit(solution)/shard_map/all_to_all | solution.py:312
  215.8 66.2 %copy-start.8 = (bf16[128,1024]{1,0:T(8,128)(2,1)S(1)}, bf16[128,1024]{1,0:T(8,128)(2,1)}, u32[]{:S(2)}) copy-start(bf16[128,1024]{1,0:T(8,128)(2,1)} %param.26) | copy-start | bytes 786436
  215.8 66.2 %copy-start.48 = (f32[1,1024]{1,0:T(1,128)S(1)}, f32[1,1024]{1,0:T(1,128)}, u32[]{:S(2)}) copy-start(f32[1,1024]{1,0:T(1,128)} %param.43) | copy-start | bytes 12292
  215.8 40.0 %all-to-all-start.1 = ((bf16[32,8,512]{2,0,1:T(8,128)(2,1)}), bf16[32,8,512]{2,0,1:T(8,128)(2,1)S(1)}, u32[]{:S(2)}, u32[]{:S(2)}) async-start(bf16[32,8,512]{2,0,1:T(8,128)(2,1)} %fusion.131), calls=%async_computation.1 | async-start | bytes 524288 | tf_op jit(solution)/shard_map/all_to_all | solution.py:334
  219.3 62.7 %reduce-scatter.9.cloned.1.call-start = ((), (), s32[]{:S(2)}) async-start(), calls=%async_computation.13 | async-start | bytes 1310720 | tf_op jit(solution)/shard_map/reduce_scatter | solution.py:20
  255.8 28.5 %copy-start.27 = (bf16[32,8,512]{2,0,1:T(8,128)(2,1)}, bf16[32,8,512]{2,0,1:T(8,128)(2,1)S(1)}, u32[]{:S(2)}) copy-start(bf16[32,8,512]{2,0,1:T(8,128)(2,1)S(1)} %all-to-all-done.1) | copy-start | bytes 786436
  255.8 29.0 %copy-start.58 = (f32[1,1024]{1,0:T(1,128)S(1)}, f32[1,1024]{1,0:T(1,128)}, u32[]{:S(2)}) copy-start(f32[1,1024]{1,0:T(1,128)} %param.46) | copy-start | bytes 12292
  258.4 28.3 %copy-start.68 = (s32[2]{0:T(128)S(1)}, s32[2]{0:T(128)}, u32[]{:S(2)}) copy-start(s32[2]{0:T(128)} %param.28) | copy-start | bytes 28
  258.4 75.2 %all-gather.22.cloned.1.call-start = ((), (), s32[]{:S(2)}) async-start(), calls=%async_computation.26 | async-start | bytes 2359296 | tf_op jit(solution)/shard_map/all_gather | solution.py:29
  259.0 91.9 %all-gather.14.cloned.1.call-start = ((), (), s32[]{:S(2)}) async-start(), calls=%async_computation.14 | async-start | bytes 1310720 | tf_op jit(solution)/shard_map/all_gather | solution.py:16
  286.6 83.1 %all-gather.16.cloned.1.call-start = ((), (), s32[]{:S(2)}) async-start(), calls=%async_computation.16 | async-start | bytes 1310720 | tf_op jit(solution)/shard_map/all_gather | solution.py:16
  288.6 71.5 %copy-start.77 = (f32[128]{0:T(128)}, f32[128]{0:T(128)S(1)}, u32[]{:S(2)}) copy-start(f32[128]{0:T(128)S(1)} %compare_convert_fusion.3) | copy-start | bytes 1540
  291.0 130.4 %all-gather.24.cloned.1.call-start = ((), (), s32[]{:S(2)}) async-start(), calls=%async_computation.27 | async-start | bytes 2359296 | tf_op jit(solution)/shard_map/all_gather | solution.py:30
  291.8 162.3 %reduce-scatter.13.cloned.1.call-start = ((), (), s32[]{:S(2)}) async-start(), calls=%async_computation.17 | async-start | bytes 1310720 | tf_op jit(solution)/shard_map/reduce_scatter | solution.py:20
  430.5 51.0 %reduce-scatter.11.cloned.1.call-start = ((), (), s32[]{:S(2)}) async-start(), calls=%async_computation.15 | async-start | bytes 1310720 | tf_op jit(solution)/shard_map/reduce_scatter | solution.py:20
  430.6 23.5 %copy-start.24 = (bf16[128,1024]{1,0:T(8,128)(2,1)S(1)}, bf16[128,1024]{1,0:T(8,128)(2,1)}, u32[]{:S(2)}) copy-start(bf16[128,1024]{1,0:T(8,128)(2,1)} %reduce-scatter.9.cloned.1.call-done) | copy-start | bytes 786436
  430.6 23.5 %copy-start.76 = (f32[128]{0:T(128)S(1)}, f32[128]{0:T(128)}, u32[]{:S(2)}) copy-start(f32[128]{0:T(128)} %copy-done.75) | copy-start | bytes 1540
  434.8 66.6 %all-gather.18.cloned.1.call-start = ((), (), s32[]{:S(2)}) async-start(), calls=%async_computation.18 | async-start | bytes 1310720 | tf_op jit(solution)/shard_map/all_gather | solution.py:16
  504.0 14.8 %all-to-all-start.2 = ((bf16[8,32,512]{2,1,0:T(8,128)(2,1)}), bf16[8,32,512]{2,1,0:T(8,128)(2,1)S(1)}, u32[]{:S(2)}, u32[]{:S(2)}) async-start(bf16[8,32,512]{2,1,0:T(8,128)(2,1)} %bitcast.372), calls=%async_computation.5 | async-start | bytes 524288 | tf_op jit(solution)/shard_map/all_to_all | solution.py:418
  637.2 27.2 %all-to-all-start.3 = ((bf16[8,2,24576]{2,1,0:T(2,128)(2,1)}), bf16[8,2,24576]{2,1,0:T(2,128)(2,1)}, u32[]{:S(2)}, u32[]{:S(2)}) async-start(bf16[8,2,24576]{2,1,0:T(2,128)(2,1)} %reshape.508), calls=%async_computation.6 | async-start | bytes 1572864 | tf_op jit(solution)/shard_map/all_to_all | solution.py:428
  641.8 64.7 %reduce-scatter.15.cloned.1.call-start = ((), (), s32[]{:S(2)}) async-start(), calls=%async_computation.19 | async-start | bytes 1310720 | tf_op jit(solution)/shard_map/reduce_scatter | solution.py:20
  681.0 187.1 %all-reduce.9.cloned.1.call-start = ((), (), s32[]{:S(2)}) async-start(), calls=%async_computation.28 | async-start | bytes 389120 | tf_op jit(solution)/shard_map/psum | solution.py:467
  708.4 292.5 %all-reduce.7.cloned.1.call-start = ((), (), s32[]{:S(2)}) async-start(), calls=%async_computation.21 | async-start | bytes 524288 | tf_op jit(solution)/shard_map/psum | solution.py:467
  712.0 355.2 %reduce-scatter.19.cloned.1.call-start = ((), (), s32[]{:S(2)}) async-start(), calls=%async_computation.22 | async-start | bytes 1179648 | tf_op jit(solution)/shard_map/reduce_scatter | solution.py:495
  713.6 445.0 %reduce-scatter.23.cloned.1.call-start = ((), (), s32[]{:S(2)}) async-start(), calls=%async_computation.24 | async-start | bytes 4718592 | tf_op jit(solution)/shard_map/reduce_scatter | solution.py:497
  718.5 532.1 %reduce-scatter.21.cloned.1.call-start = ((), (), s32[]{:S(2)}) async-start(), calls=%async_computation.23 | async-start | bytes 4718592 | tf_op jit(solution)/shard_map/reduce_scatter | solution.py:496
  723.3 606.3 %reduce-scatter.17.cloned.1.call-start = ((), (), s32[]{:S(2)}) async-start(), calls=%async_computation.20 | async-start | bytes 3538944 | tf_op jit(solution)/shard_map/reduce_scatter | solution.py:494
  (81 other events, 427.6 us)
Sparse Core Ops, SparseCore 0:
  11.7 19.4 all-gather.11
  33.3 44.1 all-gather.19
  258.6 23.3 reduce-scatter.8
  284.2 49.4 all-gather.21
  335.7 15.2 all-gather.13
  353.0 16.7 all-gather.15
  372.1 49.2 all-gather.23
  430.6 23.3 reduce-scatter.12
  456.6 24.8 reduce-scatter.10
  484.7 16.6 all-gather.17
  681.1 25.3 reduce-scatter.14
  715.1 153.0 all-reduce.8
  874.2 126.6 all-reduce.6
  1004.7 62.4 reduce-scatter.18
  1071.7 86.8 reduce-scatter.22
  1162.7 87.8 reduce-scatter.20
  1255.0 74.5 reduce-scatter.16
where the time goes:
time: 1370 us; the launch traced here: 1360 us
  waiting for transfers between devices  867 us (63%)
  matrix products  236 us (17%)
  local copies, waits for them, and re-layouts  121 us (9%)
  other arithmetic  65.6 us (5%)
  blocking collectives  36.4 us (3%)
  starting transfers between devices  19.2 us (1%)
  between operations  15.6 us (1%)
    psum x2, waiting for transfers between devices, per_device(): lax.psum((stacked[0], stacked[1], stacked[2], stacked[3], stacked[4], sta...  270 us
    reduce_scatter x1, waiting for transfers between devices, per_device(): lax.psum_scatter(large_stacked[2], 'seq', scatter_dimension=1, tiled=True)  91.9 us
    reduce_scatter x1, waiting for transfers between devices, per_device(): lax.psum_scatter(large_stacked[3], 'seq', scatter_dimension=1, tiled=True)  91.4 us
    reduce_scatter x1, waiting for transfers between devices, per_device(): lax.psum_scatter(large_stacked[0], 'seq', scatter_dimension=1, tiled=True)  79.1 us
    reduce_scatter x4, waiting for transfers between devices, sum_rows(): lax.psum_scatter(partial_rows.astype(jnp.bfloat16), 'rep', scatter_dimens...  68.8 us
    reduce_scatter x1, waiting for transfers between devices, per_device(): lax.psum_scatter(large_stacked[1], 'seq', scatter_dimension=1, tiled=True)  66.3 us
    all_gather x1, waiting for transfers between devices, gather_weights(): lax.all_gather(down_shard, 'seq', axis=0, tiled=True)  51.7 us
    unnamed x209, local copies, waits for them, and re-layouts  50.7 us
  transfers between devices with their start and end apart: 21, of which 18 were waited for; matrix products, arithmetic and copies ran while one was open for 9% of the time, Pallas kernels for 0%

commit v1 on v0

v1 whole, which is shorter than its diff:
```python
from functools import partial
import math

import jax
import jax.numpy as jnp
import numpy as np
from jax import lax
from jax.experimental import pallas as pl
from jax.experimental.pallas import tpu as pltpu
from jax.sharding import PartitionSpec as P

EPS = 1e-05
HIGH = lax.Precision.HIGHEST
F32 = jnp.float32
B16 = jnp.bfloat16
LANE = 128
HALO = 16
VMEM_BYTES = 48 * 2**20


def swap(values, axis_name, bit):
    size = lax.axis_size(axis_name)
    return lax.ppermute(values, axis_name, [(i, i ^ bit) for i in range(size)])


def gather_rel(rows):
    far = swap(rows, "rep", 2)
    near = swap(rows, "rep", 1)
    diag = swap(far, "rep", 1)
    return jnp.concatenate([rows, near, far, diag], axis=0)


def scatter_rel(part):
    rows = part.shape[0] // 4
    blocks = part.reshape(4, rows, part.shape[1])
    far_in = swap(blocks[3].astype(B16), "rep", 1)
    far_sum = (blocks[2] + far_in.astype(F32)).astype(B16)
    near_in = swap(blocks[1].astype(B16), "rep", 1)
    far_out = swap(far_sum, "rep", 2)
    return blocks[0] + near_in.astype(F32) + far_out.astype(F32)


def ring_order(count):
    if count == 8:
        return [0, 2, 4, 6, 7, 5, 3, 1]
    return list(range(count))


def ring_gather(shard):
    count = lax.axis_size("seq")
    if count != 8:
        return lax.all_gather(shard, "seq", axis=0)
    order = ring_order(count)
    ahead = [(order[i], order[(i + 1) % count]) for i in range(count)]
    back = [(b, a) for a, b in ahead]
    me = lax.axis_index("seq")
    place = jnp.asarray(np.argsort(order), jnp.int32)[me]
    owners = jnp.asarray(order, jnp.int32)
    full = jnp.zeros((count,) + shard.shape, shard.dtype)

    def put(full, piece, step, lo=0):
        owner = owners[(place + step + count) % count]
        start = (owner, lo) + (0,) * (shard.ndim - 1)
        return lax.dynamic_update_slice(full, piece[None], start)

    full = put(full, shard, 0)
    left = right = shard
    for step in range(1, count // 2):
        left = lax.ppermute(left, "seq", ahead)
        right = lax.ppermute(right, "seq", back)
        full = put(full, left, -step)
        full = put(full, right, step)
    half = shard.shape[0] // 2
    left = lax.ppermute(left[:half], "seq", ahead)
    right = lax.ppermute(right[half:], "seq", back)
    full = put(full, left, -(count // 2))
    full = put(full, right, count // 2, half)
    return full


def shift_seq(values, step):
    count = lax.axis_size("seq")
    return lax.ppermute(values, "seq", [(i, (i + step) % count) for i in range(count)])


def unmix(values, axis, index):
    size, bit = values.shape[axis], 1
    while bit < size:
        cut = values.shape[:axis] + (size // (2 * bit), 2, bit) + values.shape[axis + 1 :]
        split = values.reshape(cut)
        values = jnp.where((index // bit) % 2 == 1, jnp.flip(split, axis + 1), split).reshape(values.shape)
        bit *= 2
    return values


def sync_small(total, group, own):
    n_seq, n_rep = lax.axis_size("seq"), lax.axis_size("rep")
    group_list, own_list = [group], [own]
    for axis_name, size in (("seq", n_seq), ("rep", n_rep)):
        bit = 1
        while bit < size:
            parts = [total] + group_list + own_list
            sizes = np.cumsum([0] + [p.shape[0] for p in parts])
            came = swap(jnp.concatenate(parts, axis=0), axis_name, bit)
            came = [came[a:b] for a, b in zip(sizes[:-1], sizes[1:])]
            total = total + came[0]
            count = len(group_list)
            if axis_name == "seq":
                group_list = [group_list[0] + came[1]]
            else:
                group_list = group_list + came[1 : 1 + count]
            own_list = own_list + came[1 + count :]
            bit *= 2
    groups = unmix(jnp.stack(group_list), 0, lax.axis_index("rep"))
    owns = jnp.stack(own_list).reshape((n_rep, n_seq) + own.shape)
    owns = unmix(unmix(owns, 0, lax.axis_index("rep")), 1, lax.axis_index("seq"))
    return total, groups, owns


def layer_norm(rows, gain, shift):
    row_mean = jnp.mean(rows, axis=-1, keepdims=True)
    centred = rows - row_mean
    variance = jnp.mean(centred * centred, axis=-1, keepdims=True)
    inverse = lax.rsqrt(variance + EPS)
    normed = centred * inverse
    return (normed * gain + shift, normed, inverse)


def norm_back(grad_rows, normed, inverse, gain):
    scaled = grad_rows * gain
    mean_one = jnp.mean(scaled, axis=-1, keepdims=True)
    mean_two = jnp.mean(scaled * normed, axis=-1, keepdims=True)
    grad_in = inverse * (scaled - mean_one - normed * mean_two)
    return (grad_in, jnp.sum(grad_rows * normed, axis=0), jnp.sum(grad_rows, axis=0))


def features(length, feat_count):
    ramp_unit = jnp.linspace(0.0, 1.0, length, dtype=F32)
    angles = jnp.arange(length, dtype=F32)[:, None] * (2.0 * math.pi / length)
    band_freqs = jnp.linspace(
        0.0001, (feat_count - 1) // 2 - 1.0, (feat_count - 1) // 2, dtype=F32
    )[None, :]
    phase_grid = band_freqs * angles
    grid_out = jnp.concatenate(
        [ramp_unit[:, None], jnp.cos(phase_grid), -jnp.sin(phase_grid)], axis=1
    )
    return (grid_out, ramp_unit)


def filter_columns(
    feature_grid,
    ramp_unit,
    start_chan,
    chan_count,
    model_width,
    feat_weight,
    feat_bias,
    inner_weight,
    inner_bias,
    deep_weight,
    deep_bias,
    sine_freq,
    columns,
):
    freq = sine_freq[:, None]

    def layer(weight, bias, below):
        grown = lax.dot_general(weight, below, (((0,), (0,)), ((), ())), precision=HIGH)
        return jnp.sin(freq * (grown + bias[:, None]))

    hidden = layer(feat_weight, feat_bias, feature_grid.T)
    hidden = layer(inner_weight, inner_bias, hidden)
    hidden = layer(deep_weight, deep_bias, hidden)
    deltas = jnp.abs(
        jnp.linspace(math.log(0.01) / 0.3, math.log(0.01) / 1.5, model_width, dtype=F32)
    )
    local_rates = lax.dynamic_slice_in_dim(deltas, start_chan, chan_count)
    return lax.dot_general(
        columns, hidden, (((0,), (0,)), ((), ())), precision=HIGH
    ) * jnp.exp(-ramp_unit[None, :] * local_rates[:, None])


def transform_tables(blocks, length):
    time = np.arange(blocks * length).reshape(blocks, 1, length)
    cls = np.arange(blocks).reshape(1, blocks, 1)
    period = 4 * blocks * length
    turn = (time * (2 * cls + 1)) % period * (2.0 * np.pi / period)
    twist = np.stack([np.cos(turn), -np.sin(turn)], axis=2).astype(np.float32)
    step = np.arange(length)
    turn = (step[:, None] * step[None, :]) % length * (2.0 * np.pi / length)
    cos, sin = np.cos(turn), np.sin(turn)
    table = np.block([[cos, -sin], [sin, cos]]).astype(np.float32)
    return twist, table


def spectrum_of(signal, twist, table):
    turned = jnp.einsum("bqzl,brl->qrzl", twist[: signal.shape[0]], signal, precision=HIGH)
    flat = turned.reshape(turned.shape[:2] + (-1,))
    return jnp.einsum("qrk,kf->qrf", flat, table, precision=HIGH)


def signal_of(spectrum, twist, table):
    blocks, length = twist.shape[0], twist.shape[3]
    turned = jnp.einsum("qrf,kf->qrk", spectrum, table, precision=HIGH)
    turned = turned.reshape(turned.shape[:2] + (2, length))
    return jnp.einsum("bqzl,qrzl->brl", twist, turned, precision=HIGH) * (1.0 / (blocks * length))


def times(left, right, conj_right):
    half = left.shape[-1] // 2
    lr, li = left[..., :half], left[..., half:]
    rr, ri = right[..., :half], right[..., half:]
    if conj_right:
        return jnp.concatenate([lr * rr + li * ri, li * rr - lr * ri], axis=-1)
    return jnp.concatenate([lr * rr - li * ri, lr * ri + li * rr], axis=-1)


def dot_split(values, hi, lo, dims):
    top = values.astype(B16)
    rest = (values - top.astype(F32)).astype(B16)
    dot = partial(lax.dot_general, dimension_numbers=(dims, ((), ())), preferred_element_type=F32)
    return dot(top, hi) + dot(rest, hi) + dot(top, lo)


def turn_rows(blocks_in, twist_ref, z_ref, base, classes):
    rows, length = blocks_in[0].shape
    for q in range(classes):
        for z in range(2):
            acc = None
            for b, block in enumerate(blocks_in):
                term = block * twist_ref[b, q, z : z + 1]
                acc = term if acc is None else acc + term
            z_ref[base + q * rows : base + (q + 1) * rows, z * length : (z + 1) * length] = acc


def back_rows(w, base, rows, block, twist_ref, classes):
    length = w.shape[1] // 2
    acc = None
    for q in range(classes):
        lo, hi = base + q * rows, base + (q + 1) * rows
        for z in range(2):
            term = w[lo:hi, z * length : (z + 1) * length] * twist_ref[block, q, z : z + 1]
            acc = term if acc is None else acc + term
    return acc * (1.0 / (classes * length))


def conv_forward_kernel(short_blocks, x_ref, kern_ref, twist_ref, hi_ref, lo_ref, skip_ref, out_ref, spec_ref, z_ref):
    blocks = twist_ref.shape[0]
    rows = x_ref.shape[1]
    span = blocks * rows
    first = [x_ref[b].astype(F32) for b in range(blocks)]
    second = [x_ref[blocks + b].astype(F32) for b in range(short_blocks)]
    turn_rows(first, twist_ref, z_ref, 0, blocks)
    turn_rows(second, twist_ref, z_ref, span, blocks)
    spec = dot_split(z_ref[...], hi_ref[...], lo_ref[...], ((1,), (0,)))
    spec_ref[...] = spec
    kern = kern_ref[...]
    prod = jnp.concatenate([times(spec[:span], kern, False), times(spec[span:], kern, False)], axis=0)
    w = dot_split(prod, hi_ref[...], lo_ref[...], ((1,), (1,)))
    skip = skip_ref[...]
    for b in range(blocks):
        out_ref[b] = (back_rows(w, 0, rows, b, twist_ref, blocks) + skip * first[b]).astype(B16)
        acc = back_rows(w, span, rows, b, twist_ref, blocks)
        if b < short_blocks:
            acc = acc + skip * second[b]
        out_ref[blocks + b] = acc.astype(B16)


def conv_backward_kernel(
    short_blocks, g_ref, spec_ref, kern_ref, twist_ref, hi_ref, lo_ref, skip_ref, out_ref, grad_kern_ref, z_ref, p_ref
):
    blocks = twist_ref.shape[0]
    rows = g_ref.shape[1]
    span = blocks * rows
    first = [g_ref[b].astype(F32) for b in range(blocks)]
    second = [g_ref[blocks + b].astype(F32) for b in range(short_blocks)]
    turn_rows(first, twist_ref, z_ref, 0, blocks)
    turn_rows(second, twist_ref, z_ref, span, blocks)
    grad = dot_split(z_ref[...], hi_ref[...], lo_ref[...], ((1,), (0,)))
    kern = kern_ref[...]
    p_ref[0:span] = times(grad[:span], kern, True)
    p_ref[span : 2 * span] = times(grad[span:], kern, True)
    p_ref[2 * span :] = times(grad[:span], spec_ref[0:span], True) + times(
        grad[span:], spec_ref[span:], True
    )
    w = dot_split(p_ref[...], hi_ref[...], lo_ref[...], ((1,), (1,)))
    skip = skip_ref[...]
    for b in range(blocks):
        out_ref[b] = (back_rows(w, 0, rows, b, twist_ref, blocks) + skip * first[b]).astype(B16)
        if b < short_blocks:
            acc = back_rows(w, span, rows, b, twist_ref, blocks) + skip * second[b]
            out_ref[blocks + b] = acc.astype(B16)
        else:
            out_ref[blocks + b] = jnp.zeros(out_ref.shape[1:], B16)
        grad_kern_ref[b] = back_rows(w, 2 * span, rows, b, twist_ref, blocks)


def conv_forward(received, kern_spec, twist, table, skip_local):
    blocks, rows, length = received.shape[0] // 2, received.shape[1], received.shape[2]
    short_blocks = -(-blocks // 4)
    skip = skip_local[:, None]
    if blocks != 4:
        x = received.astype(F32)
        spec = jnp.concatenate(
            [
                spectrum_of(x[:blocks], twist, table),
                spectrum_of(x[blocks : blocks + short_blocks], twist, table),
            ],
            axis=0,
        )
        kern = jnp.concatenate([kern_spec, kern_spec], axis=0)
        prod = times(spec, kern, False)
        out = jnp.concatenate(
            [signal_of(prod[:blocks], twist, table), signal_of(prod[blocks:], twist, table)], axis=0
        )
        return ((out + skip * x).astype(B16), spec)
    hi = jnp.asarray(table).astype(B16)
    lo = (jnp.asarray(table) - hi.astype(F32)).astype(B16)
    height = 2 * blocks * rows
    out, spec = pl.pallas_call(
        partial(conv_forward_kernel, short_blocks),
        out_shape=(
            jax.ShapeDtypeStruct(received.shape, B16),
            jax.ShapeDtypeStruct((height, 2 * length), F32),
        ),
        scratch_shapes=[pltpu.VMEM((height, 2 * length), F32)],
        compiler_params=pltpu.CompilerParams(vmem_limit_bytes=VMEM_BYTES),
        name="conv_forward",
    )(received, kern_spec.reshape(blocks * rows, 2 * length), twist, hi, lo, skip)
    return out, spec


def conv_backward(grads, spec, kern_spec, twist, table, skip_local):
    blocks, rows, length = grads.shape[0] // 2, grads.shape[1], grads.shape[2]
    short_blocks = -(-blocks // 4)
    skip = skip_local[:, None]
    if blocks != 4:
        g = grads.astype(F32)
        first = spectrum_of(g[:blocks], twist, table)
        second = spectrum_of(g[blocks : blocks + short_blocks], twist, table)
        one = signal_of(times(first, kern_spec, True), twist, table)
        two = signal_of(times(second, kern_spec, True), twist, table)
        cross = times(first, spec[:blocks], True) + times(second, spec[blocks:], True)
        out = jnp.concatenate([one, two], axis=0) + skip * g
        return (out.astype(B16), signal_of(cross, twist, table))
    hi = jnp.asarray(table).astype(B16)
    lo = (jnp.asarray(table) - hi.astype(F32)).astype(B16)
    span = blocks * rows
    out, grad_kern = pl.pallas_call(
        partial(conv_backward_kernel, short_blocks),
        out_shape=(
            jax.ShapeDtypeStruct(grads.shape, B16),
            jax.ShapeDtypeStruct((blocks, rows, length), F32),
        ),
        scratch_shapes=[
            pltpu.VMEM((2 * span, 2 * length), F32),
            pltpu.VMEM((3 * span, 2 * length), F32),
        ],
        compiler_params=pltpu.CompilerParams(vmem_limit_bytes=VMEM_BYTES),
        name="conv_backward",
    )(grads, spec, kern_spec.reshape(span, 2 * length), twist, hi, lo, skip)
    return out, grad_kern


def in_order(ref, rep, lead=()):
    count = ref.shape[-1] // LANE
    return [
        ref[lead + (slice(None), pl.ds(pl.multiple_of((rep ^ j) * LANE, LANE), LANE))]
        for j in range(count)
    ]


def put_rel(ref, rep, values, lead=()):
    for j in range(ref.shape[-1] // LANE):
        ref[lead + (slice(None), pl.ds(pl.multiple_of((rep ^ j) * LANE, LANE), LANE))] = values[
            :, j * LANE : (j + 1) * LANE
        ]


def extended(proj_ref, halo_ref, exists, rep, p):
    blocks = [halo_ref[p, :, :LANE]] + in_order(proj_ref, rep, (p,)) + [halo_ref[p, :, LANE:]]
    return jnp.concatenate(blocks, axis=1).astype(F32) * exists


def short_of(ext, col_ref, p):
    return (
        col_ref[:, p : p + 1] * pltpu.roll(ext, 2, 1)
        + col_ref[:, 3 + p : 4 + p] * pltpu.roll(ext, 1, 1)
        + col_ref[:, 6 + p : 7 + p] * ext
        + col_ref[:, 9 + p : 10 + p]
    )


def gate_kernel(rep_ref, proj_ref, halo_ref, col_ref, mask_ref, out_ref):
    rep = rep_ref[0]
    mask, exists = mask_ref[0:1], mask_ref[1:2]
    gate_in = short_of(extended(proj_ref, halo_ref, exists, rep, 1), col_ref, 1)
    values = short_of(extended(proj_ref, halo_ref, exists, rep, 2), col_ref, 2)
    gated = values * gate_in * mask
    out_ref[...] = gated[:, LANE:-LANE].astype(B16)


def output_kernel(rep_ref, proj_ref, halo_ref, col_ref, mask_ref, mixed_ref, out_ref):
    rep = rep_ref[0]
    gate_out = short_of(extended(proj_ref, halo_ref, mask_ref[1:2], rep, 0), col_ref, 0)
    put_rel(out_ref, rep, (gate_out[:, LANE:-LANE] * mixed_ref[...].astype(F32)).astype(B16))


def grad_mix_kernel(rep_ref, proj_ref, halo_ref, col_ref, mask_ref, mixed_ref, gy_ref, out_ref, first_ref):
    rep = rep_ref[0]
    gate_out = short_of(extended(proj_ref, halo_ref, mask_ref[1:2], rep, 0), col_ref, 0)
    gy = jnp.concatenate(in_order(gy_ref, rep), axis=1).astype(F32)
    out_ref[...] = (gy * gate_out[:, LANE:-LANE]).astype(B16)
    first_ref[...] = gy[:, :LANE] * mixed_ref[:, :LANE].astype(F32)


def grad_proj_kernel(
    rep_ref, proj_ref, halo_ref, col_ref, mask_ref, mixed_ref, gy_ref, ggated_ref, gnext_ref, onext_ref, out_ref, sum_ref
):
    rep = rep_ref[0]
    mask, exists = mask_ref[0:1], mask_ref[1:2]
    size = mask_ref.shape[1]
    mid = slice(LANE, size - LANE)
    gy = jnp.concatenate(in_order(gy_ref, rep), axis=1).astype(F32)
    zero = jnp.zeros((gy.shape[0], LANE), F32)
    next_on = exists[:, size - LANE :]
    ext = [extended(proj_ref, halo_ref, exists, rep, p) for p in range(3)]
    short = [short_of(ext[p], col_ref, p) for p in range(3)]
    ggated = jnp.concatenate(
        [zero, ggated_ref[...].astype(F32), gnext_ref[...].astype(F32) * next_on], axis=1
    )
    ggated = ggated * mask
    gout = gy * mixed_ref[...].astype(F32)
    gshort = [
        jnp.concatenate([zero, gout, onext_ref[...] * next_on], axis=1),
        ggated * short[2],
        ggated * short[1],
    ]
    gated = short[2][:, mid] * short[1][:, mid] * mask[:, mid]
    sums = [jnp.sum(gy * short[0][:, mid] * gated, axis=1, keepdims=True)]
    for p in range(3):
        mine = gshort[p][:, mid]
        sums.append(jnp.sum(mine, axis=1, keepdims=True))
        sums.append(jnp.sum(mine * ext[p][:, mid], axis=1, keepdims=True))
        sums.append(jnp.sum(mine * pltpu.roll(ext[p], 1, 1)[:, mid], axis=1, keepdims=True))
        sums.append(jnp.sum(mine * pltpu.roll(ext[p], 2, 1)[:, mid], axis=1, keepdims=True))
        gproj = (
            col_ref[:, 6 + p : 7 + p] * gshort[p]
            + col_ref[:, 3 + p : 4 + p] * pltpu.roll(gshort[p], size - 1, 1)
            + col_ref[:, p : p + 1] * pltpu.roll(gshort[p], size - 2, 1)
        )[:, mid].astype(B16)
        sums.append(jnp.sum(gproj.astype(F32), axis=1, keepdims=True))
        put_rel(out_ref, rep, gproj, (p,))
    sum_ref[...] = jnp.concatenate(sums, axis=1)


def token_call(kernel, name, arrays, outs):
    step = 64

    def spec(shape, cut):
        if not cut:
            return pl.BlockSpec(shape, lambda i: (0,) * len(shape))
        if len(shape) == 3:
            return pl.BlockSpec((shape[0], step, shape[2]), lambda i: (0, i, 0))
        return pl.BlockSpec((step, shape[1]), lambda i: (i, 0))

    width = outs[0].shape[-2]
    return pl.pallas_call(
        kernel,
        grid=(width // step,),
        in_specs=[pl.BlockSpec(memory_space=pltpu.SMEM)] + [spec(a.shape, cut) for a, cut in arrays[1:]],
        out_specs=[spec(o.shape, True) for o in outs],
        out_shape=outs,
        compiler_params=pltpu.CompilerParams(vmem_limit_bytes=VMEM_BYTES),
        name=name,
    )(*[a for a, _ in arrays])


def rows128(values):
    flat = values.reshape(-1)
    return jnp.pad(flat, (0, -flat.shape[0] % 1024)).reshape(-1, 128)


def per_device(
    tokens,
    cotangent,
    lengths,
    in_weight,
    in_bias,
    short_taps,
    short_bias,
    feat_weight,
    feat_bias,
    inner_weight,
    inner_bias,
    deep_weight,
    deep_bias,
    sine_freq,
    kernel_weight,
    skip_gain,
    out_weight,
    out_bias,
    norm1_gain,
    norm1_shift,
    norm2_gain,
    norm2_shift,
    up_weight,
    up_bias,
    down_weight,
    down_bias,
):
    n_seq, n_rep = lax.axis_size("seq"), lax.axis_size("rep")
    seq, rep = lax.axis_index("seq"), lax.axis_index("rep")
    tok_rows, model = tokens.shape
    group = tok_rows * n_rep
    blocks = n_seq // 2
    seq_len = blocks * group
    chan = model // (n_seq * n_rep)
    width = model // n_rep
    hidden = up_weight.shape[2]
    block_start = rep * width
    chan_start = block_start + seq * chan
    rep_scalar = jnp.reshape(rep, (1,)).astype(jnp.int32)

    item_len = jnp.where(seq // blocks == 0, lengths[0], lengths[1])
    at = (seq % blocks) * group
    row_mask = (at + rep * tok_rows + jnp.arange(tok_rows, dtype=jnp.int32) < item_len).astype(F32)[:, None]
    position = at - LANE + jnp.arange(group + 2 * LANE, dtype=jnp.int32)
    mask_ext = jnp.stack([position < item_len, (position >= 0) & (position < seq_len)]).astype(F32)
    mask_ext = jnp.pad(mask_ext, ((0, 6), (0, 0)))

    full_in = ring_gather(in_weight[0]).reshape(model, 3, width)
    full_out = lax.all_gather(out_weight[0], "seq", axis=0, tiled=True)
    full_up = lax.all_gather(up_weight[0], "seq", axis=0, tiled=True)
    full_down = lax.all_gather(down_weight[0], "seq", axis=0, tiled=True)

    residual = tokens.astype(F32)
    normed_one, unit_one, scale_one = layer_norm(residual, norm1_gain[0], norm1_shift[0])
    normed_one = normed_one.astype(B16)
    rows_one = gather_rel(normed_one)
    rel = rows_one.reshape(n_rep, tok_rows, model)
    last_rows = lax.dynamic_index_in_dim(rel, rep ^ (n_rep - 1), 0, False)[-HALO:]
    first_rows = lax.dynamic_index_in_dim(rel, rep, 0, False)[:HALO]
    before = shift_seq(last_rows, 1)
    after = shift_seq(first_rows, -1)
    gap = jnp.zeros((LANE - HALO, model), B16)
    halo_rows = jnp.concatenate([gap, before, after, gap], axis=0)
    proj_bias = lax.dynamic_slice_in_dim(in_bias[0], block_start, width, 1)[:, :, None]

    def project(rows):
        return (
            jnp.einsum("td,dpc->pct", rows, full_in, preferred_element_type=F32) + proj_bias
        ).astype(B16)

    proj = project(rows_one)
    halo = project(halo_rows)

    tap_cols = lax.dynamic_slice_in_dim(short_taps[0], block_start, width, 2).reshape(9, width)
    bias_cols = lax.dynamic_slice_in_dim(short_bias[0], block_start, width, 1)
    cols = jnp.pad(jnp.concatenate([tap_cols, bias_cols], axis=0), ((0, 4), (0, 0))).T
    common = [(rep_scalar, True), (proj, True), (halo, True), (cols, True), (mask_ext, False)]
    flat_shape = jax.ShapeDtypeStruct((width, group), B16)
    (gated,) = token_call(gate_kernel, "gate", common, [flat_shape])
    received = lax.all_to_all(gated.reshape(n_seq, chan, group), "seq", 0, 0, tiled=True)

    skip_local = lax.dynamic_slice_in_dim(skip_gain[0], chan_start, chan, 0)
    columns = lax.dynamic_slice_in_dim(kernel_weight[0], chan_start, chan, 1)
    feature_grid, ramp_unit = features(seq_len, feat_weight.shape[1])
    twist, table = transform_tables(blocks, group)
    kernel, kernel_pull = jax.vjp(
        partial(filter_columns, feature_grid, ramp_unit, chan_start, chan, model),
        feat_weight[0],
        feat_bias[0],
        inner_weight[0],
        inner_bias[0],
        deep_weight[0],
        deep_bias[0],
        sine_freq[0],
        columns,
    )
    kern_blocks = kernel.reshape(chan, blocks, group).transpose(1, 0, 2)
    kern_spec = spectrum_of(kern_blocks, twist, table)
    mixed_chan, kept_spec = conv_forward(received, kern_spec, twist, table, skip_local)
    mixed = lax.all_to_all(mixed_chan, "seq", 0, 0, tiled=True).reshape(width, group)
    (y_cols,) = token_call(output_kernel, "output", common + [(mixed, True)], [flat_shape])

    middle_part = jnp.einsum("ct,oc->to", y_cols, full_out, preferred_element_type=F32)
    middle = residual + (scatter_rel(middle_part) + out_bias[0])
    normed_two, unit_two, scale_two = layer_norm(middle, norm2_gain[0], norm2_shift[0])
    rows_two = gather_rel(normed_two.astype(B16))

    grad_top = cotangent.astype(F32) * row_mask
    grad_mlp = grad_top.astype(B16)
    mlp_rows = gather_rel(grad_mlp)
    grad_act = jnp.dot(mlp_rows, full_down, preferred_element_type=F32)
    up_block = lax.dynamic_slice_in_dim(up_bias[0], rep * hidden, hidden, 0)
    pre_act = jnp.dot(rows_two, full_up, preferred_element_type=F32) + up_block
    phi = 0.5 * (1.0 + lax.erf(pre_act * math.sqrt(0.5)))
    act_rows = (pre_act * phi).astype(B16)
    slope = phi + pre_act * (jnp.exp(-0.5 * pre_act * pre_act) * (1.0 / math.sqrt(2.0 * math.pi)))
    grad_pre = (grad_act * slope).astype(B16)
    grad_two = scatter_rel(jnp.einsum("tf,df->td", grad_pre, full_up, preferred_element_type=F32))
    mlp_part = jnp.einsum("tf,of->to", act_rows, full_down, preferred_element_type=F32)
    layer_out = (middle + (scatter_rel(mlp_part) + down_bias[0])).astype(B16)
    term_down = jnp.einsum("to,tf->of", mlp_rows, act_rows, preferred_element_type=F32)
    term_up = jnp.einsum("td,tf->df", rows_two, grad_pre, preferred_element_type=F32)
    grad_down_bias = jnp.sum(grad_mlp.astype(F32), axis=0)
    grad_up_block = jnp.sum(grad_pre.astype(F32), axis=0)

    def to_owner(term):
        return lax.psum_scatter(term.astype(B16), "seq", scatter_dimension=0, tiled=True).astype(F32)

    grad_up = to_owner(term_up)
    grad_down = to_owner(term_down)

    grad_unit_two, grad_gain_two, grad_shift_two = norm_back(
        grad_two, unit_two, scale_two, norm2_gain[0]
    )
    grad_middle = grad_top + grad_unit_two
    grad_mix = grad_middle.astype(B16)
    grad_out_bias = jnp.sum(grad_mix.astype(F32), axis=0)
    mix_rows = gather_rel(grad_mix)
    gy_cols = jnp.einsum("to,oc->ct", mix_rows, full_out, preferred_element_type=F32).astype(B16)
    term_out = jnp.einsum("to,ct->oc", mix_rows, y_cols, preferred_element_type=F32)
    grad_out = to_owner(term_out)

    grad_mixed, gate_first = token_call(
        grad_mix_kernel,
        "grad_mix",
        common + [(mixed, True), (gy_cols, True)],
        [flat_shape, jax.ShapeDtypeStruct((width, LANE), F32)],
    )
    gate_next = shift_seq(gate_first, -1)
    grads_chan = lax.all_to_all(grad_mixed.reshape(n_seq, chan, group), "seq", 0, 0, tiled=True)
    ggated_chan, grad_kernel = conv_backward(grads_chan, kept_spec, kern_spec, twist, table, skip_local)
    ggated = lax.all_to_all(ggated_chan, "seq", 0, 0, tiled=True).reshape(width, group)
    ggated_next = shift_seq(ggated[:, :LANE], -1)
    kernel_grads = kernel_pull(grad_kernel.transpose(1, 0, 2).reshape(chan, seq_len))
    grad_proj, col_sums = token_call(
        grad_proj_kernel,
        "grad_proj",
        common
        + [(mixed, True), (gy_cols, True), (ggated, True), (ggated_next, True), (gate_next, True)],
        [jax.ShapeDtypeStruct((3, width, group), B16), jax.ShapeDtypeStruct((width, 16), F32)],
    )

    one_part = jnp.einsum("pct,dpc->td", grad_proj, full_in, preferred_element_type=F32)
    grad_one = scatter_rel(one_part)
    term_in = jnp.einsum("td,pct->dpc", rows_one, grad_proj, preferred_element_type=F32)
    grad_in = to_owner(term_in)
    grad_unit_one, grad_gain_one, grad_shift_one = norm_back(
        grad_one, unit_one, scale_one, norm1_gain[0]
    )
    grad_tokens = grad_middle + grad_unit_one

    totals = [
        *kernel_grads[:7],
        grad_gain_one,
        grad_shift_one,
        grad_gain_two,
        grad_shift_two,
        grad_out_bias,
        grad_down_bias,
    ]
    packed = [rows128(t) for t in totals]
    group_part = jnp.concatenate([rows128(col_sums.T), rows128(grad_up_block)], axis=0)
    total, groups, owns = sync_small(jnp.concatenate(packed, axis=0), group_part, rows128(kernel_grads[7]))
    outs = []
    start = 0
    for t, p in zip(totals, packed):
        outs.append(total[start : start + p.shape[0]].reshape(-1)[: t.size].reshape((1,) + t.shape))
        start += p.shape[0]
    flat = groups.reshape(n_rep, -1)
    sums = flat[:, : 16 * width].reshape(n_rep, 16, width).transpose(1, 0, 2).reshape(16, model)
    grad_up_bias = flat[:, 16 * width : 16 * width + hidden].reshape(1, -1)
    filt = columns.shape[0]
    grad_kernel_weight = (
        owns.reshape(n_rep, n_seq, -1)[:, :, : filt * chan]
        .reshape(n_rep, n_seq, filt, chan)
        .transpose(2, 0, 1, 3)
        .reshape(1, filt, model)
    )
    pick = lambda offset: jnp.stack([sums[1 + 5 * p + offset] for p in range(3)])
    grad_skip = sums[0][None]
    grad_short_bias = pick(0)[None]
    grad_short_taps = jnp.stack([pick(3), pick(2), pick(1)])[None]
    grad_in_bias = pick(4)[None]
    return (
        layer_out,
        grad_tokens,
        grad_in[None],
        grad_in_bias,
        grad_short_taps,
        grad_short_bias,
        outs[0],
        outs[1],
        outs[2],
        outs[3],
        outs[4],
        outs[5],
        outs[6],
        grad_kernel_weight,
        grad_skip,
        grad_out[None],
        outs[11],
        outs[7],
        outs[8],
        outs[9],
        outs[10],
        grad_up[None],
        grad_up_bias,
        grad_down[None],
        outs[12],
    )


def solution(mesh):
    rows = P(("seq", "rep"), None)
    cut = P(None, "seq", "rep")
    wide = P(None, "seq", None, "rep")
    whole = P()
    ins = [rows, rows, whole, wide] + [whole] * 12 + [cut] + [whole] * 5 + [cut, whole, cut, whole]
    outs = [rows, rows, wide] + [whole] * 12 + [cut] + [whole] * 5 + [cut, whole, cut, whole]
    return jax.shard_map(
        per_device, mesh=mesh, in_specs=tuple(ins), out_specs=tuple(outs), check_vma=False
    )
```

time: 1370 us -> 524 us (0.38)
  waiting for transfers between devices: 867 us -> 216 us
  matrix products: 236 us -> 70.3 us
  local copies, waits for them, and re-layouts: 121 us -> 42.3 us
  other arithmetic: 65.6 us -> 25.4 us
  starting transfers between devices: 19.2 us -> 58 us
  between operations: 15.6 us -> 41.6 us
  Pallas kernels: 0 us -> 25.9 us
    psum x2 -> x0, waiting for transfers between devices: 270 us -> none  [per_device(): lax.psum((stacked[0], stacked[1], stacked[2], stacked[3], stacked[4], sta...]
    reduce_scatter x8 -> x4, waiting for transfers between devices: 398 us -> 141 us  [to_owner(): lax.psum_scatter(term.astype(B16), 'seq', scatter_dimension=0, tiled=True)]
    all_gather x7 -> x2, waiting for transfers between devices: 180 us -> 0.04 us  [the longest x1 0.02 us: per_device(): full_up = lax.all_gather(up_weight[0], 'seq', axis=0, tiled=True)]
    dot_general x50 -> x17, matrix products: 197 us -> 41.7 us  [the longest x8 18.6 us: layer(): lax.dot_general(weight, below, (((0,), (0,)), ((), ())), precision=HIGH)]
    ppermute x0 -> x41, waiting for transfers between devices: none -> 71.3 us  [the longest x29 61.3 us: swap(): return lax.ppermute(values, axis_name, [(i, i ^ bit) for i in range(size)])]
    ppermute x0 -> x41, starting transfers between devices: none -> 38.6 us  [the longest x29 15.9 us: swap(): return lax.ppermute(values, axis_name, [(i, i ^ bit) for i in range(size)])]
    unnamed x209 -> x288, local copies, waits for them, and re-layouts: 50.7 us -> 20.2 us
    pallas_call x0 -> x6, Pallas kernels: none -> 25.9 us  [the longest x4 13.6 us: token_call(): pl.pallas_call(kernel, grid=(width // step,), in_specs=[pl.BlockSpec(memo...]
  transfers between devices with their start and end apart: 21 -> 51, of which waited for: 18 -> 24; matrix products, arithmetic and copies ran while one was open for 9% -> 22% of each run, Pallas kernels for 0% -> 5%
where the time goes in v1:
time: 524 us; the launch traced here: 514 us
  waiting for transfers between devices  216 us (41%)
  matrix products  70.3 us (13%)
  starting transfers between devices  58 us (11%)
  local copies, waits for them, and re-layouts  42.3 us (8%)
  between operations  41.6 us (8%)
  blocking collectives  34.8 us (7%)
  Pallas kernels  25.9 us (5%)
  other arithmetic  25.4 us (5%)
    reduce_scatter x4, waiting for transfers between devices, to_owner(): lax.psum_scatter(term.astype(B16), 'seq', scatter_dimension=0, tiled=True)  141 us
    ppermute x29, waiting for transfers between devices, swap(): return lax.ppermute(values, axis_name, [(i, i ^ bit) for i in range(size)])  61.3 us
    all_gather x1, blocking collectives, per_device(): full_out = lax.all_gather(out_weight[0], 'seq', axis=0, tiled=True)  34.8 us
    unnamed x288, local copies, waits for them, and re-layouts  20.2 us
    dot_general x8, matrix products, layer(): lax.dot_general(weight, below, (((0,), (0,)), ((), ())), precision=HIGH)  18.6 us
    ppermute x29, starting transfers between devices, swap(): return lax.ppermute(values, axis_name, [(i, i ^ bit) for i in range(size)])  15.9 us
    pallas_call x4, Pallas kernels, token_call(): pl.pallas_call(kernel, grid=(width // step,), in_specs=[pl.BlockSpec(memo...  13.6 us
    ppermute x4, starting transfers between devices, shift_seq(): lax.ppermute(values, 'seq', [(i, (i + step) % count) for i in range(count)])  13.4 us
  transfers between devices with their start and end apart: 51, of which 24 were waited for; matrix products, arithmetic and copies ran while one was open for 22% of the time, Pallas kernels for 5%

profile of v1, /device:TPU:0, one launch (start us, length us, event | category | flops | bytes accessed | tf_op | source)
XLA Modules:
  0.0 514.5 jit_solution(5666393132161329542)
XLA Ops:
  52.3 6.6 %convolution_bitcast_fusion.2 = f32[4,32,2,512]{1,0,2,3:T(4,128)} fusion(f32[32,4,512,1]{0,1,3,2:T(4,128)S(1)} %copy.138, f32[4,4,2,512]{0,1,2,3:T(4,128)} %constant.304), kind=kOutput, calls=%fused_computation.33 | convolution fusion | flops 6291456 | bytes 851968 | tf_op jit(solution)/shard_map/bqzl,brl->qrzl/dot_general | solution.py:197
  70.0 5.1 collective-permute-done.2
  78.9 3.2 collective-permute-start.12
  92.6 5.5 %all-to-all-start = ((bf16[8,32,512]{2,1,0:T(8,128)(2,1)}), bf16[8,32,512]{2,1,0:T(8,128)(2,1)}, u32[]{:S(2)}, u32[]{:S(2)}) async-start(bf16[8,32,512]{2,1,0:T(8,128)(2,1)} %bitcast.48), calls=%async_computation | async-start | bytes 524288 | tf_op jit(solution)/shard_map/all_to_all | solution.py:564
  99.0 5.7 %fusion.132.kern_ref = f32[128,1024]{1,0:T(8,128)} fusion(f32[128,1024]{1,0:T(8,128)} %bitcast.485, f32[1024,1024]{1,0:T(8,128)} %constant.285.clone), kind=kOutput, calls=%fused_computation.400 | convolution fusion | flops 1610612736 | bytes 5242880 | tf_op jit(solution)/shard_map/qrk,kf->qrf/dot_general | solution.py:199
  108.4 5.7 %conv_forward.1 = (bf16[8,32,512]{2,1,0:T(8,128)(2,1)S(1)}, f32[256,1024]{1,0:T(8,128)S(1)}) custom-call(bf16[8,32,512]{2,1,0:T(8,128)(2,1)} %all-to-all-done.x_ref, f32[128,1024]{1,0:T(8,128)S(1)} %copy-done.2, f32[4,4,2,512]{3,2,1,0:T(2,128)S(1)} %copy-done.20, bf16[1024,1024]{1,0:T(8,128)(2,1)S(1)} %copy-done.1, bf16[1024,1024]{1,0:T(8,128)(2,1)} %constant.303.lo_ref, ...), custom_call_target="tpu_custom_call" | custom-call | tf_op jit(solution)/shard_map/conv_forward/pallas_call | solution.py:320
  115.8 4.7 all-to-all-start.1
  121.3 34.8 %all-gather = bf16[1,1024,256]{2,1,0:T(8,128)(2,1)} all-gather(bf16[1,128,256]{2,1,0:T(8,128)(2,1)} %param.48), channel_id=2, replica_groups=mesh['seq'=8,'rep'=4] {'seq'}, dimensions={1}, use_global_device_ids=true | all-gather | bytes 589824 | tf_op jit(solution)/shard_map/all_gather | solution.py:533
  164.7 8.1 %collective-permute-done.15 = bf16[128,1024]{1,0:T(8,128)(2,1)} collective-permute-done((bf16[128,1024]{1,0:T(8,128)(2,1)}, bf16[128,1024]{1,0:T(8,128)(2,1)}, u32[]{:S(2)}, u32[]{:S(2)}) %collective-permute-start.15) | collective-permute-done | bytes 262176 | tf_op jit(solution)/shard_map/ppermute | solution.py:23
  179.5 6.1 %collective-permute-done.17 = bf16[128,1024]{1,0:T(8,128)(2,1)} collective-permute-done((bf16[128,1024]{1,0:T(8,128)(2,1)}, bf16[128,1024]{1,0:T(8,128)(2,1)}, u32[]{:S(2)}, u32[]{:S(2)}) %collective-permute-start.17) | collective-permute-done | bytes 262176 | tf_op jit(solution)/shard_map/ppermute | solution.py:23
  189.5 5.0 multiply_convert_fusion
  194.5 5.1 convert_reduce_fusion
  206.4 6.8 %collective-permute-done.27 = bf16[128,1024]{1,0:T(8,128)(2,1)S(1)} collective-permute-done((bf16[128,1024]{1,0:T(8,128)(2,1)S(1)}, bf16[128,1024]{1,0:T(8,128)(2,1)S(1)}, u32[]{:S(2)}, u32[]{:S(2)}) %collective-permute-start.27) | collective-permute-done | bytes 262176 | tf_op jit(solution)/shard_map/ppermute | solution.py:23
  214.1 4.3 collective-permute-done.21
  220.7 7.3 %collective-permute-done.29 = bf16[128,1024]{1,0:T(8,128)(2,1)S(1)} collective-permute-done((bf16[128,1024]{1,0:T(8,128)(2,1)S(1)}, bf16[128,1024]{1,0:T(8,128)(2,1)S(1)}, u32[]{:S(2)}, u32[]{:S(2)}) %collective-permute-start.29) | collective-permute-done | bytes 262176 | tf_op jit(solution)/shard_map/ppermute | solution.py:23
  231.7 4.1 convolution_convert_fusion.1
  241.7 5.5 %all-to-all-start.2 = ((bf16[8,32,512]{2,1,0:T(8,128)(2,1)}), bf16[8,32,512]{2,1,0:T(8,128)(2,1)}, u32[]{:S(2)}, u32[]{:S(2)}) async-start(bf16[8,32,512]{2,1,0:T(8,128)(2,1)} %bitcast.479), calls=%async_computation.2 | async-start | bytes 524288 | tf_op jit(solution)/shard_map/all_to_all | solution.py:634
  250.5 4.2 convolution_convert_fusion
  254.7 4.9 collective-permute-start.32
  262.8 6.7 %conv_backward.1 = (bf16[8,32,512]{2,1,0:T(8,128)(2,1)S(1)}, f32[4,32,512]{2,1,0:T(8,128)S(1)}) custom-call(bf16[8,32,512]{2,1,0:T(8,128)(2,1)} %all-to-all-done.2.g_ref, f32[256,1024]{1,0:T(8,128)S(1)} %copy-done.13, f32[128,1024]{1,0:T(8,128)S(1)} %copy-done.3, f32[4,4,2,512]{3,2,1,0:T(2,128)S(1)} %copy-done.21, bf16[1024,1024]{1,0:T(8,128)(2,1)S(1)} %copy-done.1, ...), custom_call_target="tpu_custom_call" | custom-call | tf_op jit(solution)/shard_map/conv_backward/pallas_call | solution.py:349
  278.2 3.8 fusion.63
  282.7 3.4 all-to-all-start.3
  290.5 3.4 fusion.64
  296.0 3.7 collective-permute-start.31
  301.6 6.2 %grad_proj.1 = (bf16[3,256,512]{2,1,0:T(8,128)(2,1)S(1)}, f32[256,16]{1,0:T(8,128)S(1)}) custom-call(s32[1]{0:T(128)} %bitcast.rep_ref, bf16[3,256,512]{2,1,0:T(8,128)(2,1)S(1)} %add_convert_fusion.proj_ref, bf16[3,256,256]{2,1,0:T(8,128)(2,1)S(1)} %fusion.21.halo_ref, f32[256,16]{1,0:T(8,128)S(1)} %copy-done.7, f32[8,768]{1,0:T(8,128)S(1)} %copy-done.19, ...), custom_call_target="tpu_custom_call" | custom-call | tf_op jit(solution)/shard_map/grad_proj/pallas_call | solution.py:468
  313.8 3.4 convolution_convert_fusion.2
  328.2 4.9 collective-permute-done.37
  336.3 4.6 collective-permute-done.38
  343.4 7.5 %collective-permute-done.40 = f32[504,128]{1,0:T(8,128)S(1)} collective-permute-done((f32[504,128]{1,0:T(8,128)S(1)}, f32[504,128]{1,0:T(8,128)S(1)}, u32[]{:S(2)}, u32[]{:S(2)}) %collective-permute-start.40) | collective-permute-done | bytes 258080 | tf_op jit(solution)/shard_map/ppermute | solution.py:23
  361.0 5.4 %reduce-scatter.9.cloned.1.call-done = bf16[128,1024]{1,0:T(8,128)(2,1)} async-done(((bf16[1024,1024]{1,0:T(8,128)(2,1)}), bf16[128,1024]{1,0:T(8,128)(2,1)}) %reduce-scatter.9.cloned.1.call-update) | async-done | bytes 262160 | tf_op jit(solution)/shard_map/reduce_scatter | solution.py:611
  368.2 69.0 %reduce-scatter.11.cloned.1.call-done = bf16[128,1024]{1,0:T(8,128)(2,1)} async-done(((bf16[1024,1024]{1,0:T(8,128)(2,1)}), bf16[128,1024]{1,0:T(8,128)(2,1)}) %reduce-scatter.11.cloned.1.call-update) | async-done | bytes 262160 | tf_op jit(solution)/shard_map/reduce_scatter | solution.py:611
  439.1 66.4 %reduce-scatter.5.cloned.1.call-done = bf16[128,3,256]{2,0,1:T(8,128)(2,1)} async-done(((bf16[1024,3,256]{2,0,1:T(8,128)(2,1)}), bf16[128,3,256]{2,0,1:T(8,128)(2,1)}) %reduce-scatter.5.cloned.1.call-update) | async-done | bytes 196624 | tf_op jit(solution)/shard_map/reduce_scatter | solution.py:611
  (534 shorter events, 151.6 us)
Async XLA Ops:
  7.3 182.2 %all-gather.6.cloned.1.call-start = ((), (), s32[]{:S(2)}) async-start(), calls=%async_computation.12 | async-start | bytes 2359296 | tf_op jit(solution)/shard_map/all_gather | solution.py:534
  7.3 60.4 %collective-permute-start = (bf16[128,3,256]{2,0,1:T(8,128)(2,1)}, bf16[128,3,256]{2,0,1:T(8,128)(2,1)S(1)}, u32[]{:S(2)}, u32[]{:S(2)}) collective-permute-start(bf16[128,3,256]{2,0,1:T(8,128)(2,1)} %bitcast.501), channel_id=1, source_target_pairs={{0,8},{8,16},{16,24},{24,28},{28,20},{20,12},{12,4},{4,0},{1,9},{9... | collective-permute-start | bytes 589832 | tf_op jit(solution)/shard_map/ppermute | solution.py:69
  10.4 59.0 %collective-permute-start.1 = (bf16[128,3,256]{2,0,1:T(8,128)(2,1)}, bf16[128,3,256]{2,0,1:T(8,128)(2,1)S(1)}, u32[]{:S(2)}, u32[]{:S(2)}) collective-permute-start(bf16[128,3,256]{2,0,1:T(8,128)(2,1)} %bitcast.502), channel_id=1, source_target_pairs={{8,0},{16,8},{24,16},{28,24},{20,28},{12,20},{4,12},{0,4},{9,1},{1... | collective-permute-start | bytes 589832 | tf_op jit(solution)/shard_map/ppermute | solution.py:70
  13.9 56.0 %collective-permute-start.9 = (bf16[128,1024]{1,0:T(8,128)(2,1)S(1)}, bf16[128,1024]{1,0:T(8,128)(2,1)S(1)}, u32[]{:S(2)}, u32[]{:S(2)}) collective-permute-start(bf16[128,1024]{1,0:T(8,128)(2,1)S(1)} %fusion.32), channel_id=1, source_target_pairs={{0,2},{1,3},{2,0},{3,1},{4,6},{5,7},{6,4},{7,5},{8,10},{9,11},{10,... | collective-permute-start | bytes 786440 | tf_op jit(solution)/shard_map/ppermute | solution.py:23
  15.9 61.3 %collective-permute-start.8 = (bf16[128,1024]{1,0:T(8,128)(2,1)S(1)}, bf16[128,1024]{1,0:T(8,128)(2,1)S(1)}, u32[]{:S(2)}, u32[]{:S(2)}) collective-permute-start(bf16[128,1024]{1,0:T(8,128)(2,1)S(1)} %fusion.32), channel_id=1, source_target_pairs={{0,1},{1,0},{2,3},{3,2},{4,5},{5,4},{6,7},{7,6},{8,9},{9,8},{10,11... | collective-permute-start | bytes 786440 | tf_op jit(solution)/shard_map/ppermute | solution.py:23
  67.8 7.4 %collective-permute-start.2 = (bf16[128,3,256]{2,0,1:T(8,128)(2,1)S(1)}, bf16[128,3,256]{2,0,1:T(8,128)(2,1)S(1)}, u32[]{:S(2)}, u32[]{:S(2)}) collective-permute-start(bf16[128,3,256]{2,0,1:T(8,128)(2,1)S(1)} %collective-permute-done), channel_id=1, source_target_pairs={{0,8},{8,16},{16,24},{24,28},{28,20},{20,12},{12,4},{4,0},{1,9},{9... | collective-permute-start | bytes 589832 | tf_op jit(solution)/shard_map/ppermute | solution.py:69
  77.4 10.6 %collective-permute-start.11 = (bf16[16,1024]{1,0:T(8,128)(2,1)S(1)}, bf16[16,1024]{1,0:T(8,128)(2,1)S(1)}, u32[]{:S(2)}, u32[]{:S(2)}) collective-permute-start(bf16[16,1024]{1,0:T(8,128)(2,1)S(1)} %get-tuple-element.126), channel_id=1, source_target_pairs={{0,4},{4,8},{8,12},{12,16},{16,20},{20,24},{24,28},{28,0},{1,5},{5... | collective-permute-start | bytes 98312 | tf_op jit(solution)/shard_map/ppermute | solution.py:83
  78.9 9.1 %collective-permute-start.12 = (bf16[16,1024]{1,0:T(8,128)(2,1)S(1)}, bf16[16,1024]{1,0:T(8,128)(2,1)S(1)}, u32[]{:S(2)}, u32[]{:S(2)}) collective-permute-start(bf16[16,1024]{1,0:T(8,128)(2,1)S(1)} %get-tuple-element.127), channel_id=1, source_target_pairs={{0,28},{4,0},{8,4},{12,8},{16,12},{20,16},{24,20},{28,24},{1,29},{... | collective-permute-start | bytes 98312 | tf_op jit(solution)/shard_map/ppermute | solution.py:83
  92.6 13.9 %all-to-all-start = ((bf16[8,32,512]{2,1,0:T(8,128)(2,1)}), bf16[8,32,512]{2,1,0:T(8,128)(2,1)}, u32[]{:S(2)}, u32[]{:S(2)}) async-start(bf16[8,32,512]{2,1,0:T(8,128)(2,1)} %bitcast.48), calls=%async_computation | async-start | bytes 524288 | tf_op jit(solution)/shard_map/all_to_all | solution.py:564
  115.8 40.3 %all-to-all-start.1 = ((bf16[8,32,512]{2,1,0:T(8,128)(2,1)}), bf16[8,32,512]{2,1,0:T(8,128)(2,1)}, u32[]{:S(2)}, u32[]{:S(2)}) async-start(bf16[8,32,512]{2,1,0:T(8,128)(2,1)} %copy-done.24), calls=%async_computation.1 | async-start | bytes 524288 | tf_op jit(solution)/shard_map/all_to_all | solution.py:584
  120.5 74.1 %all-gather.8.cloned.1.call-start = ((), (), s32[]{:S(2)}) async-start(), calls=%async_computation.13 | async-start | bytes 2359296 | tf_op jit(solution)/shard_map/all_gather | solution.py:535
  121.2 196.1 %reduce-scatter.7.cloned.1.call-start = ((), (), s32[]{:S(2)}) async-start(), calls=%async_computation.9 | async-start | bytes 589824 | tf_op jit(solution)/shard_map/reduce_scatter | solution.py:611
  164.2 8.7 %collective-permute-start.15 = (bf16[128,1024]{1,0:T(8,128)(2,1)}, bf16[128,1024]{1,0:T(8,128)(2,1)}, u32[]{:S(2)}, u32[]{:S(2)}) collective-permute-start(bf16[128,1024]{1,0:T(8,128)(2,1)} %fusion.48), channel_id=1, source_target_pairs={{0,2},{1,3},{2,0},{3,1},{4,6},{5,7},{6,4},{7,5},{8,10},{9,11},{10,... | collective-permute-start | bytes 786440 | tf_op jit(solution)/shard_map/ppermute | solution.py:23
  176.0 9.6 %collective-permute-start.17 = (bf16[128,1024]{1,0:T(8,128)(2,1)}, bf16[128,1024]{1,0:T(8,128)(2,1)}, u32[]{:S(2)}, u32[]{:S(2)}) collective-permute-start(bf16[128,1024]{1,0:T(8,128)(2,1)} %add_convert_fusion.1), channel_id=1, source_target_pairs={{0,2},{1,3},{2,0},{3,1},{4,6},{5,7},{6,4},{7,5},{8,10},{9,11},{10,... | collective-permute-start | bytes 786440 | tf_op jit(solution)/shard_map/ppermute | solution.py:23
  178.0 11.5 %collective-permute-start.23 = (bf16[128,1024]{1,0:T(8,128)(2,1)}, bf16[128,1024]{1,0:T(8,128)(2,1)}, u32[]{:S(2)}, u32[]{:S(2)}) collective-permute-start(bf16[128,1024]{1,0:T(8,128)(2,1)} %get-tuple-element.110), channel_id=1, source_target_pairs={{0,2},{1,3},{2,0},{3,1},{4,6},{5,7},{6,4},{7,5},{8,10},{9,11},{10,... | collective-permute-start | bytes 786440 | tf_op jit(solution)/shard_map/ppermute | solution.py:23
  179.5 10.0 %collective-permute-start.16 = (bf16[128,1024]{1,0:T(8,128)(2,1)}, bf16[128,1024]{1,0:T(8,128)(2,1)}, u32[]{:S(2)}, u32[]{:S(2)}) collective-permute-start(bf16[128,1024]{1,0:T(8,128)(2,1)} %add_convert_fusion.1), channel_id=1, source_target_pairs={{0,1},{1,0},{2,3},{3,2},{4,5},{5,4},{6,7},{7,6},{8,9},{9,8},{10,11... | collective-permute-start | bytes 786440 | tf_op jit(solution)/shard_map/ppermute | solution.py:23
  185.6 8.9 %collective-permute-start.22 = (bf16[128,1024]{1,0:T(8,128)(2,1)}, bf16[128,1024]{1,0:T(8,128)(2,1)}, u32[]{:S(2)}, u32[]{:S(2)}) collective-permute-start(bf16[128,1024]{1,0:T(8,128)(2,1)} %get-tuple-element.110), channel_id=1, source_target_pairs={{0,1},{1,0},{2,3},{3,2},{4,5},{5,4},{6,7},{7,6},{8,9},{9,8},{10,11... | collective-permute-start | bytes 786440 | tf_op jit(solution)/shard_map/ppermute | solution.py:23
  204.0 9.2 %collective-permute-start.27 = (bf16[128,1024]{1,0:T(8,128)(2,1)S(1)}, bf16[128,1024]{1,0:T(8,128)(2,1)S(1)}, u32[]{:S(2)}, u32[]{:S(2)}) collective-permute-start(bf16[128,1024]{1,0:T(8,128)(2,1)S(1)} %fusion.41), channel_id=1, source_target_pairs={{0,2},{1,3},{2,0},{3,1},{4,6},{5,7},{6,4},{7,5},{8,10},{9,11},{10,... | collective-permute-start | bytes 786440 | tf_op jit(solution)/shard_map/ppermute | solution.py:23
  204.6 9.5 %collective-permute-start.19 = (bf16[128,1024]{1,0:T(8,128)(2,1)S(1)}, bf16[128,1024]{1,0:T(8,128)(2,1)S(1)}, u32[]{:S(2)}, u32[]{:S(2)}) collective-permute-start(bf16[128,1024]{1,0:T(8,128)(2,1)S(1)} %get-tuple-element.122), channel_id=1, source_target_pairs={{0,1},{1,0},{2,3},{3,2},{4,5},{5,4},{6,7},{7,6},{8,9},{9,8},{10,11... | collective-permute-start | bytes 786440 | tf_op jit(solution)/shard_map/ppermute | solution.py:23
  205.1 13.3 %collective-permute-start.21 = (bf16[128,1024]{1,0:T(8,128)(2,1)S(1)}, bf16[128,1024]{1,0:T(8,128)(2,1)S(1)}, u32[]{:S(2)}, u32[]{:S(2)}) collective-permute-start(bf16[128,1024]{1,0:T(8,128)(2,1)S(1)} %fusion.43), channel_id=1, source_target_pairs={{0,2},{1,3},{2,0},{3,1},{4,6},{5,7},{6,4},{7,5},{8,10},{9,11},{10,... | collective-permute-start | bytes 786440 | tf_op jit(solution)/shard_map/ppermute | solution.py:23
  220.2 7.9 %collective-permute-start.29 = (bf16[128,1024]{1,0:T(8,128)(2,1)S(1)}, bf16[128,1024]{1,0:T(8,128)(2,1)S(1)}, u32[]{:S(2)}, u32[]{:S(2)}) collective-permute-start(bf16[128,1024]{1,0:T(8,128)(2,1)S(1)} %get-tuple-element.112), channel_id=1, source_target_pairs={{0,2},{1,3},{2,0},{3,1},{4,6},{5,7},{6,4},{7,5},{8,10},{9,11},{10,... | collective-permute-start | bytes 786440 | tf_op jit(solution)/shard_map/ppermute | solution.py:23
  220.7 7.3 %collective-permute-start.28 = (bf16[128,1024]{1,0:T(8,128)(2,1)S(1)}, bf16[128,1024]{1,0:T(8,128)(2,1)S(1)}, u32[]{:S(2)}, u32[]{:S(2)}) collective-permute-start(bf16[128,1024]{1,0:T(8,128)(2,1)S(1)} %get-tuple-element.112), channel_id=1, source_target_pairs={{0,1},{1,0},{2,3},{3,2},{4,5},{5,4},{6,7},{7,6},{8,9},{9,8},{10,11... | collective-permute-start | bytes 786440 | tf_op jit(solution)/shard_map/ppermute | solution.py:23
  231.6 134.8 %reduce-scatter.9.cloned.1.call-start = ((), (), s32[]{:S(2)}) async-start(), calls=%async_computation.10 | async-start | bytes 2359296 | tf_op jit(solution)/shard_map/reduce_scatter | solution.py:611
  241.7 18.0 %all-to-all-start.2 = ((bf16[8,32,512]{2,1,0:T(8,128)(2,1)}), bf16[8,32,512]{2,1,0:T(8,128)(2,1)}, u32[]{:S(2)}, u32[]{:S(2)}) async-start(bf16[8,32,512]{2,1,0:T(8,128)(2,1)} %bitcast.479), calls=%async_computation.2 | async-start | bytes 524288 | tf_op jit(solution)/shard_map/all_to_all | solution.py:634
  247.2 190.1 %reduce-scatter.11.cloned.1.call-start = ((), (), s32[]{:S(2)}) async-start(), calls=%async_computation.11 | async-start | bytes 2359296 | tf_op jit(solution)/shard_map/reduce_scatter | solution.py:611
  254.7 45.0 %collective-permute-start.32 = (f32[256,128]{1,0:T(8,128)}, f32[256,128]{1,0:T(8,128)}, u32[]{:S(2)}, u32[]{:S(2)}) collective-permute-start(f32[256,128]{1,0:T(8,128)} %copy-done.25), channel_id=1, source_target_pairs={{0,28},{4,0},{8,4},{12,8},{16,12},{20,16},{24,20},{28,24},{1,29},{... | collective-permute-start | bytes 393224 | tf_op jit(solution)/shard_map/ppermute | solution.py:83
  282.7 13.2 %all-to-all-start.3 = ((bf16[8,32,512]{2,1,0:T(8,128)(2,1)}), bf16[8,32,512]{2,1,0:T(8,128)(2,1)S(1)}, u32[]{:S(2)}, u32[]{:S(2)}) async-start(bf16[8,32,512]{2,1,0:T(8,128)(2,1)} %copy-done.23), calls=%async_computation.3 | async-start | bytes 524288 | tf_op jit(solution)/shard_map/all_to_all | solution.py:636
  286.1 219.4 %reduce-scatter.5.cloned.1.call-start = ((), (), s32[]{:S(2)}) async-start(), calls=%async_computation.8 | async-start | bytes 1769472 | tf_op jit(solution)/shard_map/reduce_scatter | solution.py:611
  311.7 7.3 %collective-permute-start.33 = (bf16[128,1024]{1,0:T(8,128)(2,1)S(1)}, bf16[128,1024]{1,0:T(8,128)(2,1)S(1)}, u32[]{:S(2)}, u32[]{:S(2)}) collective-permute-start(bf16[128,1024]{1,0:T(8,128)(2,1)S(1)} %get-tuple-element.118), channel_id=1, source_target_pairs={{0,1},{1,0},{2,3},{3,2},{4,5},{5,4},{6,7},{7,6},{8,9},{9,8},{10,11... | collective-permute-start | bytes 786440 | tf_op jit(solution)/shard_map/ppermute | solution.py:23
  313.3 8.3 %collective-permute-start.35 = (bf16[128,1024]{1,0:T(8,128)(2,1)S(1)}, bf16[128,1024]{1,0:T(8,128)(2,1)S(1)}, u32[]{:S(2)}, u32[]{:S(2)}) collective-permute-start(bf16[128,1024]{1,0:T(8,128)(2,1)S(1)} %fusion.39), channel_id=1, source_target_pairs={{0,2},{1,3},{2,0},{3,1},{4,6},{5,7},{6,4},{7,5},{8,10},{9,11},{10,... | collective-permute-start | bytes 786440 | tf_op jit(solution)/shard_map/ppermute | solution.py:23
  333.2 7.8 %collective-permute-start.38 = (f32[272,128]{1,0:T(8,128)S(1)}, f32[272,128]{1,0:T(8,128)S(1)}, u32[]{:S(2)}, u32[]{:S(2)}) collective-permute-start(f32[272,128]{1,0:T(8,128)S(1)} %constant_dynamic-update-slice_fusion.29), channel_id=1, source_target_pairs={{0,16},{4,20},{8,24},{12,28},{16,0},{20,4},{24,8},{28,12},{1,17},{... | collective-permute-start | bytes 417800 | tf_op jit(solution)/shard_map/ppermute | solution.py:23
  342.6 8.3 %collective-permute-start.40 = (f32[504,128]{1,0:T(8,128)S(1)}, f32[504,128]{1,0:T(8,128)S(1)}, u32[]{:S(2)}, u32[]{:S(2)}) collective-permute-start(f32[504,128]{1,0:T(8,128)S(1)} %constant_dynamic-update-slice_fusion.40), channel_id=1, source_target_pairs={{0,2},{1,3},{2,0},{3,1},{4,6},{5,7},{6,4},{7,5},{8,10},{9,11},{10,... | collective-permute-start | bytes 774152 | tf_op jit(solution)/shard_map/ppermute | solution.py:23
  (123 other events, 1139.2 us)
Sparse Core Ops, SparseCore 0:
  16.1 49.7 all-gather.5
  123.4 51.5 all-gather.7
  231.7 64.7 reduce-scatter.6
  300.4 66.0 reduce-scatter.8
  370.2 66.9 reduce-scatter.10
  441.0 64.4 reduce-scatter.4

commit v2 on v1

--- a/solution.py
+++ b/solution.py
@@ -46,15 +46,18 @@
     return list(range(count))
 
 
+def ring_maps(count):
+    order = ring_order(count)
+    ahead = [(order[i], order[(i + 1) % count]) for i in range(count)]
+    return order, ahead, [(b, a) for a, b in ahead]
+
+
 def ring_gather(shard):
     count = lax.axis_size("seq")
     if count != 8:
         return lax.all_gather(shard, "seq", axis=0)
-    order = ring_order(count)
-    ahead = [(order[i], order[(i + 1) % count]) for i in range(count)]
-    back = [(b, a) for a, b in ahead]
-    me = lax.axis_index("seq")
-    place = jnp.asarray(np.argsort(order), jnp.int32)[me]
+    order, ahead, back = ring_maps(count)
+    place = jnp.asarray(np.argsort(order), jnp.int32)[lax.axis_index("seq")]
     owners = jnp.asarray(order, jnp.int32)
     full = jnp.zeros((count,) + shard.shape, shard.dtype)
 
@@ -76,6 +79,60 @@
     full = put(full, left, -(count // 2))
     full = put(full, right, count // 2, half)
     return full
+
+
+def ring_scatter(term):
+    count = lax.axis_size("seq")
+    if count != 8:
+        return lax.psum_scatter(term, "seq", scatter_dimension=0, tiled=True).astype(F32)
+    order, ahead, back = ring_maps(count)
+    place = jnp.asarray(np.argsort(order), jnp.int32)[lax.axis_index("seq")]
+    owners = jnp.asarray(order, jnp.int32)
+    rows = term.shape[0] // count
+    half = rows // 2
+
+    def mine(step, lo):
+        owner = owners[(place + step + 2 * count) % count]
+        return lax.dynamic_slice_in_dim(term, owner * rows + lo, half, 0)
+
+    left, right = mine(-1, 0), mine(1, half)
+    for step in range(2, count + 1):
+        left = lax.ppermute(left, "seq", ahead).astype(F32) + mine(-step, 0).astype(F32)
+        right = lax.ppermute(right, "seq", back).astype(F32) + mine(step, half).astype(F32)
+        if step < count:
+            left, right = left.astype(B16), right.astype(B16)
+    return jnp.concatenate([left, right], axis=0)
+
+
+def halve_scatter(term):
+    count = lax.axis_size("seq")
+    bits = count.bit_length() - 1
+    seq = lax.axis_index("seq")
+    rows = term.shape[0] // count
+    half = rows // 2
+    split = term.reshape((2,) * bits + (2, half, term.shape[1]))
+    results = []
+    for part, order in enumerate(([0] + list(range(bits - 1, 0, -1)), list(range(bits - 1, -1, -1)))):
+        value = lax.index_in_dim(split, part, bits, keepdims=False)
+        left = list(range(bits - 1, -1, -1))
+        for bit in order:
+            at = left.index(bit)
+            on = (seq >> bit) & 1
+            keep = lax.dynamic_index_in_dim(value, on, at, keepdims=False)
+            give = lax.dynamic_index_in_dim(value, 1 - on, at, keepdims=False)
+            value = keep.astype(F32) + swap(give, "seq", 1 << bit).astype(F32)
+            left.remove(bit)
+            if left:
+                value = value.astype(B16)
+        results.append(value)
+    return jnp.concatenate(results, axis=0)
+
+
+def spread_gather(shard):
+    count = lax.axis_size("seq")
+    copies = jnp.broadcast_to(shard[None], (count,) + shard.shape)
+    full = lax.all_to_all(copies, "seq", 0, 0, tiled=True)
+    return full.reshape((count * shard.shape[0],) + shard.shape[1:])
 
 
 def shift_seq(values, step):
@@ -180,6 +237,88 @@
     ) * jnp.exp(-ramp_unit[None, :] * local_rates[:, None])
 
 
+def sin_cos(x):
+    turns = jnp.floor(x * (1.0 / math.pi) + 0.5)
+    r = x - turns * 3.140625
+    r = r - turns * 9.67502593994140625e-4
+    r = r - turns * 1.509957990978376432e-7
+    sign = 1.0 - 2.0 * (turns - 2.0 * jnp.floor(turns * 0.5))
+    q = r * r
+    sin = r + r * q * (
+        -1.6666666666e-1
+        + q * (8.3333333e-3 + q * (-1.98412698e-4 + q * (2.7557319e-6 + q * -2.505210838e-8)))
+    )
+    cos = 1.0 + q * (
+        -0.5
+        + q * (4.16666666e-2 + q * (-1.3888888e-3 + q * (2.48015873e-5 + q * (-2.75573192e-7 + q * 2.0876757e-9))))
+    )
+    return sin * sign, cos * sign
+
+
+def dot_high(left, right, dims):
+    return lax.dot_general(left, right, (dims, ((), ())), precision=HIGH, preferred_element_type=F32)
+
+
+def filter_forward_kernel(
+    grid_ref, ramp_ref, rate_ref, w1_ref, w2_ref, w3_ref, small_ref, columns_ref, twist_ref, hi_ref, lo_ref,
+    spec_ref, sin_ref, cos_ref, z_ref
+):
+    blocks, length = twist_ref.shape[0], twist_ref.shape[3]
+    freq = small_ref[:, 3:4]
+    below = grid_ref[...]
+    for i, w_ref in enumerate((w1_ref, w2_ref, w3_ref)):
+        grown = dot_high(w_ref[...].T, below, ((1,), (0,)))
+        sin, cos = sin_cos(freq * (grown + small_ref[:, i : i + 1]))
+        sin_ref[i] = sin
+        cos_ref[i] = cos
+        below = sin
+    kern = dot_high(columns_ref[...].T, below, ((1,), (0,))) * jnp.exp(-rate_ref[...] * ramp_ref[...])
+    cut = [kern[:, b * length : (b + 1) * length] for b in range(blocks)]
+    turn_rows(cut, twist_ref, z_ref, 0, blocks)
+    spec_ref[...] = dot_split(z_ref[...], hi_ref[...], lo_ref[...], ((1,), (0,)))
+
+
+def filter_backward_kernel(
+    gk_ref, grid_ref, ramp_ref, rate_ref, w1_ref, w2_ref, w3_ref, small_ref, columns_ref, sin_ref, cos_ref,
+    gc_ref, g1_ref, g2_ref, g3_ref, gsmall_ref
+):
+    freq = small_ref[:, 3:4]
+    gk = jnp.concatenate([gk_ref[b] for b in range(gk_ref.shape[0])], axis=1)
+    gk = gk * jnp.exp(-rate_ref[...] * ramp_ref[...])
+    last = ((1,), (1,))
+    gc_ref[...] = dot_high(sin_ref[2], gk, last)
+    grad = dot_high(columns_ref[...], gk, ((1,), (0,)))
+    gfreq = jnp.zeros(freq.shape, F32)
+    gbias = [None] * 3
+    for i, w_ref, g_ref in ((2, w3_ref, g3_ref), (1, w2_ref, g2_ref), (0, w1_ref, g1_ref)):
+        turn = grad * cos_ref[i]
+        below = sin_ref[i - 1] if i else grid_ref[...]
+        raw = dot_high(turn, below, last)
+        total = jnp.sum(turn, axis=1, keepdims=True)
+        g_ref[...] = raw * freq
+        gbias[i] = total * freq
+        gfreq = gfreq + jnp.sum(raw * w_ref[...].T, axis=1, keepdims=True) + total * small_ref[:, i : i + 1]
+        if i:
+            grad = dot_high(w_ref[...], turn * freq, ((1,), (0,)))
+    gsmall_ref[...] = jnp.concatenate(gbias + [gfreq], axis=1)
+
+
+def feature_table(length, feat_count):
+    ramp = np.linspace(0.0, 1.0, length, dtype=np.float32)
+    angles = np.arange(length, dtype=np.float32)[:, None] * np.float32(2.0 * math.pi / length)
+    half = (feat_count - 1) // 2
+    bands = np.linspace(0.0001, half - 1.0, half, dtype=np.float32)[None, :]
+    phase = (bands * angles).astype(np.float64)
+    table = np.concatenate([ramp[:, None], np.cos(phase), -np.sin(phase)], axis=1)
+    return np.ascontiguousarray(table.T).astype(np.float32), ramp[None, :]
+
+
+def decay_rates(model):
+    return np.abs(
+        np.linspace(math.log(0.01) / 0.3, math.log(0.01) / 1.5, model, dtype=np.float32)
+    )[:, None]
+
+
 def transform_tables(blocks, length):
     time = np.arange(blocks * length).reshape(blocks, 1, length)
     cls = np.arange(blocks).reshape(1, blocks, 1)
@@ -191,6 +330,11 @@
     cos, sin = np.cos(turn), np.sin(turn)
     table = np.block([[cos, -sin], [sin, cos]]).astype(np.float32)
     return twist, table
+
+
+def split_table(table):
+    hi = table.astype(B16)
+    return jnp.asarray(hi), jnp.asarray((table - hi.astype(np.float32)).astype(B16))
 
 
 def spectrum_of(signal, twist, table):
@@ -314,8 +458,7 @@
             [signal_of(prod[:blocks], twist, table), signal_of(prod[blocks:], twist, table)], axis=0
         )
         return ((out + skip * x).astype(B16), spec)
-    hi = jnp.asarray(table).astype(B16)
-    lo = (jnp.asarray(table) - hi.astype(F32)).astype(B16)
+    hi, lo = split_table(table)
     height = 2 * blocks * rows
     out, spec = pl.pallas_call(
         partial(conv_forward_kernel, short_blocks),
@@ -343,8 +486,7 @@
         cross = times(first, spec[:blocks], True) + times(second, spec[blocks:], True)
         out = jnp.concatenate([one, two], axis=0) + skip * g
         return (out.astype(B16), signal_of(cross, twist, table))
-    hi = jnp.asarray(table).astype(B16)
-    lo = (jnp.asarray(table) - hi.astype(F32)).astype(B16)
+    hi, lo = split_table(table)
     span = blocks * rows
     out, grad_kern = pl.pallas_call(
         partial(conv_backward_kernel, short_blocks),
@@ -530,7 +672,7 @@
     mask_ext = jnp.pad(mask_ext, ((0, 6), (0, 0)))
 
     full_in = ring_gather(in_weight[0]).reshape(model, 3, width)
-    full_out = lax.all_gather(out_weight[0], "seq", axis=0, tiled=True)
+    full_out = spread_gather(out_weight[0])
     full_up = lax.all_gather(up_weight[0], "seq", axis=0, tiled=True)
     full_down = lax.all_gather(down_weight[0], "seq", axis=0, tiled=True)
 
@@ -565,21 +707,58 @@
 
     skip_local = lax.dynamic_slice_in_dim(skip_gain[0], chan_start, chan, 0)
     columns = lax.dynamic_slice_in_dim(kernel_weight[0], chan_start, chan, 1)
-    feature_grid, ramp_unit = features(seq_len, feat_weight.shape[1])
     twist, table = transform_tables(blocks, group)
-    kernel, kernel_pull = jax.vjp(
-        partial(filter_columns, feature_grid, ramp_unit, chan_start, chan, model),
-        feat_weight[0],
-        feat_bias[0],
-        inner_weight[0],
-        inner_bias[0],
-        deep_weight[0],
-        deep_bias[0],
-        sine_freq[0],
-        columns,
-    )
-    kern_blocks = kernel.reshape(chan, blocks, group).transpose(1, 0, 2)
-    kern_spec = spectrum_of(kern_blocks, twist, table)
+    nets = (feat_weight[0], inner_weight[0], deep_weight[0])
+    if blocks == 4:
+        grid, ramp = feature_table(seq_len, feat_weight.shape[1])
+        rates = lax.dynamic_slice_in_dim(jnp.asarray(decay_rates(model)), chan_start, chan, 0)
+        smalls = jnp.concatenate([feat_bias, inner_bias, deep_bias, sine_freq], axis=0).T
+        filt = smalls.shape[0]
+        hi, lo = split_table(table)
+        kern_spec, sines, cosines = pl.pallas_call(
+            filter_forward_kernel,
+            out_shape=(
+                jax.ShapeDtypeStruct((blocks * chan, 2 * group), F32),
+                jax.ShapeDtypeStruct((3, filt, seq_len), F32),
+                jax.ShapeDtypeStruct((3, filt, seq_len), F32),
+            ),
+            scratch_shapes=[pltpu.VMEM((blocks * chan, 2 * group), F32)],
+            compiler_params=pltpu.CompilerParams(vmem_limit_bytes=VMEM_BYTES),
+            cost_estimate=pl.CostEstimate(flops=10**6, bytes_accessed=10**6, transcendentals=0),
+            name="filter_forward",
+        )(grid, ramp, rates, *nets, smalls, columns, twist, hi, lo)
+        kern_spec = kern_spec.reshape(blocks, chan, 2 * group)
+
+        def kernel_pull(grad_kernel):
+            shapes = [columns.shape] + [w.shape[::-1] for w in nets] + [smalls.shape]
+            gcols, g1, g2, g3, gsmalls = pl.pallas_call(
+                filter_backward_kernel,
+                out_shape=tuple(jax.ShapeDtypeStruct(shape, F32) for shape in shapes),
+                compiler_params=pltpu.CompilerParams(vmem_limit_bytes=VMEM_BYTES),
+                cost_estimate=pl.CostEstimate(flops=10**6, bytes_accessed=10**6, transcendentals=0),
+                name="filter_backward",
+            )(grad_kernel, grid, ramp, rates, *nets, smalls, columns, sines, cosines)
+            gs = gsmalls.T
+            return (g1.T, gs[0], g2.T, gs[1], g3.T, gs[2], gs[3], gcols)
+
+    else:
+        feature_grid, ramp_unit = features(seq_len, feat_weight.shape[1])
+        kernel, pull = jax.vjp(
+            partial(filter_columns, feature_grid, ramp_unit, chan_start, chan, model),
+            feat_weight[0],
+            feat_bias[0],
+            inner_weight[0],
+            inner_bias[0],
+            deep_weight[0],
+            deep_bias[0],
+            sine_freq[0],
+            columns,
+        )
+        kern_spec = spectrum_of(kernel.reshape(chan, blocks, group).transpose(1, 0, 2), twist, table)
+
+        def kernel_pull(grad_kernel):
+            return pull(grad_kernel.transpose(1, 0, 2).reshape(chan, seq_len))
+
     mixed_chan, kept_spec = conv_forward(received, kern_spec, twist, table, skip_local)
     mixed = lax.all_to_all(mixed_chan, "seq", 0, 0, tiled=True).reshape(width, group)
     (y_cols,) = token_call(output_kernel, "output", common + [(mixed, True)], [flat_shape])
@@ -604,14 +783,14 @@
     layer_out = (middle + (scatter_rel(mlp_part) + down_bias[0])).astype(B16)
     term_down = jnp.einsum("to,tf->of", mlp_rows, act_rows, preferred_element_type=F32)
     term_up = jnp.einsum("td,tf->df", rows_two, grad_pre, preferred_element_type=F32)
+    grad_two, term_down = lax.optimization_barrier((grad_two, term_down.astype(B16)))
     grad_down_bias = jnp.sum(grad_mlp.astype(F32), axis=0)
     grad_up_block = jnp.sum(grad_pre.astype(F32), axis=0)
 
-    def to_owner(term):
-        return lax.psum_scatter(term.astype(B16), "seq", scatter_dimension=0, tiled=True).astype(F32)
-
-    grad_up = to_owner(term_up)
-    grad_down = to_owner(term_down)
+    grad_down = lax.psum_scatter(
+        term_down, "seq", scatter_dimension=0, tiled=True
+    ).astype(F32)
+    grad_up = ring_scatter(term_up.astype(B16))
 
     grad_unit_two, grad_gain_two, grad_shift_two = norm_back(
         grad_two, unit_two, scale_two, norm2_gain[0]
@@ -622,7 +801,7 @@
     mix_rows = gather_rel(grad_mix)
     gy_cols = jnp.einsum("to,oc->ct", mix_rows, full_out, preferred_element_type=F32).astype(B16)
     term_out = jnp.einsum("to,ct->oc", mix_rows, y_cols, preferred_element_type=F32)
-    grad_out = to_owner(term_out)
+    grad_out = halve_scatter(term_out.astype(B16))
 
     grad_mixed, gate_first = token_call(
         grad_mix_kernel,
@@ -635,7 +814,7 @@
     ggated_chan, grad_kernel = conv_backward(grads_chan, kept_spec, kern_spec, twist, table, skip_local)
     ggated = lax.all_to_all(ggated_chan, "seq", 0, 0, tiled=True).reshape(width, group)
     ggated_next = shift_seq(ggated[:, :LANE], -1)
-    kernel_grads = kernel_pull(grad_kernel.transpose(1, 0, 2).reshape(chan, seq_len))
+    kernel_grads = kernel_pull(grad_kernel)
     grad_proj, col_sums = token_call(
         grad_proj_kernel,
         "grad_proj",
@@ -647,7 +826,8 @@
     one_part = jnp.einsum("pct,dpc->td", grad_proj, full_in, preferred_element_type=F32)
     grad_one = scatter_rel(one_part)
     term_in = jnp.einsum("td,pct->dpc", rows_one, grad_proj, preferred_element_type=F32)
-    grad_in = to_owner(term_in)
+    grad_in = halve_scatter(term_in.reshape(model, 3 * width).astype(B16))
+    grad_in = grad_in.reshape(-1, 3, width)
     grad_unit_one, grad_gain_one, grad_shift_one = norm_back(
         grad_one, unit_one, scale_one, norm1_gain[0]
     )

time: 524 us -> 449 us (0.86)
  waiting for transfers between devices: 216 us -> 119 us
  matrix products: 70.3 us -> 31.8 us
  local copies, waits for them, and re-layouts: 42.3 us -> 71.8 us
  starting transfers between devices: 58 us -> 79.3 us
  blocking collectives: 34.8 us -> 14 us
  between operations: 41.6 us -> 58.7 us
  Pallas kernels: 25.9 us -> 34.1 us
  other arithmetic: 25.4 us -> 32.8 us
    reduce_scatter x4 -> x1, waiting for transfers between devices: 141 us -> 0.01 us  [per_device(): lax.psum_scatter(term_down, 'seq', scatter_dimension=0, tiled=True)]
    dot_general x13 -> x0, matrix products: 38.2 us -> none  [the longest x8 18.6 us: layer(): lax.dot_general(weight, below, (((0,), (0,)), ((), ())), precision=HIGH)]
    all_gather x1 -> x0, blocking collectives: 34.8 us -> none  [per_device(): full_out = lax.all_gather(out_weight[0], 'seq', axis=0, tiled=True)]
    unnamed x288 -> x289, local copies, waits for them, and re-layouts: 20.2 us -> 35.7 us
    ppermute x29 -> x41, waiting for transfers between devices: 61.3 us -> 76.2 us  [swap(): return lax.ppermute(values, axis_name, [(i, i ^ bit) for i in range(size)])]
    ppermute x0 -> x14, starting transfers between devices: none -> 14.6 us  [the longest x7 8.26 us: ring_scatter(): lax.ppermute(right, 'seq', back).astype(F32) + mine(step, half).astype(F32)]
    all_to_all x0 -> x1, blocking collectives: none -> 14 us  [per_device(): lax.all_to_all(mixed_chan, 'seq', 0, 0, tiled=True).reshape(width, group)]
    pallas_call x0 -> x2, Pallas kernels: none -> 10.7 us  [the longest x1 6.75 us: per_device(): pl.pallas_call(filter_forward_kernel, out_shape=(jax.ShapeDtypeStruct((bl...]
  transfers between devices with their start and end apart: 51 -> 74, of which waited for: 24 -> 33; matrix products, arithmetic and copies ran while one was open for 22% -> 24% of each run, Pallas kernels for 5% -> 8%
where the time goes in v2:
time: 449 us; the launch traced here: 442 us
  waiting for transfers between devices  119 us (27%)
  starting transfers between devices  79.3 us (18%)
  local copies, waits for them, and re-layouts  71.8 us (16%)
  between operations  58.7 us (13%)
  Pallas kernels  34.1 us (8%)
  other arithmetic  32.8 us (7%)
  matrix products  31.8 us (7%)
  blocking collectives  14 us (3%)
    ppermute x41, waiting for transfers between devices, swap(): return lax.ppermute(values, axis_name, [(i, i ^ bit) for i in range(size)])  76.2 us
    unnamed x289, local copies, waits for them, and re-layouts  35.7 us
    ppermute x41, starting transfers between devices, swap(): return lax.ppermute(values, axis_name, [(i, i ^ bit) for i in range(size)])  26.1 us
    all_to_all x1, blocking collectives, per_device(): lax.all_to_all(mixed_chan, 'seq', 0, 0, tiled=True).reshape(width, group)  14 us
    ppermute x4, starting transfers between devices, shift_seq(): lax.ppermute(values, 'seq', [(i, (i + step) % count) for i in range(count)])  12 us
    all_to_all x1, waiting for transfers between devices, per_device(): lax.all_to_all(ggated_chan, 'seq', 0, 0, tiled=True).reshape(width, group)  10.5 us
    pallas_call x4, Pallas kernels, token_call(): pl.pallas_call(kernel, grid=(width // step,), in_specs=[pl.BlockSpec(memo...  10.5 us
  transfers between devices with their start and end apart: 74, of which 33 were waited for; matrix products, arithmetic and copies ran while one was open for 24% of the time, Pallas kernels for 8%

profile of v2, /device:TPU:0, one launch (start us, length us, event | category | flops | bytes accessed | tf_op | source)
XLA Modules:
  0.0 442.0 jit_solution(14566421975757713331)
XLA Ops:
  7.3 3.1 collective-permute-start
  56.1 7.7 %collective-permute-done.2 = bf16[128,3,256]{2,0,1:T(8,128)(2,1)S(1)} collective-permute-done((bf16[128,3,256]{2,0,1:T(8,128)(2,1)S(1)}, bf16[128,3,256]{2,0,1:T(8,128)(2,1)S(1)}, u32[]{:S(2)}, u32[]{:S(2)}) %collective-permute-start.2) | collective-permute-done | bytes 196640 | tf_op jit(solution)/shard_map/ppermute | solution.py:72
  63.8 3.7 collective-permute-start.4
  71.0 2.7 collective-permute-start.12
  85.1 4.5 %all-to-all-start = ((bf16[8,32,512]{2,1,0:T(8,128)(2,1)}), bf16[8,32,512]{2,1,0:T(8,128)(2,1)S(1)}, u32[]{:S(2)}, u32[]{:S(2)}) async-start(bf16[8,32,512]{2,1,0:T(8,128)(2,1)} %bitcast.48), calls=%async_computation | async-start | bytes 524288 | tf_op jit(solution)/shard_map/all_to_all | solution.py:706
  98.7 6.7 %filter_forward.1 = (f32[128,1024]{1,0:T(8,128)S(1)}, f32[3,64,2048]{2,1,0:T(8,128)S(1)}, f32[3,64,2048]{2,1,0:T(8,128)S(1)}) custom-call(f32[33,2048]{1,0:T(8,128)S(1)} %copy-done.14, f32[1,2048]{1,0:T(1,128)S(1)} %copy-done.42, f32[32,1]{1,0:T(8,128)S(1)} %constant_dynamic-slice_fusion.4.rate_ref, f32[33,64]{1,0:T(8,128)S(1)} %bitcast.540, ...), custom_call_target="tpu_custom_call" | custom-call | flops 1000000 | bytes 1000000 | tf_op jit(solution)/shard_map/filter_forward/pallas_call | solution.py:718
  111.9 5.6 %conv_forward.1 = (bf16[8,32,512]{2,1,0:T(8,128)(2,1)S(1)}, f32[256,1024]{1,0:T(8,128)S(1)}) custom-call(bf16[8,32,512]{2,1,0:T(8,128)(2,1)S(1)} %all-to-all-done.x_ref, f32[128,1024]{1,0:T(8,128)S(1)} %copy-done.8, f32[4,4,2,512]{3,2,1,0:T(2,128)S(1)} %copy-done.27, bf16[1024,1024]{1,0:T(8,128)(2,1)S(1)} %copy-done.2, ...), custom_call_target="tpu_custom_call" | custom-call | tf_op jit(solution)/shard_map/conv_forward/pallas_call | solution.py:463
  118.4 14.0 %all_to_all.25 = bf16[8,32,512]{2,1,0:T(8,128)(2,1)S(1)} all-to-all(bf16[8,32,512]{2,1,0:T(8,128)(2,1)S(1)} %get-tuple-element.44), channel_id=1, replica_groups=mesh['seq'=8,'rep'=4] {'seq'}, dimensions={0} | all-to-all | bytes 524288 | tf_op jit(solution)/shard_map/all_to_all | solution.py:763
  133.3 4.1 all-to-all-start.2
  142.0 6.4 %all-to-all-done.2 = bf16[8,128,256]{2,1,0:T(8,128)(2,1)} async-done(((bf16[8,128,256]{2,1,0:T(8,128)(2,1)}), bf16[8,128,256]{2,1,0:T(8,128)(2,1)}, u32[]{:S(2)}, u32[]{:S(2)}) %all-to-all-start.2) | async-done | bytes 524320 | tf_op jit(solution)/shard_map/all_to_all | solution.py:134
  154.6 7.5 %collective-permute-done.15 = bf16[128,1024]{1,0:T(8,128)(2,1)} collective-permute-done((bf16[128,1024]{1,0:T(8,128)(2,1)}, bf16[128,1024]{1,0:T(8,128)(2,1)}, u32[]{:S(2)}, u32[]{:S(2)}) %collective-permute-start.15) | collective-permute-done | bytes 262176 | tf_op jit(solution)/shard_map/ppermute | solution.py:23
  168.8 6.1 %collective-permute-done.17 = bf16[128,1024]{1,0:T(8,128)(2,1)} collective-permute-done((bf16[128,1024]{1,0:T(8,128)(2,1)}, bf16[128,1024]{1,0:T(8,128)(2,1)}, u32[]{:S(2)}, u32[]{:S(2)}) %collective-permute-start.17) | collective-permute-done | bytes 262176 | tf_op jit(solution)/shard_map/ppermute | solution.py:23
  188.6 5.0 %multiply_convert_fusion = (bf16[512,1024]{1,0:T(8,128)(2,1)}, f32[512,1024]{1,0:T(8,128)}) fusion(f32[1024]{0:T(1024)} %bitcast.609, bf16[1,1024,1024]{2,1,0:T(8,128)(2,1)} %all-gather.5.cloned.1.call-done, bf16[128,1024]{1,0:T(8,128)(2,1)} %collective-permute-done.18, bf16[128,1024]{1,0:T(8,128)(2,1)} %collective-permute-done.17, ...), kind=kOutput, calls=%fused_computation.16 | convolution fusion | flops 1081081856 | bytes 6295552 | tf_op jit(solution)/shard_map/dot_general | solution.py:776
  193.6 5.0 %convert_reduce_fusion = (f32[1024]{0:T(1024)}, bf16[512,1024]{1,0:T(8,128)(2,1)S(1)}) fusion(f32[512,1024]{1,0:T(8,128)} %get-tuple-element.251, f32[1024]{0:T(1024)} %bitcast.610, bf16[1,1024,1024]{2,1,0:T(8,128)(2,1)} %all-gather.7.cloned.1.call-done, bf16[128,1024]{1,0:T(8,128)(2,1)} %collective-permute-done.24, ...), kind=kOutput, calls=%fused_computation.15 | convolution fusion | flops 1084750848 | bytes 6299648 | tf_op jit(solution)/shard_map/dot_general | solution.py:774
  198.6 2.6 convolution_convert_fusion
  203.4 2.6 fusion.89
  206.9 2.6 fusion.88
  213.6 3.9 convolution_convert_fusion.1
  266.5 4.0 all-to-all-start.3
  270.6 4.6 %collective-permute-start.32 = (f32[256,128]{1,0:T(8,128)}, f32[256,128]{1,0:T(8,128)}, u32[]{:S(2)}, u32[]{:S(2)}) collective-permute-start(f32[256,128]{1,0:T(8,128)} %copy-done.44), channel_id=1, source_target_pairs={{0,28},{4,0},{8,4},{12,8},{16,12},{20,16},{24,20},{28,24},{1,29},{... | collective-permute-start | bytes 393224 | tf_op jit(solution)/shard_map/ppermute | solution.py:140
  279.7 15.4 %collective-permute-done.48 = bf16[2,64,256]{2,1,0:T(8,128)(2,1)S(1)} collective-permute-done((bf16[2,64,256]{2,1,0:T(8,128)(2,1)S(1)}, bf16[2,64,256]{2,1,0:T(8,128)(2,1)S(1)}, u32[]{:S(2)}, u32[]{:S(2)}) %collective-permute-start.48) | collective-permute-done | bytes 65568 | tf_op jit(solution)/shard_map/ppermute | solution.py:23
  295.4 3.8 collective-permute-done.49
  303.9 7.4 %conv_backward.1 = (bf16[8,32,512]{2,1,0:T(8,128)(2,1)}, f32[4,32,512]{2,1,0:T(8,128)S(1)}) custom-call(bf16[8,32,512]{2,1,0:T(8,128)(2,1)} %all-to-all-done.3.g_ref, f32[256,1024]{1,0:T(8,128)S(1)} %copy-done.19, f32[128,1024]{1,0:T(8,128)S(1)} %copy-done.9, f32[4,4,2,512]{3,2,1,0:T(2,128)S(1)} %copy-done.28, bf16[1024,1024]{1,0:T(8,128)(2,1)S(1)} %copy-done.2, ...), custom_call_target="tpu_custom_call" | custom-call | tf_op jit(solution)/shard_map/conv_backward/pallas_call | solution.py:491
  311.4 3.9 filter_backward.1
  316.3 3.5 all-to-all-start.4
  323.1 10.5 %all-to-all-done.4 = bf16[8,32,512]{2,1,0:T(8,128)(2,1)S(1)} async-done(((bf16[8,32,512]{2,1,0:T(8,128)(2,1)}), bf16[8,32,512]{2,1,0:T(8,128)(2,1)S(1)}, u32[]{:S(2)}, u32[]{:S(2)}) %all-to-all-start.4) | async-done | bytes 262176 | tf_op jit(solution)/shard_map/all_to_all | solution.py:815
  338.2 6.1 %grad_proj.1 = (bf16[3,256,512]{2,1,0:T(8,128)(2,1)S(1)}, f32[256,16]{1,0:T(8,128)S(1)}) custom-call(s32[1]{0:T(128)} %bitcast.rep_ref, bf16[3,256,512]{2,1,0:T(8,128)(2,1)S(1)} %add_convert_fusion.proj_ref, bf16[3,256,256]{2,1,0:T(8,128)(2,1)S(1)} %fusion.16.halo_ref, f32[256,16]{1,0:T(8,128)S(1)} %copy-done.6, f32[8,768]{1,0:T(8,128)S(1)} %copy-done.25, ...), custom_call_target="tpu_custom_call" | custom-call | tf_op jit(solution)/shard_map/grad_proj/pallas_call | solution.py:610
  350.0 2.9 convert_element_type.423
  364.4 5.2 %collective-permute-done.36 = bf16[2,2,64,768]{3,2,1,0:T(8,128)(2,1)S(1)} collective-permute-done((bf16[2,2,64,768]{3,2,1,0:T(8,128)(2,1)}, bf16[2,2,64,768]{3,2,1,0:T(8,128)(2,1)S(1)}, u32[]{:S(2)}, u32[]{:S(2)}) %collective-permute-start.36) | collective-permute-done | bytes 393248 | tf_op jit(solution)/shard_map/ppermute | solution.py:23
  369.8 17.3 %collective-permute-done.39 = bf16[2,2,64,768]{3,2,1,0:T(8,128)(2,1)S(1)} collective-permute-done((bf16[2,2,64,768]{3,2,1,0:T(8,128)(2,1)S(1)}, bf16[2,2,64,768]{3,2,1,0:T(8,128)(2,1)S(1)}, u32[]{:S(2)}, u32[]{:S(2)}) %collective-permute-start.39) | collective-permute-done | bytes 393248 | tf_op jit(solution)/shard_map/ppermute | solution.py:23
  407.3 6.0 %collective-permute-done.44 = f32[272,128]{1,0:T(8,128)S(1)} collective-permute-done((f32[272,128]{1,0:T(8,128)S(1)}, f32[272,128]{1,0:T(8,128)S(1)}, u32[]{:S(2)}, u32[]{:S(2)}) %collective-permute-start.44) | collective-permute-done | bytes 139296 | tf_op jit(solution)/shard_map/ppermute | solution.py:23
  416.6 6.7 %collective-permute-done.46 = f32[504,128]{1,0:T(8,128)S(1)} collective-permute-done((f32[504,128]{1,0:T(8,128)S(1)}, f32[504,128]{1,0:T(8,128)S(1)}, u32[]{:S(2)}, u32[]{:S(2)}) %collective-permute-start.46) | collective-permute-done | bytes 258080 | tf_op jit(solution)/shard_map/ppermute | solution.py:23
  (596 shorter events, 191.9 us)
Async XLA Ops:
  7.2 181.3 %all-gather.5.cloned.1.call-start = ((), (), s32[]{:S(2)}) async-start(), calls=%async_computation.7 | async-start | bytes 2359296 | tf_op jit(solution)/shard_map/all_gather | solution.py:676
  7.3 46.5 %collective-permute-start = (bf16[128,3,256]{2,0,1:T(8,128)(2,1)}, bf16[128,3,256]{2,0,1:T(8,128)(2,1)S(1)}, u32[]{:S(2)}, u32[]{:S(2)}) collective-permute-start(bf16[128,3,256]{2,0,1:T(8,128)(2,1)} %bitcast.567), channel_id=1, source_target_pairs={{0,8},{8,16},{16,24},{24,28},{28,20},{20,12},{12,4},{4,0},{1,9},{9... | collective-permute-start | bytes 589832 | tf_op jit(solution)/shard_map/ppermute | solution.py:72
  10.3 45.1 %collective-permute-start.1 = (bf16[128,3,256]{2,0,1:T(8,128)(2,1)}, bf16[128,3,256]{2,0,1:T(8,128)(2,1)S(1)}, u32[]{:S(2)}, u32[]{:S(2)}) collective-permute-start(bf16[128,3,256]{2,0,1:T(8,128)(2,1)} %bitcast.568), channel_id=1, source_target_pairs={{8,0},{16,8},{24,16},{28,24},{20,28},{12,20},{4,12},{0,4},{9,1},{1... | collective-permute-start | bytes 589832 | tf_op jit(solution)/shard_map/ppermute | solution.py:73
  13.8 42.1 %collective-permute-start.9 = (bf16[128,1024]{1,0:T(8,128)(2,1)S(1)}, bf16[128,1024]{1,0:T(8,128)(2,1)S(1)}, u32[]{:S(2)}, u32[]{:S(2)}) collective-permute-start(bf16[128,1024]{1,0:T(8,128)(2,1)S(1)} %fusion.29), channel_id=1, source_target_pairs={{0,2},{1,3},{2,0},{3,1},{4,6},{5,7},{6,4},{7,5},{8,10},{9,11},{10,... | collective-permute-start | bytes 786440 | tf_op jit(solution)/shard_map/ppermute | solution.py:23
  15.9 52.9 %collective-permute-start.8 = (bf16[128,1024]{1,0:T(8,128)(2,1)S(1)}, bf16[128,1024]{1,0:T(8,128)(2,1)S(1)}, u32[]{:S(2)}, u32[]{:S(2)}) collective-permute-start(bf16[128,1024]{1,0:T(8,128)(2,1)S(1)} %fusion.29), channel_id=1, source_target_pairs={{0,1},{1,0},{2,3},{3,2},{4,5},{5,4},{6,7},{7,6},{8,9},{9,8},{10,11... | collective-permute-start | bytes 786440 | tf_op jit(solution)/shard_map/ppermute | solution.py:23
  55.5 13.0 %collective-permute-start.3 = (bf16[128,3,256]{2,0,1:T(8,128)(2,1)S(1)}, bf16[128,3,256]{2,0,1:T(8,128)(2,1)S(1)}, u32[]{:S(2)}, u32[]{:S(2)}) collective-permute-start(bf16[128,3,256]{2,0,1:T(8,128)(2,1)S(1)} %collective-permute-done.1), channel_id=1, source_target_pairs={{8,0},{16,8},{24,16},{28,24},{20,28},{12,20},{4,12},{0,4},{9,1},{1... | collective-permute-start | bytes 589832 | tf_op jit(solution)/shard_map/ppermute | solution.py:73
  56.0 12.8 %collective-permute-start.10 = (bf16[128,1024]{1,0:T(8,128)(2,1)S(1)}, bf16[128,1024]{1,0:T(8,128)(2,1)S(1)}, u32[]{:S(2)}, u32[]{:S(2)}) collective-permute-start(bf16[128,1024]{1,0:T(8,128)(2,1)S(1)} %collective-permute-done.9), channel_id=1, source_target_pairs={{0,1},{1,0},{2,3},{3,2},{4,5},{5,4},{6,7},{7,6},{8,9},{9,8},{10,11... | collective-permute-start | bytes 786440 | tf_op jit(solution)/shard_map/ppermute | solution.py:23
  85.1 24.1 %all-to-all-start = ((bf16[8,32,512]{2,1,0:T(8,128)(2,1)}), bf16[8,32,512]{2,1,0:T(8,128)(2,1)S(1)}, u32[]{:S(2)}, u32[]{:S(2)}) async-start(bf16[8,32,512]{2,1,0:T(8,128)(2,1)} %bitcast.48), calls=%async_computation | async-start | bytes 524288 | tf_op jit(solution)/shard_map/all_to_all | solution.py:706
  133.3 15.1 %all-to-all-start.2 = ((bf16[8,128,256]{2,1,0:T(8,128)(2,1)}), bf16[8,128,256]{2,1,0:T(8,128)(2,1)}, u32[]{:S(2)}, u32[]{:S(2)}) async-start(bf16[8,128,256]{2,1,0:T(8,128)(2,1)} %broadcast_in_dim.85), calls=%async_computation.2 | async-start | bytes 1048576 | tf_op jit(solution)/shard_map/all_to_all | solution.py:134
  137.4 56.2 %all-gather.7.cloned.1.call-start = ((), (), s32[]{:S(2)}) async-start(), calls=%async_computation.8 | async-start | bytes 2359296 | tf_op jit(solution)/shard_map/all_gather | solution.py:677
  138.2 295.3 %reduce-scatter.2.cloned.1.call-start = ((), (), s32[]{:S(2)}) async-start(), calls=%async_computation.6 | async-start | bytes 2359296 | tf_op jit(solution)/shard_map/reduce_scatter | solution.py:790
  167.9 20.6 %collective-permute-start.23 = (bf16[128,1024]{1,0:T(8,128)(2,1)}, bf16[128,1024]{1,0:T(8,128)(2,1)}, u32[]{:S(2)}, u32[]{:S(2)}) collective-permute-start(bf16[128,1024]{1,0:T(8,128)(2,1)} %get-tuple-element.128), channel_id=1, source_target_pairs={{0,2},{1,3},{2,0},{3,1},{4,6},{5,7},{6,4},{7,5},{8,10},{9,11},{10,... | collective-permute-start | bytes 786440 | tf_op jit(solution)/shard_map/ppermute | solution.py:23
  168.8 19.7 %collective-permute-start.16 = (bf16[128,1024]{1,0:T(8,128)(2,1)}, bf16[128,1024]{1,0:T(8,128)(2,1)}, u32[]{:S(2)}, u32[]{:S(2)}) collective-permute-start(bf16[128,1024]{1,0:T(8,128)(2,1)} %add_convert_fusion.1), channel_id=1, source_target_pairs={{0,1},{1,0},{2,3},{3,2},{4,5},{5,4},{6,7},{7,6},{8,9},{9,8},{10,11... | collective-permute-start | bytes 786440 | tf_op jit(solution)/shard_map/ppermute | solution.py:23
  174.9 13.6 %collective-permute-start.18 = (bf16[128,1024]{1,0:T(8,128)(2,1)}, bf16[128,1024]{1,0:T(8,128)(2,1)}, u32[]{:S(2)}, u32[]{:S(2)}) collective-permute-start(bf16[128,1024]{1,0:T(8,128)(2,1)} %collective-permute-done.17), channel_id=1, source_target_pairs={{0,1},{1,0},{2,3},{3,2},{4,5},{5,4},{6,7},{7,6},{8,9},{9,8},{10,11... | collective-permute-start | bytes 786440 | tf_op jit(solution)/shard_map/ppermute | solution.py:23
  174.9 18.7 %collective-permute-start.22 = (bf16[128,1024]{1,0:T(8,128)(2,1)}, bf16[128,1024]{1,0:T(8,128)(2,1)}, u32[]{:S(2)}, u32[]{:S(2)}) collective-permute-start(bf16[128,1024]{1,0:T(8,128)(2,1)} %get-tuple-element.128), channel_id=1, source_target_pairs={{0,1},{1,0},{2,3},{3,2},{4,5},{5,4},{6,7},{7,6},{8,9},{9,8},{10,11... | collective-permute-start | bytes 786440 | tf_op jit(solution)/shard_map/ppermute | solution.py:23
  206.9 21.1 %collective-permute-start.20 = (bf16[128,1024]{1,0:T(8,128)(2,1)}, bf16[128,1024]{1,0:T(8,128)(2,1)}, u32[]{:S(2)}, u32[]{:S(2)}) collective-permute-start(bf16[128,1024]{1,0:T(8,128)(2,1)} %get-tuple-element.158), channel_id=1, source_target_pairs={{0,1},{1,0},{2,3},{3,2},{4,5},{5,4},{6,7},{7,6},{8,9},{9,8},{10,11... | collective-permute-start | bytes 786440 | tf_op jit(solution)/shard_map/ppermute | solution.py:23
  210.8 24.2 %collective-permute-start.25 = (bf16[128,1024]{1,0:T(8,128)(2,1)}, bf16[128,1024]{1,0:T(8,128)(2,1)}, u32[]{:S(2)}, u32[]{:S(2)}) collective-permute-start(bf16[128,1024]{1,0:T(8,128)(2,1)} %get-tuple-element.155), channel_id=1, source_target_pairs={{0,1},{1,0},{2,3},{3,2},{4,5},{5,4},{6,7},{7,6},{8,9},{9,8},{10,11... | collective-permute-start | bytes 786440 | tf_op jit(solution)/shard_map/ppermute | solution.py:23
  217.8 25.4 %collective-permute-start.19 = (bf16[128,1024]{1,0:T(8,128)(2,1)}, bf16[128,1024]{1,0:T(8,128)(2,1)S(1)}, u32[]{:S(2)}, u32[]{:S(2)}) collective-permute-start(bf16[128,1024]{1,0:T(8,128)(2,1)} %get-tuple-element.157), channel_id=1, source_target_pairs={{0,1},{1,0},{2,3},{3,2},{4,5},{5,4},{6,7},{7,6},{8,9},{9,8},{10,11... | collective-permute-start | bytes 786440 | tf_op jit(solution)/shard_map/ppermute | solution.py:23
  224.9 11.4 %collective-permute-start.27 = (bf16[128,1024]{1,0:T(8,128)(2,1)S(1)}, bf16[128,1024]{1,0:T(8,128)(2,1)S(1)}, u32[]{:S(2)}, u32[]{:S(2)}) collective-permute-start(bf16[128,1024]{1,0:T(8,128)(2,1)S(1)} %fusion.38), channel_id=1, source_target_pairs={{0,2},{1,3},{2,0},{3,1},{4,6},{5,7},{6,4},{7,5},{8,10},{9,11},{10,... | collective-permute-start | bytes 786440 | tf_op jit(solution)/shard_map/ppermute | solution.py:23
  260.0 15.3 %collective-permute-start.47 = (bf16[2,2,64,256]{3,2,1,0:T(8,128)(2,1)}, bf16[2,2,64,256]{3,2,1,0:T(8,128)(2,1)}, u32[]{:S(2)}, u32[]{:S(2)}) collective-permute-start(bf16[2,2,64,256]{3,2,1,0:T(8,128)(2,1)} %dynamic-slice_bitcast_fusion.5), channel_id=1, source_target_pairs={{0,4},{4,0},{8,12},{12,8},{16,20},{20,16},{24,28},{28,24},{1,5},{5... | collective-permute-start | bytes 393224 | tf_op jit(solution)/shard_map/ppermute | solution.py:23
  261.4 17.2 %collective-permute-start.50 = (bf16[2,2,64,256]{3,2,1,0:T(8,128)(2,1)}, bf16[2,2,64,256]{3,2,1,0:T(8,128)(2,1)}, u32[]{:S(2)}, u32[]{:S(2)}) collective-permute-start(bf16[2,2,64,256]{3,2,1,0:T(8,128)(2,1)} %dynamic-slice_bitcast_fusion.4), channel_id=1, source_target_pairs={{0,16},{4,20},{8,24},{12,28},{16,0},{20,4},{24,8},{28,12},{1,17},{... | collective-permute-start | bytes 393224 | tf_op jit(solution)/shard_map/ppermute | solution.py:23
  266.5 33.5 %all-to-all-start.3 = ((bf16[8,32,512]{2,1,0:T(8,128)(2,1)}), bf16[8,32,512]{2,1,0:T(8,128)(2,1)}, u32[]{:S(2)}, u32[]{:S(2)}) async-start(bf16[8,32,512]{2,1,0:T(8,128)(2,1)} %bitcast.539), calls=%async_computation.3 | async-start | bytes 524288 | tf_op jit(solution)/shard_map/all_to_all | solution.py:813
  270.6 66.2 %collective-permute-start.32 = (f32[256,128]{1,0:T(8,128)}, f32[256,128]{1,0:T(8,128)}, u32[]{:S(2)}, u32[]{:S(2)}) collective-permute-start(f32[256,128]{1,0:T(8,128)} %copy-done.44), channel_id=1, source_target_pairs={{0,28},{4,0},{8,4},{12,8},{16,12},{20,16},{24,20},{28,24},{1,29},{... | collective-permute-start | bytes 393224 | tf_op jit(solution)/shard_map/ppermute | solution.py:140
  276.3 18.9 %collective-permute-start.48 = (bf16[2,64,256]{2,1,0:T(8,128)(2,1)S(1)}, bf16[2,64,256]{2,1,0:T(8,128)(2,1)S(1)}, u32[]{:S(2)}, u32[]{:S(2)}) collective-permute-start(bf16[2,64,256]{2,1,0:T(8,128)(2,1)S(1)} %dynamic-slice_bitcast_fusion.9), channel_id=1, source_target_pairs={{0,16},{4,20},{8,24},{12,28},{16,0},{20,4},{24,8},{28,12},{1,17},{... | collective-permute-start | bytes 196616 | tf_op jit(solution)/shard_map/ppermute | solution.py:23
  279.6 15.6 %collective-permute-start.51 = (bf16[2,64,256]{2,1,0:T(8,128)(2,1)S(1)}, bf16[2,64,256]{2,1,0:T(8,128)(2,1)S(1)}, u32[]{:S(2)}, u32[]{:S(2)}) collective-permute-start(bf16[2,64,256]{2,1,0:T(8,128)(2,1)S(1)} %dynamic-slice_bitcast_fusion.8), channel_id=1, source_target_pairs={{0,8},{4,12},{8,0},{12,4},{16,24},{20,28},{24,16},{28,20},{1,9},{5... | collective-permute-start | bytes 196616 | tf_op jit(solution)/shard_map/ppermute | solution.py:23
  316.3 17.3 %all-to-all-start.4 = ((bf16[8,32,512]{2,1,0:T(8,128)(2,1)}), bf16[8,32,512]{2,1,0:T(8,128)(2,1)S(1)}, u32[]{:S(2)}, u32[]{:S(2)}) async-start(bf16[8,32,512]{2,1,0:T(8,128)(2,1)} %get-tuple-element.48), calls=%async_computation.4 | async-start | bytes 524288 | tf_op jit(solution)/shard_map/all_to_all | solution.py:815
  347.6 14.1 %collective-permute-start.34 = (bf16[128,1024]{1,0:T(8,128)(2,1)}, bf16[128,1024]{1,0:T(8,128)(2,1)}, u32[]{:S(2)}, u32[]{:S(2)}) collective-permute-start(bf16[128,1024]{1,0:T(8,128)(2,1)} %get-tuple-element.154), channel_id=1, source_target_pairs={{0,1},{1,0},{2,3},{3,2},{4,5},{5,4},{6,7},{7,6},{8,9},{9,8},{10,11... | collective-permute-start | bytes 786440 | tf_op jit(solution)/shard_map/ppermute | solution.py:23
  357.2 12.3 %collective-permute-start.36 = (bf16[2,2,64,768]{3,2,1,0:T(8,128)(2,1)}, bf16[2,2,64,768]{3,2,1,0:T(8,128)(2,1)S(1)}, u32[]{:S(2)}, u32[]{:S(2)}) collective-permute-start(bf16[2,2,64,768]{3,2,1,0:T(8,128)(2,1)} %dynamic-slice_bitcast_fusion.1), channel_id=1, source_target_pairs={{0,4},{4,0},{8,12},{12,8},{16,20},{20,16},{24,28},{28,24},{1,5},{5... | collective-permute-start | bytes 1179656 | tf_op jit(solution)/shard_map/ppermute | solution.py:23
  360.2 28.1 %collective-permute-start.33 = (bf16[128,1024]{1,0:T(8,128)(2,1)}, bf16[128,1024]{1,0:T(8,128)(2,1)}, u32[]{:S(2)}, u32[]{:S(2)}) collective-permute-start(bf16[128,1024]{1,0:T(8,128)(2,1)} %get-tuple-element.153), channel_id=1, source_target_pairs={{0,1},{1,0},{2,3},{3,2},{4,5},{5,4},{6,7},{7,6},{8,9},{9,8},{10,11... | collective-permute-start | bytes 786440 | tf_op jit(solution)/shard_map/ppermute | solution.py:23
  361.6 25.5 %collective-permute-start.39 = (bf16[2,2,64,768]{3,2,1,0:T(8,128)(2,1)S(1)}, bf16[2,2,64,768]{3,2,1,0:T(8,128)(2,1)S(1)}, u32[]{:S(2)}, u32[]{:S(2)}) collective-permute-start(bf16[2,2,64,768]{3,2,1,0:T(8,128)(2,1)S(1)} %dynamic-slice_bitcast_fusion), channel_id=1, source_target_pairs={{0,16},{4,20},{8,24},{12,28},{16,0},{20,4},{24,8},{28,12},{1,17},{... | collective-permute-start | bytes 1179656 | tf_op jit(solution)/shard_map/ppermute | solution.py:23
  362.8 25.5 %collective-permute-start.35 = (bf16[128,1024]{1,0:T(8,128)(2,1)S(1)}, bf16[128,1024]{1,0:T(8,128)(2,1)S(1)}, u32[]{:S(2)}, u32[]{:S(2)}) collective-permute-start(bf16[128,1024]{1,0:T(8,128)(2,1)S(1)} %fusion.36), channel_id=1, source_target_pairs={{0,2},{1,3},{2,0},{3,1},{4,6},{5,7},{6,4},{7,5},{8,10},{9,11},{10,... | collective-permute-start | bytes 786440 | tf_op jit(solution)/shard_map/ppermute | solution.py:23
  369.8 26.4 %collective-permute-start.37 = (bf16[2,64,768]{2,1,0:T(8,128)(2,1)S(1)}, bf16[2,64,768]{2,1,0:T(8,128)(2,1)S(1)}, u32[]{:S(2)}, u32[]{:S(2)}) collective-permute-start(bf16[2,64,768]{2,1,0:T(8,128)(2,1)S(1)} %dynamic-slice_bitcast_fusion.3), channel_id=1, source_target_pairs={{0,16},{4,20},{8,24},{12,28},{16,0},{20,4},{24,8},{28,12},{1,17},{... | collective-permute-start | bytes 589832 | tf_op jit(solution)/shard_map/ppermute | solution.py:23
  (146 other events, 1407.1 us)
Sparse Core Ops, SparseCore 0:
  16.0 52.4 all-gather.4
  140.4 50.3 all-gather.6
  252.6 82.1 reduce-scatter.1

commit v3 on v2

--- a/solution.py
+++ b/solution.py
@@ -894,6 +894,963 @@
     )
 
 
+NN = ((1,), (0,))
+NT = ((1,), (1,))
+TN = ((0,), (0,))
+PART = 64
+REP, SEQ, AT, ITEM, OLDER, YOUNGER, OWNER, LEFT, RIGHT = 0, 1, 2, 3, 4, 5, 8, 16, 25
+RING = [0, 2, 4, 6, 7, 5, 3, 1]
+AHEAD = [(RING[i], RING[(i + 1) % 8]) for i in range(8)]
+BACK = [(b, a) for a, b in AHEAD]
+
+
+def meta_table(group):
+    rows = []
+    for seq in range(8):
+        p = RING.index(seq)
+        for rep in range(4):
+            row = [rep, seq, (seq % 4) * group, seq // 4, int(seq % 4 != 0), int(seq % 4 != 3), 0, 0]
+            row += [RING[(p + k) % 8] for k in (0, -1, 1, -2, 2, -3, 3, 4)]
+            row += [RING[(p - k) % 8] for k in range(9)]
+            row += [RING[(p + k) % 8] for k in range(9)]
+            rows.append(row)
+    return np.asarray(rows, np.int32)
+
+
+def call(kernel, name, args, outs, scratch=(), limit=24):
+    def space(a):
+        small = a.dtype == jnp.int32
+        return pl.BlockSpec(memory_space=pltpu.SMEM if small else pltpu.VMEM)
+
+    return pl.pallas_call(
+        kernel,
+        out_shape=outs,
+        in_specs=[space(a) for a in args],
+        out_specs=[pl.BlockSpec(memory_space=pltpu.VMEM) for _ in outs],
+        scratch_shapes=list(scratch),
+        compiler_params=pltpu.CompilerParams(vmem_limit_bytes=limit * 2**20),
+        cost_estimate=pl.CostEstimate(flops=10**6, bytes_accessed=10**5, transcendentals=0),
+        name=name,
+    )(*args)
+
+
+def shape(dims, kind):
+    return jax.ShapeDtypeStruct(tuple(dims), kind)
+
+
+def dot(left, right, dims):
+    return lax.dot_general(left, right, (dims, ((), ())), preferred_element_type=F32)
+
+
+def place(index):
+    return pl.ds(pl.multiple_of(index * LANE, LANE), LANE)
+
+
+def normed_of(rows):
+    centred = rows - jnp.mean(rows, axis=1, keepdims=True)
+    inverse = lax.rsqrt(jnp.mean(centred * centred, axis=1, keepdims=True) + EPS)
+    return centred * inverse, inverse
+
+
+def item_length(meta_ref, len_ref):
+    return jnp.where(meta_ref[ITEM] == 0, len_ref[0], len_ref[1])
+
+
+def lane_masks(meta_ref, len_ref, size):
+    lane = lax.broadcasted_iota(jnp.int32, (1, size), 1)
+    real = (meta_ref[AT] - LANE + lane < item_length(meta_ref, len_ref)).astype(F32)
+    older, younger = meta_ref[OLDER].astype(F32), meta_ref[YOUNGER].astype(F32)
+    exists = jnp.where(lane < LANE, older, jnp.where(lane >= size - LANE, younger, 1.0))
+    return real, exists
+
+
+def pack_io_kernel(in_ref, out_w_ref, out_ref):
+    width = out_w_ref.shape[2]
+    for p in range(3):
+        out_ref[:, p * width : (p + 1) * width] = in_ref[0, :, p, :]
+    out_ref[:, 3 * width :] = out_w_ref[0]
+
+
+def pack_ud_kernel(up_ref, down_ref, out_ref):
+    out_ref[0] = up_ref[0]
+    out_ref[1] = down_ref[0]
+
+
+def halves_kernel(left_ref, right_ref, a_ref, b_ref):
+    half = a_ref.shape[0]
+    a_ref[...] = left_ref[:half]
+    b_ref[...] = right_ref[half:]
+
+
+def assemble_kernel(meta_ref, p0, p1, p2, p3, p4, p5, p6, a_ref, b_ref, out_ref):
+    for k, ref in enumerate((p0, p1, p2, p3, p4, p5, p6)):
+        out_ref[meta_ref[OWNER + k]] = ref[...]
+    half = a_ref.shape[0]
+    out_ref[meta_ref[OWNER + 7], :half] = a_ref[...]
+    out_ref[meta_ref[OWNER + 7], half:] = b_ref[...]
+
+
+def norm_first_kernel(x_ref, gain_ref, shift_ref, out_ref):
+    unit, _ = normed_of(x_ref[...].astype(F32))
+    out_ref[...] = (unit * gain_ref[...] + shift_ref[...]).astype(B16)
+
+
+def own_mask(meta_ref, len_ref, rows):
+    row = lax.broadcasted_iota(jnp.int32, (rows, 1), 0)
+    return (meta_ref[AT] + meta_ref[REP] * rows + row < item_length(meta_ref, len_ref)).astype(F32)
+
+
+def top_kernel(meta_ref, len_ref, top_ref, out_ref):
+    mask = own_mask(meta_ref, len_ref, top_ref.shape[0])
+    out_ref[...] = (top_ref[...].astype(F32) * mask).astype(B16)
+
+
+def setup_kernel(
+    meta_ref, taps_ref, short_bias_ref, in_bias_ref, up_bias_ref, skip_ref, rate_ref, kern_w_ref, fb_ref, ib_ref, db_ref, sf_ref,
+    cols_ref, up_ref, chan_ref, columns_ref, small_col_ref, small_row_ref
+):
+    width = cols_ref.shape[0]
+    chan = chan_ref.shape[0]
+    rep, seq = meta_ref[REP], meta_ref[SEQ]
+    lanes = pl.ds(pl.multiple_of(rep * width, width), width)
+    rows = [taps_ref[0, j, :, lanes] for j in range(3)] + [short_bias_ref[0, :, lanes], in_bias_ref[0, :, lanes]]
+    stack = jnp.concatenate(rows + [jnp.zeros((LANE - 15, width), F32)], axis=0)
+    cols_ref[...] = stack.T[:, :16]
+    up_ref[...] = up_bias_ref[:, pl.ds(pl.multiple_of(rep * up_ref.shape[1], LANE), up_ref.shape[1])]
+    turn = width - seq * chan
+    stack = jnp.concatenate([skip_ref[:, lanes], rate_ref[:, lanes], jnp.zeros((LANE - 2, width), F32)], axis=0)
+    chan_ref[...] = pltpu.roll(stack, turn, 1)[:, :LANE].T[:chan, :2]
+    columns_ref[...] = pltpu.roll(kern_w_ref[0, :, lanes], turn, 1)[:, :chan]
+    filt = small_row_ref.shape[1]
+    small = jnp.concatenate([fb_ref[...], ib_ref[...], db_ref[...], sf_ref[...]], axis=0)
+    small_row_ref[...] = small
+    wide = jnp.concatenate([small, jnp.zeros((4, LANE - filt), F32)], axis=1)
+    wide = jnp.concatenate([wide, jnp.zeros((LANE - 4, LANE), F32)], axis=0)
+    small_col_ref[...] = wide.T[:filt, :4]
+
+
+def edges_kernel(meta_ref, x0, x1, x2, x3, last_ref, first_ref):
+    rep = meta_ref[REP]
+    refs = (x0, x1, x2, x3)
+
+    def chosen(index, lo):
+        value = refs[0][lo : lo + HALO]
+        for i in range(1, 4):
+            value = jnp.where(index == i, refs[i][lo : lo + HALO].astype(F32), value.astype(F32))
+        return value.astype(B16)
+
+    last_ref[...] = chosen(rep ^ 3, x0.shape[0] - HALO)
+    first_ref[...] = chosen(rep, 0)
+
+
+def ext_of(proj_ref, halo_ref, exists, p, rows):
+    return (
+        jnp.concatenate(
+            [halo_ref[p, rows, :LANE], proj_ref[p, rows, :], halo_ref[p, rows, LANE:]], axis=1
+        ).astype(F32)
+        * exists
+    )
+
+
+def short_from(ext, cols, p):
+    return (
+        cols[:, p : p + 1] * pltpu.roll(ext, 2, 1)
+        + cols[:, 3 + p : 4 + p] * pltpu.roll(ext, 1, 1)
+        + cols[:, 6 + p : 7 + p] * ext
+        + cols[:, 9 + p : 10 + p]
+    )
+
+
+def project_kernel(
+    meta_ref, len_ref, x0, x1, x2, x3, before_ref, after_ref, io_ref, cols_ref, proj_ref, halo_ref, gated_ref
+):
+    rep = meta_ref[REP]
+    width, group = gated_ref.shape
+    weight = io_ref[:, : 3 * width]
+    for i, x_ref in enumerate((x0, x1, x2, x3)):
+        cut = dot(x_ref[...], weight, NN).T
+        for p in range(3):
+            proj_ref[p, :, place(rep ^ i)] = (
+                cut[p * width : (p + 1) * width] + cols_ref[:, 12 + p : 13 + p]
+            ).astype(B16)
+    edge = dot(jnp.concatenate([before_ref[...], after_ref[...]], axis=0), weight, NN)
+    gap = jnp.zeros((LANE - HALO, 3 * width), F32)
+    edge = jnp.concatenate([gap, edge, gap], axis=0).T
+    for p in range(3):
+        halo_ref[p] = (edge[p * width : (p + 1) * width] + cols_ref[:, 12 + p : 13 + p]).astype(B16)
+    mask, exists = lane_masks(meta_ref, len_ref, group + 2 * LANE)
+    for lo in range(0, width, PART):
+        rows = slice(lo, lo + PART)
+        cols = cols_ref[rows, :]
+        gate_in = short_from(ext_of(proj_ref, halo_ref, exists, 1, rows), cols, 1)
+        values = short_from(ext_of(proj_ref, halo_ref, exists, 2, rows), cols, 2)
+        gated_ref[rows, :] = (values * gate_in * mask)[:, LANE:-LANE].astype(B16)
+
+
+def out_project_kernel(
+    meta_ref, len_ref, proj_ref, halo_ref, cols_ref, mixed_ref, io_ref, y_ref, give3_ref, give1_ref, keep2_ref, keep0_ref
+):
+    rep = meta_ref[REP]
+    width, group = mixed_ref.shape
+    _, exists = lane_masks(meta_ref, len_ref, group + 2 * LANE)
+    for lo in range(0, width, LANE):
+        rows = slice(lo, lo + LANE)
+        gate_out = short_from(ext_of(proj_ref, halo_ref, exists, 0, rows), cols_ref[rows, :], 0)
+        y = gate_out[:, LANE:-LANE] * mixed_ref[rows, :].astype(F32)
+        for j in range(4):
+            y_ref[rep ^ j, :, rows] = y[:, j * LANE : (j + 1) * LANE].T.astype(B16)
+    outs = (keep0_ref, give1_ref, keep2_ref, give3_ref)
+    left = y_ref[...].reshape(-1, width)
+    rows = y_ref.shape[1]
+    for lo in range(0, io_ref.shape[0], 256):
+        part = dot(left, io_ref[lo : lo + 256, 3 * width :], NT)
+        for i, ref in enumerate(outs):
+            ref[:, lo : lo + 256] = part[i * rows : (i + 1) * rows].astype(ref.dtype)
+
+
+def norm_second_kernel(x_ref, keep_ref, near_ref, far_ref, bias_ref, gain_ref, shift_ref, middle_ref, out_ref):
+    middle = x_ref[...].astype(F32) + (
+        keep_ref[...] + near_ref[...].astype(F32) + far_ref[...].astype(F32) + bias_ref[...]
+    )
+    middle_ref[...] = middle
+    unit, _ = normed_of(middle)
+    out_ref[...] = (unit * gain_ref[...] + shift_ref[...]).astype(B16)
+
+
+def mlp_kernel(x0, x1, x2, x3, g0, g1, g2, g3, ud_ref, bias_ref, act_ref, gpre_ref, sum_ref):
+    step = 256
+    rows, model = x0.shape
+    pieces = ((x0, g0), (x1, g1), (x2, g2), (x3, g3))
+    for lo in range(0, act_ref.shape[1], step):
+        cut = slice(lo, lo + step)
+        up = ud_ref[:, 0, :, cut].reshape(model, step)
+        down = ud_ref[:, 1, :, cut].reshape(model, step)
+        total = None
+        for i, (x_ref, g_ref) in enumerate(pieces):
+            at = slice(i * rows, (i + 1) * rows)
+            pre = dot(x_ref[...], up, NN) + bias_ref[:, cut]
+            gact = dot(g_ref[...], down, NN)
+            phi = 0.5 * (1.0 + lax.erf(pre * math.sqrt(0.5)))
+            slope = phi + pre * (jnp.exp(-0.5 * pre * pre) * (1.0 / math.sqrt(2.0 * math.pi)))
+            act_ref[at, cut] = (pre * phi).astype(B16)
+            gpre = (gact * slope).astype(B16)
+            gpre_ref[at, cut] = gpre
+            part = jnp.sum(gpre.astype(F32), axis=0, keepdims=True)
+            total = part if total is None else total + part
+        sum_ref[:, cut] = total
+
+
+def rows_kernel(which, left_ref, ud_ref, give3_ref, give1_ref, keep2_ref, keep0_ref):
+    rows, model = give3_ref.shape
+    owned = ud_ref.shape[2]
+    outs = (keep0_ref, give1_ref, keep2_ref, give3_ref)
+    for k in range(0, ud_ref.shape[0], 2):
+        weight = ud_ref[k : k + 2, which].reshape(2 * owned, -1)
+        part = dot(left_ref[...], weight, NT)
+        for i, ref in enumerate(outs):
+            ref[:, k * owned : (k + 2) * owned] = part[i * rows : (i + 1) * rows].astype(ref.dtype)
+
+
+def mlp_grad_kernel(meta_ref, x0, x1, x2, x3, g0, g1, g2, g3, act_ref, gpre_ref, out_ref, left_ref, right_ref):
+    owners, _, owned, wide = out_ref.shape
+    for which, refs, right in ((0, (x0, x1, x2, x3), gpre_ref), (1, (g0, g1, g2, g3), act_ref)):
+        for k in range(0, owners, 2):
+            left = jnp.concatenate([r[:, k * owned : (k + 2) * owned] for r in refs], axis=0)
+            part = dot(left, right[...], TN).astype(B16)
+            out_ref[k, which] = part[:owned]
+            out_ref[k + 1, which] = part[owned:]
+    left_ref[...] = out_ref[meta_ref[LEFT + 1], 0]
+    right_ref[...] = out_ref[meta_ref[RIGHT + 1], 1]
+
+
+def ring_add_kernel(step, meta_ref, term_ref, left_in, right_in, left_ref, right_ref):
+    mine = term_ref[meta_ref[LEFT + step], 0].astype(F32)
+    left_ref[...] = (left_in[...].astype(F32) + mine).astype(left_ref.dtype)
+    mine = term_ref[meta_ref[RIGHT + step], 1].astype(F32)
+    right_ref[...] = (right_in[...].astype(F32) + mine).astype(right_ref.dtype)
+
+
+def norm_second_back_kernel(
+    meta_ref, len_ref, keep_ref, near_ref, far_ref, middle_ref, top_ref, gain_ref, out_ref, gx_ref, sum_ref
+):
+    grad = keep_ref[...] + near_ref[...].astype(F32) + far_ref[...].astype(F32)
+    unit, inverse = normed_of(middle_ref[...])
+    scaled = grad * gain_ref[...]
+    one = jnp.mean(scaled, axis=1, keepdims=True)
+    two = jnp.mean(scaled * unit, axis=1, keepdims=True)
+    top = top_ref[...].astype(F32) * own_mask(meta_ref, len_ref, top_ref.shape[0])
+    out = top + inverse * (scaled - one - unit * two)
+    out_ref[...] = out
+    gx = out.astype(B16)
+    gx_ref[...] = gx
+    rows = [grad * unit, grad, gx.astype(F32), top]
+    sums = [jnp.sum(r, axis=0, keepdims=True) for r in rows]
+    sum_ref[...] = jnp.concatenate(sums + [jnp.zeros((4, sums[0].shape[1]), F32)], axis=0)
+
+
+def grad_gate_kernel(
+    meta_ref, len_ref, x0, x1, x2, x3, io_ref, proj_ref, halo_ref, cols_ref, mixed_ref, gy_ref, gmix_ref, first_ref
+):
+    rep = meta_ref[REP]
+    width, group = mixed_ref.shape
+    _, exists = lane_masks(meta_ref, len_ref, group + 2 * LANE)
+    weight = io_ref[:, 3 * width :]
+    for i, x_ref in enumerate((x0, x1, x2, x3)):
+        gy_ref[:, place(rep ^ i)] = dot(x_ref[...], weight, NN).T.astype(B16)
+    for lo in range(0, width, PART):
+        rows = slice(lo, lo + PART)
+        gate_out = short_from(ext_of(proj_ref, halo_ref, exists, 0, rows), cols_ref[rows, :], 0)
+        gy = gy_ref[rows, :].astype(F32)
+        gmix_ref[rows, :] = (gy * gate_out[:, LANE:-LANE]).astype(B16)
+        first_ref[rows, :] = gy[:, :LANE] * mixed_ref[rows, :LANE].astype(F32)
+
+
+def conv_back_kernel(
+    g_ref, spec_ref, kern_ref, twist_ref, hi_ref, lo_ref, chan_ref, out_ref, grad_kern_ref, z_ref, p_ref
+):
+    blocks, rows, length = twist_ref.shape[0], g_ref.shape[1], g_ref.shape[2]
+    short_blocks = blocks // 4
+    span = blocks * rows
+    first = [g_ref[b].astype(F32) for b in range(blocks)]
+    second = [g_ref[blocks + b].astype(F32) for b in range(short_blocks)]
+    turn_rows(first, twist_ref, z_ref, 0, blocks)
+    turn_rows(second, twist_ref, z_ref, span, blocks)
+    grad = dot_split(z_ref[...], hi_ref[...], lo_ref[...], ((1,), (0,)))
+    kern = kern_ref[...]
+    p_ref[0:span] = times(grad[:span], kern, True)
+    p_ref[span : 2 * span] = times(grad[span:], kern, True)
+    p_ref[2 * span :] = times(grad[:span], spec_ref[0:span], True) + times(grad[span:], spec_ref[span:], True)
+    w = dot_split(p_ref[...], hi_ref[...], lo_ref[...], ((1,), (1,)))
+    skip = chan_ref[:, 0:1]
+    zero = jnp.zeros((rows, LANE), B16)
+    for b in range(blocks):
+        acc = (back_rows(w, 0, rows, b, twist_ref, blocks) + skip * first[b]).astype(B16)
+        out_ref[b, :, :length] = acc
+        if b:
+            out_ref[b - 1, :, length:] = acc[:, :LANE]
+        if b < short_blocks:
+            acc = (back_rows(w, span, rows, b, twist_ref, blocks) + skip * second[b]).astype(B16)
+        else:
+            acc = jnp.zeros((rows, length), B16)
+        out_ref[blocks + b, :, :length] = acc
+        if b:
+            out_ref[blocks + b - 1, :, length:] = acc[:, :LANE]
+        grad_kern_ref[b] = back_rows(w, 2 * span, rows, b, twist_ref, blocks)
+    out_ref[blocks - 1, :, length:] = zero
+    out_ref[2 * blocks - 1, :, length:] = zero
+
+
+def conv_ahead_kernel(x_ref, kern_ref, twist_ref, hi_ref, lo_ref, chan_ref, out_ref, spec_ref, z_ref):
+    conv_forward_kernel(
+        twist_ref.shape[0] // 4, x_ref, kern_ref, twist_ref, hi_ref, lo_ref, chan_ref.at[:, 0:1], out_ref, spec_ref, z_ref
+    )
+
+
+def filter_ahead_kernel(
+    grid_ref, ramp_ref, chan_ref, w1_ref, w2_ref, w3_ref, small_ref, columns_ref, twist_ref, hi_ref, lo_ref,
+    spec_ref, sin_ref, cos_ref, z_ref
+):
+    filter_forward_kernel(
+        grid_ref, ramp_ref, chan_ref.at[:, 1:2], w1_ref.at[0], w2_ref.at[0], w3_ref.at[0], small_ref, columns_ref,
+        twist_ref, hi_ref, lo_ref, spec_ref, sin_ref, cos_ref, z_ref
+    )
+
+
+def filter_back_kernel(
+    meta_ref, gk_ref, grid_ref, ramp_ref, chan_ref, w1_ref, w2_ref, w3_ref, col_ref, row_ref, columns_ref, sin_ref, cos_ref,
+    side_ref, wide_ref
+):
+    freq, freq_row = col_ref[:, 3:4], row_ref[3:4, :]
+    filt = freq.shape[0]
+    gk = jnp.concatenate([gk_ref[b] for b in range(gk_ref.shape[0])], axis=1)
+    gk = gk * jnp.exp(-chan_ref[:, 1:2] * ramp_ref[...])
+    gcols = dot_high(sin_ref[2], gk, NT)
+    chan, width = gcols.shape[1], wide_ref.shape[1]
+    row = lax.broadcasted_iota(jnp.int32, (chan, width), 0)
+    lane = lax.broadcasted_iota(jnp.int32, (chan, width), 1)
+    pick = (lane == row + meta_ref[SEQ] * chan).astype(F32)
+    wide_ref[...] = dot_high(gcols, pick, NN)
+    grad = dot_high(columns_ref[...], gk, NN)
+    ones = jnp.ones((8, gk.shape[1]), F32)
+    gfreq = jnp.zeros((1, filt), F32)
+    grads, biases = [None] * 3, [None] * 3
+    for i, w_ref in ((2, w3_ref), (1, w2_ref), (0, w1_ref)):
+        turn = grad * cos_ref[i]
+        below = sin_ref[i - 1] if i else grid_ref[...]
+        raw = dot_high(below, turn, NT)
+        total = dot_high(ones, turn, NT)[0:1]
+        grads[i] = raw * freq_row
+        biases[i] = total * freq_row
+        gfreq = gfreq + jnp.sum(raw * w_ref[0], axis=0, keepdims=True) + total * row_ref[i : i + 1, :]
+        if i:
+            grad = dot_high(w_ref[0], turn * freq, NN)
+    gap = jnp.zeros((filt - grads[0].shape[0], filt), F32)
+    small = jnp.concatenate(biases + [gfreq, jnp.zeros((filt - 4, filt), F32)], axis=0)
+    side_ref[...] = jnp.concatenate(
+        [grads[1], grads[2], jnp.concatenate([grads[0], gap], axis=0), small], axis=1
+    )
+
+
+def grad_short_kernel(
+    meta_ref, len_ref, proj_ref, halo_ref, cols_ref, mixed_ref, gy_ref, ggated_ref, onext_ref, io_ref,
+    x0, x1, x2, x3, gain_ref, shift_ref,
+    tok_ref, sum_ref, norm_ref, give3_ref, give1_ref, keep2_ref, keep0_ref
+):
+    rep = meta_ref[REP]
+    width, group = mixed_ref.shape
+    size = group + 2 * LANE
+    mask, exists = lane_masks(meta_ref, len_ref, size)
+    mid = slice(LANE, size - LANE)
+    next_on = exists[:, size - LANE :]
+    ones = jnp.ones((LANE, group), F32)
+    del ones
+    columns = []
+    for lo in range(0, width, PART):
+        rows = slice(lo, lo + PART)
+        cols = cols_ref[rows, :]
+        gy = gy_ref[rows, :].astype(F32)
+        zero = jnp.zeros((PART, LANE), F32)
+        ext = [ext_of(proj_ref, halo_ref, exists, p, rows) for p in range(3)]
+        short = [short_from(ext[p], cols, p) for p in range(3)]
+        ggated = jnp.concatenate([zero, ggated_ref[rows, :].astype(F32)], axis=1) * (mask * exists)
+        gout = gy * mixed_ref[rows, :].astype(F32)
+        gshort = [
+            jnp.concatenate([zero, gout, onext_ref[rows, :] * next_on], axis=1),
+            ggated * short[2],
+            ggated * short[1],
+        ]
+        gated = short[2][:, mid] * short[1][:, mid] * mask[:, mid]
+
+        def summed(value):
+            parts = [value[:, k : k + LANE] for k in range(0, group, LANE)]
+            total = parts[0]
+            for part in parts[1:]:
+                total = total + part
+            return jnp.sum(total, axis=1, keepdims=True)
+
+        sums = [summed(gy * short[0][:, mid] * gated)]
+        for p in range(3):
+            mine = gshort[p][:, mid]
+            sums.append(summed(mine))
+            sums.append(summed(mine * ext[p][:, mid]))
+            sums.append(summed(mine * pltpu.roll(ext[p], 1, 1)[:, mid]))
+            sums.append(summed(mine * pltpu.roll(ext[p], 2, 1)[:, mid]))
+            gproj = (
+                cols[:, 6 + p : 7 + p] * gshort[p]
+                + cols[:, 3 + p : 4 + p] * pltpu.roll(gshort[p], size - 1, 1)
+                + cols[:, p : p + 1] * pltpu.roll(gshort[p], size - 2, 1)
+            )[:, mid].astype(B16).astype(F32)
+            sums.append(summed(gproj))
+            at = slice(p * width + lo, p * width + lo + PART)
+            for j in range(4):
+                tok_ref[rep ^ j, :, at] = gproj[:, j * LANE : (j + 1) * LANE].T.astype(B16)
+        columns.append(jnp.concatenate(sums + [jnp.zeros((PART, LANE - 16), F32)], axis=1))
+    sum_ref[...] = jnp.concatenate(columns, axis=0).T[:16]
+    outs = (keep0_ref, give1_ref, keep2_ref, give3_ref)
+    left = tok_ref[...].reshape(-1, 3 * width)
+    tall = tok_ref.shape[1]
+    for lo in range(0, io_ref.shape[0], 256):
+        cut = slice(lo, lo + 256)
+        part = dot(left, io_ref[cut, : 3 * width], NT)
+        plain = jnp.sum(part, axis=0, keepdims=True)
+        cross = None
+        for i, (ref, x_ref) in enumerate(zip(outs, (x0, x1, x2, x3))):
+            mine = part[i * tall : (i + 1) * tall]
+            ref[:, cut] = mine.astype(ref.dtype)
+            two = jnp.sum(mine * x_ref[:, cut].astype(F32), axis=0, keepdims=True)
+            cross = two if cross is None else cross + two
+        norm_ref[0:1, cut] = (cross - shift_ref[:, cut] * plain) / gain_ref[:, cut]
+        norm_ref[1:2, cut] = plain
+
+
+def give_first(meta_ref, term_ref, a_ref, b_ref):
+    half = a_ref.shape[2]
+    seq = meta_ref[SEQ]
+    s0, s1 = seq & 1, (seq >> 1) & 1
+    for i in range(2):
+        for j in range(2):
+            a_ref[i, j] = term_ref[i, j, 1 - s0, :half]
+            b_ref[i, j] = term_ref[i, 1 - s1, j, half:]
+
+
+def weight_grad_kernel(meta_ref, x0, x1, x2, x3, right_ref, out_ref, a_ref, b_ref):
+    owned, wide = out_ref.shape[3], out_ref.shape[4]
+    right = right_ref[...].reshape(-1, wide)
+    for k in range(0, 8, 2):
+        left = jnp.concatenate([r[:, k * owned : (k + 2) * owned] for r in (x0, x1, x2, x3)], axis=0)
+        part = dot(left, right, TN).astype(B16)
+        out_ref[k // 4, (k // 2) % 2, 0] = part[:owned]
+        out_ref[k // 4, (k // 2) % 2, 1] = part[owned:]
+    give_first(meta_ref, out_ref, a_ref, b_ref)
+
+
+def halve_one_kernel(meta_ref, term_ref, a_in, b_in, keep_a, keep_b, give_a, give_b):
+    half = a_in.shape[2]
+    seq = meta_ref[SEQ]
+    s0, s1 = seq & 1, (seq >> 1) & 1
+    for i in range(2):
+        keep_a[i] = term_ref[i, s1, s0, :half].astype(F32) + a_in[i, s1].astype(F32)
+        give_a[i] = (term_ref[i, 1 - s1, s0, :half].astype(F32) + a_in[i, 1 - s1].astype(F32)).astype(B16)
+        keep_b[i] = term_ref[i, s1, s0, half:].astype(F32) + b_in[i, s0].astype(F32)
+        give_b[i] = (term_ref[i, s1, 1 - s0, half:].astype(F32) + b_in[i, 1 - s0].astype(F32)).astype(B16)
+
+
+def halve_two_kernel(meta_ref, keep_a_in, keep_b_in, a_in, b_in, keep_a, keep_b, give_a, give_b):
+    s2 = meta_ref[SEQ] >> 2
+    keep_a[...] = keep_a_in[s2] + a_in[s2].astype(F32)
+    give_a[...] = (keep_a_in[1 - s2] + a_in[1 - s2].astype(F32)).astype(B16)
+    keep_b[...] = keep_b_in[s2] + b_in[s2].astype(F32)
+    give_b[...] = (keep_b_in[1 - s2] + b_in[1 - s2].astype(F32)).astype(B16)
+
+
+def halve_last_kernel(keep_a, keep_b, a_in, b_in, out_ref):
+    half = keep_a.shape[0]
+    if len(out_ref.shape) == 3:
+        out_ref[0, :half] = keep_a[...] + a_in[...].astype(F32)
+        out_ref[0, half:] = keep_b[...] + b_in[...].astype(F32)
+        return
+    width = out_ref.shape[3]
+    for p in range(3):
+        cut = slice(p * width, (p + 1) * width)
+        out_ref[0, :half, p, :] = keep_a[:, cut] + a_in[:, cut].astype(F32)
+        out_ref[0, half:, p, :] = keep_b[:, cut] + b_in[:, cut].astype(F32)
+
+
+def norm_first_back_kernel(keep_ref, near_ref, far_ref, x_ref, middle_ref, gain_ref, out_ref):
+    grad = keep_ref[...] + near_ref[...].astype(F32) + far_ref[...].astype(F32)
+    unit, inverse = normed_of(x_ref[...].astype(F32))
+    scaled = grad * gain_ref[...]
+    one = jnp.mean(scaled, axis=1, keepdims=True)
+    two = jnp.mean(scaled * unit, axis=1, keepdims=True)
+    out_ref[...] = middle_ref[...] + inverse * (scaled - one - unit * two)
+
+
+def layer_out_kernel(keep_ref, near_ref, far_ref, middle_ref, bias_ref, out_ref):
+    part = keep_ref[...] + near_ref[...].astype(F32) + far_ref[...].astype(F32)
+    out_ref[...] = (middle_ref[...] + (part + bias_ref[...])).astype(B16)
+
+
+def add_far_kernel(keep_ref, came_ref, out_ref):
+    out_ref[...] = (keep_ref[...] + came_ref[...].astype(F32)).astype(B16)
+
+
+HALF = 88
+
+
+def pack_small_kernel(side_ref, wide_ref, col_ref, up_ref, one_ref, two_ref, out_ref):
+    filt, width = side_ref.shape
+    out_ref[:filt] = side_ref[...]
+    at = filt
+    for ref, count in ((one_ref, 2), (two_ref, 4)):
+        for r in range(count):
+            for k in range(4):
+                out_ref[at : at + 1] = ref[r : r + 1, k * width : (k + 1) * width]
+                at += 1
+    out_ref[HALF : HALF + 16] = col_ref[...]
+    for k in range(4):
+        out_ref[HALF + 16 + k : HALF + 17 + k] = up_ref[:, k * width : (k + 1) * width]
+    out_ref[HALF + 20 : HALF + 24] = jnp.zeros((4, width), F32)
+    out_ref[HALF + 24 :] = wide_ref[...]
+
+
+def add_small_kernel(mine_ref, came_ref, out_ref):
+    out_ref[...] = mine_ref[...] + came_ref[...]
+
+
+def list_small_kernel(meta_ref, mine_ref, came_ref, out_ref):
+    y = meta_ref[REP] >> 1
+    out_ref[:HALF] = mine_ref[:HALF] + came_ref[:HALF]
+    out_ref[pl.ds(pl.multiple_of((1 + y) * HALF, 8), HALF)] = mine_ref[HALF:]
+    out_ref[pl.ds(pl.multiple_of((2 - y) * HALF, 8), HALF)] = came_ref[HALF:]
+
+
+def unpack_small_kernel(
+    meta_ref, mine_ref, came_ref,
+    in_bias, taps, short_bias, fw, fb, iw, ib, dw, db, sf, kern_w, skip, out_b, n1g, n1s, n2g, n2s, up_b, down_b
+):
+    core = meta_ref[REP] & 1
+    filt, width = fw.shape[2], mine_ref.shape[1]
+    total = mine_ref[:HALF] + came_ref[:HALF]
+    iw[0] = total[:filt, :filt]
+    dw[0] = total[:filt, filt : 2 * filt]
+    fw[0] = total[: fw.shape[1], 2 * filt : 3 * filt]
+    for k, ref in enumerate((fb, ib, db, sf)):
+        ref[...] = total[k : k + 1, 3 * filt :]
+    at = filt
+    for ref in (n1g, n1s, n2g, n2s, out_b, down_b):
+        for k in range(4):
+            ref[:, k * width : (k + 1) * width] = total[at : at + 1]
+            at += 1
+    for y in range(2):
+        lo = (1 + y) * HALF
+        mine, came = mine_ref[lo : lo + HALF], came_ref[lo : lo + HALF]
+        for c in range(2):
+            block = jnp.where(core == c, mine, came)
+            lanes = slice((2 * y + c) * width, (2 * y + c + 1) * width)
+            skip[:, lanes] = block[0:1]
+            for p in range(3):
+                row = 1 + 5 * p
+                short_bias[0, p : p + 1, lanes] = block[row : row + 1]
+                for j in range(3):
+                    taps[0, j, p : p + 1, lanes] = block[row + 3 - j : row + 4 - j]
+                in_bias[0, p : p + 1, lanes] = block[row + 4 : row + 5]
+            for k in range(4):
+                lo_up = (2 * y + c) * 4 * width + k * width
+                up_b[:, lo_up : lo_up + width] = block[16 + k : 17 + k]
+            kern_w[0, :, lanes] = block[24 : 24 + filt]
+
+
+def tie(values, *others):
+    return lax.optimization_barrier((values, others))[0]
+
+
+class RingGather:
+    def __init__(self, name, meta, shard):
+        self.name, self.meta = name, meta
+        self.pieces = [shard]
+        self.send(shard, shard)
+
+    def send(self, left, right):
+        self.came = (lax.ppermute(left, "seq", AHEAD), lax.ppermute(right, "seq", BACK))
+
+    def step(self, *others):
+        left, right = tie(self.came, *others)
+        self.pieces += [left, right]
+        count = len(self.pieces)
+        if count == 7:
+            half = shape((left.shape[0] // 2,) + left.shape[1:], B16)
+            left, right = call(halves_kernel, self.name + "_halves", [left, right], [half, half])
+        if count < 9:
+            self.send(left, right)
+        return self.came
+
+    def full(self, *others):
+        left, right = tie(self.came, *others)
+        pieces = self.pieces + [left, right]
+        return call(
+            assemble_kernel,
+            self.name + "_assemble",
+            [self.meta, *pieces],
+            [shape((8,) + self.pieces[0].shape, B16)],
+        )[0]
+
+
+def gather_four(rows):
+    far = swap(rows, "rep", 2)
+    near = swap(rows, "rep", 1)
+    diag = swap(far, "rep", 1)
+    return [rows, near, far, diag]
+
+
+def pass_far(give3, give1, keep2):
+    came = swap(give3, "rep", 1)
+    near = swap(give1, "rep", 1)
+    (summed,) = call(add_far_kernel, "add_far", [keep2, came], [shape(keep2.shape, B16)])
+    return near, swap(summed, "rep", 2), summed
+
+
+class Halving:
+    def __init__(self, name, meta, term, give, out_dims):
+        self.name, self.meta, self.term, self.out_dims = name, meta, term, out_dims
+        self.stage = 0
+        self.came = (swap(give[0], "seq", 1), swap(give[1], "seq", 2))
+
+    def step(self, *others):
+        came = tie(self.came, *others)
+        self.stage += 1
+        rows, cols = self.term.shape[3] // 2, self.term.shape[4]
+        if self.stage == 1:
+            lead = (2, rows, cols)
+            ka, kb, ga, gb = call(
+                halve_one_kernel, self.name + "_one", [self.meta, self.term, *came],
+                [shape(lead, F32)] * 2 + [shape(lead, B16)] * 2,
+            )
+            self.came = (swap(ga, "seq", 2), swap(gb, "seq", 1))
+        elif self.stage == 2:
+            lead = (rows, cols)
+            ka, kb, ga, gb = call(
+                halve_two_kernel, self.name + "_two", [self.meta, *self.keep, *came],
+                [shape(lead, F32)] * 2 + [shape(lead, B16)] * 2,
+            )
+            self.came = (swap(ga, "seq", 4), swap(gb, "seq", 4))
+        else:
+            return call(halve_last_kernel, self.name + "_last", [*self.keep, *came], [shape(self.out_dims, F32)])[0]
+        self.keep = (ka, kb)
+        return self.keep
+
+
+def per_device_fast(
+    tokens,
+    cotangent,
+    lengths,
+    in_weight,
+    in_bias,
+    short_taps,
+    short_bias,
+    feat_weight,
+    feat_bias,
+    inner_weight,
+    inner_bias,
+    deep_weight,
+    deep_bias,
+    sine_freq,
+    kernel_weight,
+    skip_gain,
+    out_weight,
+    out_bias,
+    norm1_gain,
+    norm1_shift,
+    norm2_gain,
+    norm2_shift,
+    up_weight,
+    up_bias,
+    down_weight,
+    down_bias,
+):
+    tok_rows, model = tokens.shape
+    group = tok_rows * 4
+    blocks = 4
+    seq_len = blocks * group
+    chan = model // 32
+    width = model // 4
+    hidden = up_weight.shape[2]
+    owned = model // 8
+    filt = feat_weight.shape[2]
+    device = lax.axis_index("seq") * 4 + lax.axis_index("rep")
+    meta = lax.dynamic_index_in_dim(jnp.asarray(meta_table(group)), device, 0, keepdims=False)
+    row_f32, row_b16 = shape((tok_rows, model), F32), shape((tok_rows, model), B16)
+    sums_shapes = [row_b16, row_b16, row_f32, row_f32]
+    flat_shape = shape((width, group), B16)
+
+    (io_shard,) = call(pack_io_kernel, "pack_io", [in_weight, out_weight], [shape((owned, 4 * width), B16)])
+    io_ring = RingGather("io", meta, io_shard)
+    (normed,) = call(norm_first_kernel, "norm_first", [tokens, norm1_gain, norm1_shift], [row_b16])
+    x_one = gather_four(normed)
+    twist, table = transform_tables(blocks, group)
+    hi, lo = split_table(table)
+    grid, ramp = feature_table(seq_len, feat_weight.shape[1])
+    twist, grid, ramp = jnp.asarray(twist), jnp.asarray(grid), jnp.asarray(ramp)
+    rates = jnp.asarray(decay_rates(model).T)
+    cols, up_block, chans, columns, small_col, small_row = call(
+        setup_kernel,
+        "setup",
+        [
+            meta, short_taps, short_bias, in_bias, up_bias, skip_gain, rates, kernel_weight,
+            feat_bias, inner_bias, deep_bias, sine_freq,
+        ],
+        [
+            shape((width, 16), F32), shape((1, hidden), F32), shape((chan, 2), F32), shape((filt, chan), F32),
+            shape((filt, 4), F32), shape((4, filt), F32),
+        ],
+    )
+    (ud_shard,) = call(pack_ud_kernel, "pack_ud", [up_weight, down_weight], [shape((2, owned, hidden), B16)])
+    (top_rows,) = call(top_kernel, "top", [meta, lengths, cotangent], [row_b16])
+    io_ring.step(cols, ud_shard, top_rows)
+    nets = (feat_weight, inner_weight, deep_weight)
+    kern_spec, sines, cosines = call(
+        filter_ahead_kernel,
+        "filter_ahead",
+        [grid, ramp, chans, *nets, tie(small_col, io_ring.pieces[-1]), columns, twist, hi, lo],
+        [
+            shape((blocks * chan, 2 * group), F32),
+            shape((3, filt, seq_len), F32),
+            shape((3, filt, seq_len), F32),
+        ],
+        scratch=[pltpu.VMEM((blocks * chan, 2 * group), F32)],
+    )
+    io_ring.step(kern_spec)
+
+    edge = shape((HALO, model), B16)
+    last, first = call(edges_kernel, "edges", [meta, *x_one], [edge, edge])
+    before = lax.ppermute(last, "seq", [(i, (i + 1) % 8) for i in range(8)])
+    after = lax.ppermute(first, "seq", [(i, (i + 7) % 8) for i in range(8)])
+    io_ring.step()
+    full_io = io_ring.full().reshape(model, 4 * width)
+    ud_ring = RingGather("ud", meta, tie(ud_shard, full_io))
+    g_top = gather_four(tie(top_rows, x_one[3]))
+    proj, halo, gated = call(
+        project_kernel,
+        "project",
+        [meta, lengths, *x_one, before, after, full_io, cols],
+        [shape((3, width, group), B16), shape((3, width, 2 * LANE), B16), flat_shape],
+    )
+    common = [proj, halo, cols]
+
+    received = lax.all_to_all(gated.reshape(8, chan, group), "seq", 0, 0, tiled=True)
+    ud_ring.step(received)
+    spec_rows = 2 * blocks * chan
+    mixed_chan, kept_spec = call(
+        conv_ahead_kernel,
+        "conv_ahead",
+        [received, kern_spec, twist, hi, lo, chans],
+        [shape(received.shape, B16), shape((spec_rows, 2 * group), F32)],
+        scratch=[pltpu.VMEM((spec_rows, 2 * group), F32)],
+    )
+    mixed = lax.all_to_all(mixed_chan, "seq", 0, 0, tiled=True).reshape(width, group)
+    ud_ring.step(mixed)
+
+    y_tok, give3, give1, keep2, keep0 = call(
+        out_project_kernel,
+        "out_project",
+        [meta, lengths, *common, mixed, full_io],
+        [shape((4, tok_rows, width), B16)] + sums_shapes,
+    )
+    near, far, _ = pass_far(give3, give1, keep2)
+    middle, normed_two = call(
+        norm_second_kernel,
+        "norm_second",
+        [tokens, keep0, near, far, out_bias, norm2_gain, norm2_shift],
+        [row_f32, row_b16],
+    )
+    ud_ring.step(normed_two)
+    x_two = gather_four(normed_two)
+    full_ud = ud_ring.full(x_two[2])
+
+    tall = shape((group, hidden), B16)
+    act, gpre, gup = call(
+        mlp_kernel, "mlp", [*x_two, *g_top, full_ud, up_block], [tall, tall, shape((1, hidden), F32)]
+    )
+    give3, give1, keep2, keep0 = call(partial(rows_kernel, 0), "grad_two", [gpre, full_ud], sums_shapes)
+    near, far, passed = pass_far(give3, give1, keep2)
+    one_way = shape((owned, hidden), B16)
+    mlp_terms, left, right = call(
+        mlp_grad_kernel,
+        "mlp_grad",
+        [meta, *x_two, *g_top, act, tie(gpre, passed)],
+        [shape((8, 2, owned, hidden), B16), one_way, one_way],
+    )
+
+    def ring_send(left, right):
+        return lax.ppermute(left, "seq", AHEAD), lax.ppermute(right, "seq", BACK)
+
+    def ring_add(step, came, *others):
+        left, right = tie(came, *others)
+        out = shape((owned, hidden), F32 if step == 8 else B16)
+        return call(
+            partial(ring_add_kernel, step), "ring_add_%d" % step, [meta, mlp_terms, left, right], [out, out]
+        )
+
+    ring = ring_send(left, right)
+    grad_middle, gx, norm_sums = call(
+        norm_second_back_kernel,
+        "norm_second_back",
+        [meta, lengths, keep0, near, tie(far, left), middle, cotangent, norm2_gain],
+        [row_f32, row_b16, shape((8, model), F32)],
+    )
+    g_mid = gather_four(gx)
+    m3, m1, m2, m0 = call(partial(rows_kernel, 1), "mlp_rows", [tie(act, gx), full_ud], sums_shapes)
+    ring = ring_send(*ring_add(2, ring, g_mid[2], m3))
+    gy, gmix, gate_first = call(
+        grad_gate_kernel,
+        "grad_gate",
+        [meta, lengths, *tie(tuple(g_mid), m3), full_io, *common, mixed],
+        [flat_shape, flat_shape, shape((width, LANE), F32)],
+    )
+
+    grads_chan = lax.all_to_all(gmix.reshape(8, chan, group), "seq", 0, 0, tiled=True)
+    gate_next = lax.ppermute(gate_first, "seq", [(i, (i + 7) % 8) for i in range(8)])
+    m_near, m_far, _ = pass_far(tie(m3, gmix), m1, m2)
+    ring = ring_send(*ring_add(3, ring, grads_chan))
+    ggated_chan, grad_kernel = call(
+        conv_back_kernel,
+        "conv_back",
+        [grads_chan, kept_spec, kern_spec, twist, hi, lo, chans],
+        [shape((8, chan, group + LANE), B16), shape((blocks, chan, group), F32)],
+        scratch=[pltpu.VMEM((spec_rows, 2 * group), F32), pltpu.VMEM((3 * spec_rows // 2, 2 * group), F32)],
+    )
+    out_cube = (2, 2, 2, owned, width)
+    give = shape((2, 2, owned // 2, width), B16)
+    out_terms, ga, gb = call(
+        weight_grad_kernel,
+        "grad_out",
+        [meta, *tie(tuple(g_mid), grads_chan), y_tok],
+        [shape(out_cube, B16), give, give],
+    )
+    ring = ring_send(*ring_add(4, ring, ggated_chan))
+    ggated = lax.all_to_all(ggated_chan, "seq", 0, 0, tiled=True).reshape(width, group + LANE)
+    out_back = Halving("grad_out", meta, out_terms, (ga, gb), (1, owned, width))
+    ring = ring_send(*ring_add(5, ring, ggated))
+    gproj_tok, col_sums, norm_one, give3, give1, keep2, keep0 = call(
+        grad_short_kernel,
+        "grad_short",
+        [meta, lengths, *common, mixed, gy, ggated, gate_next, full_io, *x_one, norm1_gain, norm1_shift],
+        [shape((4, tok_rows, 3 * width), B16), shape((16, width), F32), shape((2, model), F32)] + sums_shapes,
+    )
+    near, far, passed = pass_far(give3, give1, keep2)
+    give = shape((2, 2, owned // 2, 3 * width), B16)
+    in_terms, ga, gb = call(
+        weight_grad_kernel,
+        "grad_in",
+        [meta, *x_one, gproj_tok],
+        [shape((2, 2, 2, owned, 3 * width), B16), give, give],
+    )
+    in_back = Halving("grad_in", meta, in_terms, (ga, gb), (1, owned, 3, width))
+    side, wide = call(
+        filter_back_kernel,
+        "filter_back",
+        [
+            meta, tie(grad_kernel, ga), grid, ramp, chans, *nets, small_col, small_row, columns, sines, cosines
+        ],
+        [shape((filt, 4 * filt), F32), shape((filt, width), F32)],
+    )
+
+    (small,) = call(
+        pack_small_kernel,
+        "pack_small",
+        [side, wide, col_sums, gup, norm_one, norm_sums],
+        [shape((2 * HALF, width), F32)],
+    )
+    came = swap(small, "seq", 1)
+    (grad_tokens,) = call(
+        norm_first_back_kernel, "norm_first_back", [keep0, near, tie(far, small), tokens, grad_middle, norm1_gain], [row_f32]
+    )
+    (layer_out,) = call(layer_out_kernel, "layer_out", [m0, m_near, tie(m_far, small), middle, down_bias], [row_b16])
+    ring = ring_send(*ring_add(6, ring, small))
+    out_back.step(small)
+    (small,) = call(add_small_kernel, "add_small", [small, came], [small])
+    came = swap(small, "seq", 2)
+    in_back.step(small)
+    ring = ring_send(*ring_add(7, ring, small))
+    (small,) = call(add_small_kernel, "add_small", [small, came], [small])
+    came = swap(small, "seq", 4)
+    out_back.step(small)
+    (small,) = call(add_small_kernel, "add_small", [small, came], [small])
+    came = swap(small, "rep", 2)
+    in_back.step(small)
+    grad_up, grad_down = ring_add(8, ring, small)
+    (small,) = call(
+        list_small_kernel, "list_small", [meta, small, came], [shape((3 * HALF, width), F32)]
+    )
+    came = swap(small, "rep", 1)
+    grad_out = out_back.step(small)
+    grad_in = in_back.step(small)
+    vector = shape((1, model), F32)
+    square, short = shape((1, filt, filt), F32), shape((1, filt), F32)
+    triple = shape((1, 3, model), F32)
+    outs = call(
+        unpack_small_kernel,
+        "unpack_small",
+        [meta, small, came],
+        [
+            triple, shape((1, 3, 3, model), F32), triple, shape(feat_weight.shape, F32), short, square, short, square,
+            short, short, shape(kernel_weight.shape, F32), vector, vector, vector, vector, vector, vector,
+            shape(up_bias.shape, F32), vector,
+        ],
+    )
+    return (
+        layer_out,
+        grad_tokens,
+        grad_in,
+        *outs[:12],
+        grad_out,
+        *outs[12:17],
+        grad_up[None],
+        outs[17],
+        grad_down[None],
+        outs[18],
+    )
+
+
 def solution(mesh):
     rows = P(("seq", "rep"), None)
     cut = P(None, "seq", "rep")
@@ -901,6 +1858,7 @@
     whole = P()
     ins = [rows, rows, whole, wide] + [whole] * 12 + [cut] + [whole] * 5 + [cut, whole, cut, whole]
     outs = [rows, rows, wide] + [whole] * 12 + [cut] + [whole] * 5 + [cut, whole, cut, whole]
+    fast = mesh.shape["seq"] == 8 and mesh.shape["rep"] == 4
     return jax.shard_map(
-        per_device, mesh=mesh, in_specs=tuple(ins), out_specs=tuple(outs), check_vma=False
-    )
+        per_device_fast if fast else per_device, mesh=mesh, in_specs=tuple(ins), out_specs=tuple(outs), check_vma=False
+    )

time: 449 us -> 327 us (0.73)
  between operations: 58.7 us -> 2.21 us
  waiting for transfers between devices: 119 us -> 79.2 us
  Pallas kernels: 34.1 us -> 72.2 us
  other arithmetic: 32.8 us -> 0 us
  matrix products: 31.8 us -> 0 us
  local copies, waits for them, and re-layouts: 71.8 us -> 52.2 us
  starting transfers between devices: 79.3 us -> 93.2 us
  blocking collectives: 14 us -> 24.3 us
    pallas_call x8 -> x51, Pallas kernels: 34.1 us -> 72.2 us  [call(): pl.pallas_call(kernel, out_shape=outs, in_specs=[space(a) for a in args],...]
    dot_general x13 -> x0, matrix products: 31.8 us -> none  [the longest x1 5.01 us: per_device(): grad_act = jnp.dot(mlp_rows, full_down, preferred_element_type=F32)]
    ppermute x41, waiting for transfers between devices: 76.2 us -> 46.9 us  [swap(): return lax.ppermute(values, axis_name, [(i, i ^ bit) for i in range(size)])]
    ppermute x26 -> x33, starting transfers between devices: 36.6 us -> 55.7 us  [the longest x14 30.5 us: ring_send(): return (lax.ppermute(left, 'seq', AHEAD), lax.ppermute(right, 'seq', BACK))]
    all_to_all x4 -> x2, waiting for transfers between devices: 16.9 us -> 0.01 us  [the longest x1 0.01 us: per_device_fast(): lax.all_to_all(gmix.reshape(8, chan, group), 'seq', 0, 0, tiled=True)]
    convert_element_type x21 -> x0, other arithmetic: 16.2 us -> none  [the longest x6 6.76 us: ring_scatter(): left, right = (left.astype(B16), right.astype(B16))]
    unnamed x289 -> x242, local copies, waits for them, and re-layouts: 35.7 us -> 51.5 us
    all_to_all x1 -> x2, blocking collectives: 14 us -> 24.3 us  [the longest x1 13.7 us: per_device_fast(): lax.all_to_all(gated.reshape(8, chan, group), 'seq', 0, 0, tiled=True)]
  transfers between devices with their start and end apart: 74 -> 76, of which waited for: 33 -> 30; matrix products, arithmetic and copies ran while one was open for 24% -> 1% of each run, Pallas kernels for 8% -> 20%
where the time goes in v3:
time: 327 us; the launch traced here: 323 us
  starting transfers between devices  93.2 us (29%)
  waiting for transfers between devices  79.2 us (24%)
  Pallas kernels  72.2 us (22%)
  local copies, waits for them, and re-layouts  52.2 us (16%)
  blocking collectives  24.3 us (7%)
    pallas_call x51, Pallas kernels, call(): pl.pallas_call(kernel, out_shape=outs, in_specs=[space(a) for a in args],...  72.2 us
    unnamed x242, local copies, waits for them, and re-layouts  51.5 us
    ppermute x41, waiting for transfers between devices, swap(): return lax.ppermute(values, axis_name, [(i, i ^ bit) for i in range(size)])  46.9 us
    ppermute x14, starting transfers between devices, ring_send(): return (lax.ppermute(left, 'seq', AHEAD), lax.ppermute(right, 'seq', BACK))  30.5 us
    ppermute x41, starting transfers between devices, swap(): return lax.ppermute(values, axis_name, [(i, i ^ bit) for i in range(size)])  27.6 us
    all_to_all x1, blocking collectives, per_device_fast(): lax.all_to_all(gated.reshape(8, chan, group), 'seq', 0, 0, tiled=True)  13.7 us
    ppermute x14, waiting for transfers between devices, ring_send(): return (lax.ppermute(left, 'seq', AHEAD), lax.ppermute(right, 'seq', BACK))  11.5 us
    all_to_all x1, blocking collectives, per_device_fast(): lax.all_to_all(mixed_chan, 'seq', 0, 0, tiled=True).reshape(width, group)  10.6 us
  transfers between devices with their start and end apart: 76, of which 30 were waited for; matrix products, arithmetic and copies ran while one was open for 1% of the time, Pallas kernels for 20%

profile of v3, /device:TPU:0, one launch (start us, length us, event | category | flops | bytes accessed | tf_op | source)
XLA Modules:
  0.0 323.2 jit_solution(2621335515966342018)
XLA Ops:
  3.1 3.0 collective-permute-start.6
  30.9 4.4 %filter_ahead.1 = (f32[128,1024]{1,0:T(8,128)S(1)}, f32[3,64,2048]{2,1,0:T(8,128)S(1)}, f32[3,64,2048]{2,1,0:T(8,128)S(1)}) custom-call(f32[33,2048]{1,0:T(8,128)S(1)} %copy-done.31, f32[1,2048]{1,0:T(1,128)S(1)} %copy-done.87, f32[32,2]{1,0:T(8,128)S(1)} %get-tuple-element.203.chan_ref, f32[1,33,64]{2,1,0:T(8,128)S(1)} %copy.62.w1_ref, ...), custom_call_target="tpu_custom_call" | custom-call | flops 1000000 | bytes 100000 | tf_op jit(solution)/shard_map/filter_ahead/pallas_call | solution.py:925
  38.0 4.1 %collective-permute-done.9.left_ref.p5 = bf16[128,1024]{1,0:T(8,128)(2,1)S(1)} collective-permute-done((bf16[128,1024]{1,0:T(8,128)(2,1)S(1)}, bf16[128,1024]{1,0:T(8,128)(2,1)S(1)}, u32[]{:S(2)}, u32[]{:S(2)}) %collective-permute-start.9) | collective-permute-done | bytes 262176 | tf_op jit(solution)/shard_map/ppermute | solution.py:1514
  45.5 2.9 collective-permute-done.11.a_ref
  54.7 4.3 %collective-permute-start.4 = (bf16[16,1024]{1,0:T(8,128)(2,1)S(1)}, bf16[16,1024]{1,0:T(8,128)(2,1)S(1)}, u32[]{:S(2)}, u32[]{:S(2)}) collective-permute-start(bf16[16,1024]{1,0:T(8,128)(2,1)S(1)} %get-tuple-element.199), channel_id=1, source_target_pairs={{0,28},{4,0},{8,4},{12,8},{16,12},{20,16},{24,20},{28,24},{1,29},{... | collective-permute-start | bytes 98312 | tf_op jit(solution)/shard_map/ppermute | solution.py:1666
  59.0 4.6 %collective-permute-done.3.before_ref = bf16[16,1024]{1,0:T(8,128)(2,1)S(1)} collective-permute-done((bf16[16,1024]{1,0:T(8,128)(2,1)S(1)}, bf16[16,1024]{1,0:T(8,128)(2,1)S(1)}, u32[]{:S(2)}, u32[]{:S(2)}) %collective-permute-start.3) | collective-permute-done | bytes 32800 | tf_op jit(solution)/shard_map/ppermute | solution.py:1665
  63.6 3.3 %project.1 = (bf16[3,256,512]{2,1,0:T(8,128)(2,1)S(1)}, bf16[3,256,256]{2,1,0:T(8,128)(2,1)S(1)}, bf16[256,512]{1,0:T(8,128)(2,1)S(1)}) custom-call(s32[34]{0:T(128)S(1)} %dynamic-slice_bitcast_fusion.meta_ref, s32[2]{0:T(128)S(1)} %copy-done.92, bf16[128,1024]{1,0:T(8,128)(2,1)S(1)} %norm_first.1.x0, bf16[128,1024]{1,0:T(8,128)(2,1)S(1)} %collective-permute-done.x1, ...), custom_call_target="tpu_custom_call" | custom-call | flops 1000000 | bytes 100000 | tf_op jit(solution)/shard_map/project/pallas_call | solution.py:925
  67.0 13.7 %all_to_all.20.x_ref = bf16[8,32,512]{2,1,0:T(8,128)(2,1)S(1)} all-to-all(bf16[8,32,512]{2,1,0:T(8,128)(2,1)S(1)} %bitcast.17), channel_id=1, replica_groups=mesh['seq'=8,'rep'=4] {'seq'}, dimensions={0} | all-to-all | bytes 524288 | tf_op jit(solution)/shard_map/all_to_all | solution.py:1679
  83.1 4.1 %conv_ahead.1 = (bf16[8,32,512]{2,1,0:T(8,128)(2,1)S(1)}, f32[256,1024]{1,0:T(8,128)S(1)}) custom-call(bf16[8,32,512]{2,1,0:T(8,128)(2,1)S(1)} %all_to_all.20.x_ref, f32[128,1024]{1,0:T(8,128)S(1)} %get-tuple-element.207.kern_ref, f32[4,4,2,512]{3,2,1,0:T(2,128)S(1)} %copy-done.48, bf16[1024,1024]{1,0:T(8,128)(2,1)S(1)} %copy-done.8, ...), custom_call_target="tpu_custom_call" | custom-call | flops 1000000 | bytes 100000 | tf_op jit(solution)/shard_map/conv_ahead/pallas_call | solution.py:925
  88.1 10.6 %all_to_all.21 = bf16[8,32,512]{2,1,0:T(8,128)(2,1)S(1)} all-to-all(bf16[8,32,512]{2,1,0:T(8,128)(2,1)S(1)} %get-tuple-element.219), channel_id=1, replica_groups=mesh['seq'=8,'rep'=4] {'seq'}, dimensions={0} | all-to-all | bytes 524288 | tf_op jit(solution)/shard_map/all_to_all | solution.py:1689
  105.3 7.1 %collective-permute-done.15.far_ref = bf16[128,1024]{1,0:T(8,128)(2,1)S(1)} collective-permute-done((bf16[128,1024]{1,0:T(8,128)(2,1)S(1)}, bf16[128,1024]{1,0:T(8,128)(2,1)S(1)}, u32[]{:S(2)}, u32[]{:S(2)}) %collective-permute-start.15) | collective-permute-done | bytes 262176 | tf_op jit(solution)/shard_map/ppermute | solution.py:23
  118.1 5.1 %collective-permute-done.17.x2 = bf16[128,1024]{1,0:T(8,128)(2,1)S(1)} collective-permute-done((bf16[128,1024]{1,0:T(8,128)(2,1)S(1)}, bf16[128,1024]{1,0:T(8,128)(2,1)S(1)}, u32[]{:S(2)}, u32[]{:S(2)}) %collective-permute-start.17) | collective-permute-done | bytes 262176 | tf_op jit(solution)/shard_map/ppermute | solution.py:23
  125.2 3.2 %mlp.1 = (bf16[512,1024]{1,0:T(8,128)(2,1)S(1)}, bf16[512,1024]{1,0:T(8,128)(2,1)S(1)}, f32[1,1024]{1,0:T(1,128)S(1)}) custom-call(bf16[128,1024]{1,0:T(8,128)(2,1)S(1)} %get-tuple-element.224.x0, bf16[128,1024]{1,0:T(8,128)(2,1)S(1)} %collective-permute-done.16.x1, bf16[128,1024]{1,0:T(8,128)(2,1)S(1)} %collective-permute-done.17.x2, ...), custom_call_target="tpu_custom_call" | custom-call | flops 1000000 | bytes 100000 | tf_op jit(solution)/shard_map/mlp/pallas_call | solution.py:925
  132.5 3.8 %mlp_grad.1 = (bf16[8,2,128,1024]{3,2,1,0:T(8,128)(2,1)S(1)}, bf16[128,1024]{1,0:T(8,128)(2,1)}, bf16[128,1024]{1,0:T(8,128)(2,1)}) custom-call(s32[34]{0:T(128)S(1)} %dynamic-slice_bitcast_fusion.meta_ref, bf16[128,1024]{1,0:T(8,128)(2,1)S(1)} %get-tuple-element.224.x0, bf16[128,1024]{1,0:T(8,128)(2,1)S(1)} %collective-permute-done.16.x1, ...), custom_call_target="tpu_custom_call" | custom-call | flops 1000000 | bytes 100000 | tf_op jit(solution)/shard_map/mlp_grad/pallas_call | solution.py:925
  142.7 7.0 %collective-permute-done.35.x2 = bf16[128,1024]{1,0:T(8,128)(2,1)S(1)} collective-permute-done((bf16[128,1024]{1,0:T(8,128)(2,1)S(1)}, bf16[128,1024]{1,0:T(8,128)(2,1)S(1)}, u32[]{:S(2)}, u32[]{:S(2)}) %collective-permute-start.35) | collective-permute-done | bytes 262176 | tf_op jit(solution)/shard_map/ppermute | solution.py:23
  157.8 4.0 %all-to-all-start.2 = ((bf16[8,32,512]{2,1,0:T(8,128)(2,1)}), bf16[8,32,512]{2,1,0:T(8,128)(2,1)}, u32[]{:S(2)}, u32[]{:S(2)}) async-start(bf16[8,32,512]{2,1,0:T(8,128)(2,1)} %bitcast.16), calls=%async_computation.2 | async-start | bytes 524288 | tf_op jit(solution)/shard_map/all_to_all | solution.py:1750
  167.9 11.7 %collective-permute-start.63 = (bf16[128,1024]{1,0:T(8,128)(2,1)}, bf16[128,1024]{1,0:T(8,128)(2,1)}, u32[]{:S(2)}, u32[]{:S(2)}) collective-permute-start(bf16[128,1024]{1,0:T(8,128)(2,1)} %get-tuple-element.344), channel_id=1, source_target_pairs={{8,0},{16,8},{24,16},{28,24},{20,28},{12,20},{4,12},{0,4},{9,1},{1... | collective-permute-start | bytes 786440 | tf_op jit(solution)/shard_map/ppermute | solution.py:1724
  186.6 6.1 %conv_back.1 = (bf16[8,32,640]{2,1,0:T(8,128)(2,1)S(1)}, f32[4,32,512]{2,1,0:T(8,128)S(1)}) custom-call(bf16[8,32,512]{2,1,0:T(8,128)(2,1)} %all-to-all-done.2.g_ref, f32[256,1024]{1,0:T(8,128)S(1)} %copy-done.46, f32[128,1024]{1,0:T(8,128)S(1)} %copy-done.26, f32[4,4,2,512]{3,2,1,0:T(2,128)S(1)} %copy-done.49, bf16[1024,1024]{1,0:T(8,128)(2,1)S(1)} %copy-done.9, ...), custom_call_target="tpu_custom_call" | custom-call | flops 1000000 | bytes 100000 | tf_op jit(solution)/shard_map/conv_back/pallas_call | solution.py:925
  194.1 5.9 %all-to-all-start.3 = ((bf16[8,32,640]{2,1,0:T(8,128)(2,1)}), bf16[8,32,640]{2,1,0:T(8,128)(2,1)}, u32[]{:S(2)}, u32[]{:S(2)}) async-start(bf16[8,32,640]{2,1,0:T(8,128)(2,1)} %copy-done.58), calls=%async_computation.3 | async-start | bytes 655360 | tf_op jit(solution)/shard_map/all_to_all | solution.py:1770
  205.7 6.6 %collective-permute-done.64.left_in = bf16[128,1024]{1,0:T(8,128)(2,1)S(1)} collective-permute-done((bf16[128,1024]{1,0:T(8,128)(2,1)S(1)}, bf16[128,1024]{1,0:T(8,128)(2,1)S(1)}, u32[]{:S(2)}, u32[]{:S(2)}) %collective-permute-start.64) | collective-permute-done | bytes 262176 | tf_op jit(solution)/shard_map/ppermute | solution.py:1724
  217.1 2.4 collective-permute-start.39
  222.9 3.5 %collective-permute-done.39.onext_ref = f32[256,128]{1,0:T(8,128)S(1)} collective-permute-done((f32[256,128]{1,0:T(8,128)S(1)}, f32[256,128]{1,0:T(8,128)S(1)}, u32[]{:S(2)}, u32[]{:S(2)}) %collective-permute-start.39) | collective-permute-done | bytes 131104 | tf_op jit(solution)/shard_map/ppermute | solution.py:1751
  233.6 7.5 %grad_short.1 = (bf16[4,128,768]{2,1,0:T(8,128)(2,1)S(1)}, f32[16,256]{1,0:T(8,128)S(1)}, f32[2,1024]{1,0:T(2,128)S(1)}, bf16[128,1024]{1,0:T(8,128)(2,1)S(1)}, ...) custom-call(s32[34]{0:T(128)S(1)} %dynamic-slice_bitcast_fusion.meta_ref, ...), custom_call_target="tpu_custom_call" | custom-call | flops 1000000 | bytes 100000 | tf_op jit(solution)/shard_map/grad_short/pallas_call | solution.py:925
  243.1 5.9 %filter_back.1 = (f32[64,256]{1,0:T(8,128)S(1)}, f32[64,256]{1,0:T(8,128)S(1)}) custom-call(s32[34]{0:T(128)S(1)} %dynamic-slice_bitcast_fusion.meta_ref, f32[4,32,512]{2,1,0:T(8,128)S(1)} %copy-done.67, f32[33,2048]{1,0:T(8,128)S(1)} %copy-done.32, f32[1,2048]{1,0:T(1,128)S(1)} %copy-done.88, f32[32,2]{1,0:T(8,128)S(1)} %copy-done.61, ...), custom_call_target="tpu_custom_call" | custom-call | flops 1000000 | bytes 100000 | tf_op jit(solution)/shard_map/filter_back/pallas_call | solution.py:925
  252.5 3.1 collective-permute-done.55.b_in
  256.9 3.4 %collective-permute-start.56 = (bf16[2,64,256]{2,1,0:T(8,128)(2,1)S(1)}, bf16[2,64,256]{2,1,0:T(8,128)(2,1)S(1)}, u32[]{:S(2)}, u32[]{:S(2)}) collective-permute-start(bf16[2,64,256]{2,1,0:T(8,128)(2,1)S(1)} %get-tuple-element.324), channel_id=1, source_target_pairs={{0,8},{4,12},{8,0},{12,4},{16,24},{20,28},{24,16},{28,20},{1,9},{5... | collective-permute-start | bytes 196616 | tf_op jit(solution)/shard_map/ppermute | solution.py:23
  260.9 8.0 %collective-permute-done.56.a_in = bf16[2,64,256]{2,1,0:T(8,128)(2,1)S(1)} collective-permute-done((bf16[2,64,256]{2,1,0:T(8,128)(2,1)S(1)}, bf16[2,64,256]{2,1,0:T(8,128)(2,1)S(1)}, u32[]{:S(2)}, u32[]{:S(2)}) %collective-permute-start.56) | collective-permute-done | bytes 65568 | tf_op jit(solution)/shard_map/ppermute | solution.py:23
  274.1 3.1 collective-permute-done.69.right_in
  277.9 5.8 %collective-permute-start.70 = (bf16[128,1024]{1,0:T(8,128)(2,1)S(1)}, bf16[128,1024]{1,0:T(8,128)(2,1)S(1)}, u32[]{:S(2)}, u32[]{:S(2)}) collective-permute-start(bf16[128,1024]{1,0:T(8,128)(2,1)S(1)} %get-tuple-element.359), channel_id=1, source_target_pairs={{0,8},{8,16},{16,24},{24,28},{28,20},{20,12},{12,4},{4,0},{1,9},{9... | collective-permute-start | bytes 786440 | tf_op jit(solution)/shard_map/ppermute | solution.py:1724
  291.6 2.4 collective-permute-start.58
  296.5 2.6 collective-permute-start.72
  301.5 5.2 %collective-permute-done.59.b_in = bf16[64,256]{1,0:T(8,128)(2,1)S(1)} collective-permute-done((bf16[64,256]{1,0:T(8,128)(2,1)S(1)}, bf16[64,256]{1,0:T(8,128)(2,1)S(1)}, u32[]{:S(2)}, u32[]{:S(2)}) %collective-permute-start.59) | collective-permute-done | bytes 32800 | tf_op jit(solution)/shard_map/ppermute | solution.py:23
  (416 shorter events, 152.6 us)
Async XLA Ops:
  3.1 16.6 %collective-permute-start.6 = (bf16[128,1024]{1,0:T(8,128)(2,1)S(1)}, bf16[128,1024]{1,0:T(8,128)(2,1)S(1)}, u32[]{:S(2)}, u32[]{:S(2)}) collective-permute-start(bf16[128,1024]{1,0:T(8,128)(2,1)S(1)} %pack_io.1.p0), channel_id=1, source_target_pairs={{8,0},{16,8},{24,16},{28,24},{20,28},{12,20},{4,12},{0,4},{9,1},{1... | collective-permute-start | bytes 786440 | tf_op jit(solution)/shard_map/ppermute | solution.py:1514
  6.1 13.7 %collective-permute-start.5 = (bf16[128,1024]{1,0:T(8,128)(2,1)S(1)}, bf16[128,1024]{1,0:T(8,128)(2,1)}, u32[]{:S(2)}, u32[]{:S(2)}) collective-permute-start(bf16[128,1024]{1,0:T(8,128)(2,1)S(1)} %pack_io.1.p0), channel_id=1, source_target_pairs={{0,8},{8,16},{16,24},{24,28},{28,20},{20,12},{12,4},{4,0},{1,9},{9... | collective-permute-start | bytes 786440 | tf_op jit(solution)/shard_map/ppermute | solution.py:1514
  19.8 15.6 %collective-permute-start.7 = (bf16[128,1024]{1,0:T(8,128)(2,1)}, bf16[128,1024]{1,0:T(8,128)(2,1)S(1)}, u32[]{:S(2)}, u32[]{:S(2)}) collective-permute-start(bf16[128,1024]{1,0:T(8,128)(2,1)} %collective-permute-done.5.p1), channel_id=1, source_target_pairs={{0,8},{8,16},{16,24},{24,28},{28,20},{20,12},{12,4},{4,0},{1,9},{9... | collective-permute-start | bytes 786440 | tf_op jit(solution)/shard_map/ppermute | solution.py:1514
  21.8 13.6 %collective-permute-start.8 = (bf16[128,1024]{1,0:T(8,128)(2,1)S(1)}, bf16[128,1024]{1,0:T(8,128)(2,1)S(1)}, u32[]{:S(2)}, u32[]{:S(2)}) collective-permute-start(bf16[128,1024]{1,0:T(8,128)(2,1)S(1)} %collective-permute-done.6.p2), channel_id=1, source_target_pairs={{8,0},{16,8},{24,16},{28,24},{20,28},{12,20},{4,12},{0,4},{9,1},{1... | collective-permute-start | bytes 786440 | tf_op jit(solution)/shard_map/ppermute | solution.py:1514
  23.5 14.0 %collective-permute-start.1 = (bf16[128,1024]{1,0:T(8,128)(2,1)S(1)}, bf16[128,1024]{1,0:T(8,128)(2,1)S(1)}, u32[]{:S(2)}, u32[]{:S(2)}) collective-permute-start(bf16[128,1024]{1,0:T(8,128)(2,1)S(1)} %norm_first.1.x0), channel_id=1, source_target_pairs={{0,2},{1,3},{2,0},{3,1},{4,6},{5,7},{6,4},{7,5},{8,10},{9,11},{10,... | collective-permute-start | bytes 786440 | tf_op jit(solution)/shard_map/ppermute | solution.py:23
  37.5 16.1 %collective-permute-start = (bf16[128,1024]{1,0:T(8,128)(2,1)S(1)}, bf16[128,1024]{1,0:T(8,128)(2,1)S(1)}, u32[]{:S(2)}, u32[]{:S(2)}) collective-permute-start(bf16[128,1024]{1,0:T(8,128)(2,1)S(1)} %norm_first.1.x0), channel_id=1, source_target_pairs={{0,1},{1,0},{2,3},{3,2},{4,5},{5,4},{6,7},{7,6},{8,9},{9,8},{10,11... | collective-permute-start | bytes 786440 | tf_op jit(solution)/shard_map/ppermute | solution.py:23
  37.5 16.1 %collective-permute-start.2 = (bf16[128,1024]{1,0:T(8,128)(2,1)S(1)}, bf16[128,1024]{1,0:T(8,128)(2,1)S(1)}, u32[]{:S(2)}, u32[]{:S(2)}) collective-permute-start(bf16[128,1024]{1,0:T(8,128)(2,1)S(1)} %collective-permute-done.1.x2), channel_id=1, source_target_pairs={{0,1},{1,0},{2,3},{3,2},{4,5},{5,4},{6,7},{7,6},{8,9},{9,8},{10,11... | collective-permute-start | bytes 786440 | tf_op jit(solution)/shard_map/ppermute | solution.py:23
  51.5 29.2 %collective-permute-start.23 = (bf16[2,128,1024]{2,1,0:T(8,128)(2,1)S(1)}, bf16[2,128,1024]{2,1,0:T(8,128)(2,1)S(1)}, u32[]{:S(2)}, u32[]{:S(2)}) collective-permute-start(bf16[2,128,1024]{2,1,0:T(8,128)(2,1)S(1)} %pack_ud.1.p0), channel_id=1, source_target_pairs={{8,0},{16,8},{24,16},{28,24},{20,28},{12,20},{4,12},{0,4},{9,1},{1... | collective-permute-start | bytes 1572872 | tf_op jit(solution)/shard_map/ppermute | solution.py:1514
  52.0 28.7 %collective-permute-start.22 = (bf16[2,128,1024]{2,1,0:T(8,128)(2,1)S(1)}, bf16[2,128,1024]{2,1,0:T(8,128)(2,1)S(1)}, u32[]{:S(2)}, u32[]{:S(2)}) collective-permute-start(bf16[2,128,1024]{2,1,0:T(8,128)(2,1)S(1)} %pack_ud.1.p0), channel_id=1, source_target_pairs={{0,8},{8,16},{16,24},{24,28},{28,20},{20,12},{12,4},{4,0},{1,9},{9... | collective-permute-start | bytes 1572872 | tf_op jit(solution)/shard_map/ppermute | solution.py:1514
  80.7 20.4 %collective-permute-start.24 = (bf16[2,128,1024]{2,1,0:T(8,128)(2,1)S(1)}, bf16[2,128,1024]{2,1,0:T(8,128)(2,1)S(1)}, u32[]{:S(2)}, u32[]{:S(2)}) collective-permute-start(bf16[2,128,1024]{2,1,0:T(8,128)(2,1)S(1)} %collective-permute-done.22.p1), channel_id=1, source_target_pairs={{0,8},{8,16},{16,24},{24,28},{28,20},{20,12},{12,4},{4,0},{1,9},{9... | collective-permute-start | bytes 1572872 | tf_op jit(solution)/shard_map/ppermute | solution.py:1514
  81.0 20.1 %collective-permute-start.25 = (bf16[2,128,1024]{2,1,0:T(8,128)(2,1)S(1)}, bf16[2,128,1024]{2,1,0:T(8,128)(2,1)S(1)}, u32[]{:S(2)}, u32[]{:S(2)}) collective-permute-start(bf16[2,128,1024]{2,1,0:T(8,128)(2,1)S(1)} %collective-permute-done.23.p2), channel_id=1, source_target_pairs={{8,0},{16,8},{24,16},{28,24},{20,28},{12,20},{4,12},{0,4},{9,1},{1... | collective-permute-start | bytes 1572872 | tf_op jit(solution)/shard_map/ppermute | solution.py:1514
  101.1 14.3 %collective-permute-start.26 = (bf16[2,128,1024]{2,1,0:T(8,128)(2,1)S(1)}, bf16[2,128,1024]{2,1,0:T(8,128)(2,1)S(1)}, u32[]{:S(2)}, u32[]{:S(2)}) collective-permute-start(bf16[2,128,1024]{2,1,0:T(8,128)(2,1)S(1)} %collective-permute-done.24.p3), channel_id=1, source_target_pairs={{0,8},{8,16},{16,24},{24,28},{28,20},{20,12},{12,4},{4,0},{1,9},{9... | collective-permute-start | bytes 1572872 | tf_op jit(solution)/shard_map/ppermute | solution.py:1514
  101.2 14.3 %collective-permute-start.27 = (bf16[2,128,1024]{2,1,0:T(8,128)(2,1)S(1)}, bf16[2,128,1024]{2,1,0:T(8,128)(2,1)S(1)}, u32[]{:S(2)}, u32[]{:S(2)}) collective-permute-start(bf16[2,128,1024]{2,1,0:T(8,128)(2,1)S(1)} %collective-permute-done.25.p4), channel_id=1, source_target_pairs={{8,0},{16,8},{24,16},{28,24},{20,28},{12,20},{4,12},{0,4},{9,1},{1... | collective-permute-start | bytes 1572872 | tf_op jit(solution)/shard_map/ppermute | solution.py:1514
  103.8 14.2 %collective-permute-start.20 = (bf16[128,1024]{1,0:T(8,128)(2,1)S(1)}, bf16[128,1024]{1,0:T(8,128)(2,1)S(1)}, u32[]{:S(2)}, u32[]{:S(2)}) collective-permute-start(bf16[128,1024]{1,0:T(8,128)(2,1)S(1)} %top.1.g0), channel_id=1, source_target_pairs={{0,2},{1,3},{2,0},{3,1},{4,6},{5,7},{6,4},{7,5},{8,10},{9,11},{10,... | collective-permute-start | bytes 786440 | tf_op jit(solution)/shard_map/ppermute | solution.py:23
  157.8 21.8 %all-to-all-start.2 = ((bf16[8,32,512]{2,1,0:T(8,128)(2,1)}), bf16[8,32,512]{2,1,0:T(8,128)(2,1)}, u32[]{:S(2)}, u32[]{:S(2)}) async-start(bf16[8,32,512]{2,1,0:T(8,128)(2,1)} %bitcast.16), calls=%async_computation.2 | async-start | bytes 524288 | tf_op jit(solution)/shard_map/all_to_all | solution.py:1750
  166.0 34.0 %collective-permute-start.62 = (bf16[128,1024]{1,0:T(8,128)(2,1)}, bf16[128,1024]{1,0:T(8,128)(2,1)}, u32[]{:S(2)}, u32[]{:S(2)}) collective-permute-start(bf16[128,1024]{1,0:T(8,128)(2,1)} %get-tuple-element.343), channel_id=1, source_target_pairs={{0,8},{8,16},{16,24},{24,28},{28,20},{20,12},{12,4},{4,0},{1,9},{9... | collective-permute-start | bytes 786440 | tf_op jit(solution)/shard_map/ppermute | solution.py:1724
  167.9 32.2 %collective-permute-start.63 = (bf16[128,1024]{1,0:T(8,128)(2,1)}, bf16[128,1024]{1,0:T(8,128)(2,1)}, u32[]{:S(2)}, u32[]{:S(2)}) collective-permute-start(bf16[128,1024]{1,0:T(8,128)(2,1)} %get-tuple-element.344), channel_id=1, source_target_pairs={{8,0},{16,8},{24,16},{28,24},{20,28},{12,20},{4,12},{0,4},{9,1},{1... | collective-permute-start | bytes 786440 | tf_op jit(solution)/shard_map/ppermute | solution.py:1724
  194.1 33.6 %all-to-all-start.3 = ((bf16[8,32,640]{2,1,0:T(8,128)(2,1)}), bf16[8,32,640]{2,1,0:T(8,128)(2,1)}, u32[]{:S(2)}, u32[]{:S(2)}) async-start(bf16[8,32,640]{2,1,0:T(8,128)(2,1)} %copy-done.58), calls=%async_computation.3 | async-start | bytes 655360 | tf_op jit(solution)/shard_map/all_to_all | solution.py:1770
  205.7 16.4 %collective-permute-start.37 = (bf16[128,1024]{1,0:T(8,128)(2,1)S(1)}, bf16[128,1024]{1,0:T(8,128)(2,1)S(1)}, u32[]{:S(2)}, u32[]{:S(2)}) collective-permute-start(bf16[128,1024]{1,0:T(8,128)(2,1)S(1)} %copy-done.111), channel_id=1, source_target_pairs={{0,1},{1,0},{2,3},{3,2},{4,5},{5,4},{6,7},{7,6},{8,9},{9,8},{10,11... | collective-permute-start | bytes 786440 | tf_op jit(solution)/shard_map/ppermute | solution.py:23
  215.3 33.9 %collective-permute-start.66 = (bf16[128,1024]{1,0:T(8,128)(2,1)}, bf16[128,1024]{1,0:T(8,128)(2,1)}, u32[]{:S(2)}, u32[]{:S(2)}) collective-permute-start(bf16[128,1024]{1,0:T(8,128)(2,1)} %get-tuple-element.351), channel_id=1, source_target_pairs={{0,8},{8,16},{16,24},{24,28},{28,20},{20,12},{12,4},{4,0},{1,9},{9... | collective-permute-start | bytes 786440 | tf_op jit(solution)/shard_map/ppermute | solution.py:1724
  219.5 30.1 %collective-permute-start.67 = (bf16[128,1024]{1,0:T(8,128)(2,1)}, bf16[128,1024]{1,0:T(8,128)(2,1)}, u32[]{:S(2)}, u32[]{:S(2)}) collective-permute-start(bf16[128,1024]{1,0:T(8,128)(2,1)} %get-tuple-element.352), channel_id=1, source_target_pairs={{8,0},{16,8},{24,16},{28,24},{20,28},{12,20},{4,12},{0,4},{9,1},{1... | collective-permute-start | bytes 786440 | tf_op jit(solution)/shard_map/ppermute | solution.py:1724
  222.1 27.0 %collective-permute-start.54 = (bf16[2,2,64,256]{3,2,1,0:T(8,128)(2,1)}, bf16[2,2,64,256]{3,2,1,0:T(8,128)(2,1)}, u32[]{:S(2)}, u32[]{:S(2)}) collective-permute-start(bf16[2,2,64,256]{3,2,1,0:T(8,128)(2,1)} %get-tuple-element.318), channel_id=1, source_target_pairs={{0,4},{4,0},{8,12},{12,8},{16,20},{20,16},{24,28},{28,24},{1,5},{5... | collective-permute-start | bytes 393224 | tf_op jit(solution)/shard_map/ppermute | solution.py:23
  222.1 34.8 %collective-permute-start.33 = (bf16[128,1024]{1,0:T(8,128)(2,1)}, bf16[128,1024]{1,0:T(8,128)(2,1)}, u32[]{:S(2)}, u32[]{:S(2)}) collective-permute-start(bf16[128,1024]{1,0:T(8,128)(2,1)} %get-tuple-element.251), channel_id=1, source_target_pairs={{0,1},{1,0},{2,3},{3,2},{4,5},{5,4},{6,7},{7,6},{8,9},{9,8},{10,11... | collective-permute-start | bytes 786440 | tf_op jit(solution)/shard_map/ppermute | solution.py:23
  227.1 33.6 %collective-permute-start.38 = (bf16[128,1024]{1,0:T(8,128)(2,1)}, bf16[128,1024]{1,0:T(8,128)(2,1)}, u32[]{:S(2)}, u32[]{:S(2)}) collective-permute-start(bf16[128,1024]{1,0:T(8,128)(2,1)} %add_far.6), channel_id=1, source_target_pairs={{0,2},{1,3},{2,0},{3,1},{4,6},{5,7},{6,4},{7,5},{8,10},{9,11},{10,... | collective-permute-start | bytes 786440 | tf_op jit(solution)/shard_map/ppermute | solution.py:23
  249.6 28.3 %collective-permute-start.44 = (bf16[2,2,64,768]{3,2,1,0:T(8,128)(2,1)S(1)}, bf16[2,2,64,768]{3,2,1,0:T(8,128)(2,1)S(1)}, u32[]{:S(2)}, u32[]{:S(2)}) collective-permute-start(bf16[2,2,64,768]{3,2,1,0:T(8,128)(2,1)S(1)} %get-tuple-element.285), channel_id=1, source_target_pairs={{0,8},{4,12},{8,0},{12,4},{16,24},{20,28},{24,16},{28,20},{1,9},{5... | collective-permute-start | bytes 1179656 | tf_op jit(solution)/shard_map/ppermute | solution.py:23
  255.6 16.2 %collective-permute-start.68 = (bf16[128,1024]{1,0:T(8,128)(2,1)S(1)}, bf16[128,1024]{1,0:T(8,128)(2,1)S(1)}, u32[]{:S(2)}, u32[]{:S(2)}) collective-permute-start(bf16[128,1024]{1,0:T(8,128)(2,1)S(1)} %get-tuple-element.355), channel_id=1, source_target_pairs={{0,8},{8,16},{16,24},{24,28},{28,20},{20,12},{12,4},{4,0},{1,9},{9... | collective-permute-start | bytes 786440 | tf_op jit(solution)/shard_map/ppermute | solution.py:1724
  271.0 14.0 %collective-permute-start.43 = (bf16[2,2,64,768]{3,2,1,0:T(8,128)(2,1)S(1)}, bf16[2,2,64,768]{3,2,1,0:T(8,128)(2,1)S(1)}, u32[]{:S(2)}, u32[]{:S(2)}) collective-permute-start(bf16[2,2,64,768]{3,2,1,0:T(8,128)(2,1)S(1)} %get-tuple-element.266), channel_id=1, source_target_pairs={{0,4},{4,0},{8,12},{12,8},{16,20},{20,16},{24,28},{28,24},{1,5},{5... | collective-permute-start | bytes 1179656 | tf_op jit(solution)/shard_map/ppermute | solution.py:23
  271.7 15.4 %collective-permute-start.41 = (bf16[128,1024]{1,0:T(8,128)(2,1)S(1)}, bf16[128,1024]{1,0:T(8,128)(2,1)S(1)}, u32[]{:S(2)}, u32[]{:S(2)}) collective-permute-start(bf16[128,1024]{1,0:T(8,128)(2,1)S(1)} %get-tuple-element.281), channel_id=1, source_target_pairs={{0,1},{1,0},{2,3},{3,2},{4,5},{5,4},{6,7},{7,6},{8,9},{9,8},{10,11... | collective-permute-start | bytes 786440 | tf_op jit(solution)/shard_map/ppermute | solution.py:23
  289.3 18.5 %collective-permute-start.42 = (bf16[128,1024]{1,0:T(8,128)(2,1)S(1)}, bf16[128,1024]{1,0:T(8,128)(2,1)S(1)}, u32[]{:S(2)}, u32[]{:S(2)}) collective-permute-start(bf16[128,1024]{1,0:T(8,128)(2,1)S(1)} %add_far.7), channel_id=1, source_target_pairs={{0,2},{1,3},{2,0},{3,1},{4,6},{5,7},{6,4},{7,5},{8,10},{9,11},{10,... | collective-permute-start | bytes 786440 | tf_op jit(solution)/shard_map/ppermute | solution.py:23
  294.6 24.5 %collective-permute-start.53 = (f32[264,256]{1,0:T(8,128)S(1)}, f32[264,256]{1,0:T(8,128)S(1)}, u32[]{:S(2)}, u32[]{:S(2)}) collective-permute-start(f32[264,256]{1,0:T(8,128)S(1)} %list_small.1.mine_ref), channel_id=1, source_target_pairs={{0,1},{1,0},{2,3},{3,2},{4,5},{5,4},{6,7},{7,6},{8,9},{9,8},{10,11... | collective-permute-start | bytes 811016 | tf_op jit(solution)/shard_map/ppermute | solution.py:23
  296.5 21.0 %collective-permute-start.72 = (bf16[128,1024]{1,0:T(8,128)(2,1)S(1)}, bf16[128,1024]{1,0:T(8,128)(2,1)S(1)}, u32[]{:S(2)}, u32[]{:S(2)}) collective-permute-start(bf16[128,1024]{1,0:T(8,128)(2,1)S(1)} %get-tuple-element.363), channel_id=1, source_target_pairs={{0,8},{8,16},{16,24},{24,28},{28,20},{20,12},{12,4},{4,0},{1,9},{9... | collective-permute-start | bytes 786440 | tf_op jit(solution)/shard_map/ppermute | solution.py:1724
  299.1 18.4 %collective-permute-start.73 = (bf16[128,1024]{1,0:T(8,128)(2,1)S(1)}, bf16[128,1024]{1,0:T(8,128)(2,1)S(1)}, u32[]{:S(2)}, u32[]{:S(2)}) collective-permute-start(bf16[128,1024]{1,0:T(8,128)(2,1)S(1)} %get-tuple-element.364), channel_id=1, source_target_pairs={{8,0},{16,8},{24,16},{28,24},{20,28},{12,20},{4,12},{0,4},{9,1},{1... | collective-permute-start | bytes 786440 | tf_op jit(solution)/shard_map/ppermute | solution.py:1724
  (160 other events, 1469.9 us)

commit v4 on v3

--- a/solution.py
+++ b/solution.py
@@ -917,19 +917,53 @@
     return np.asarray(rows, np.int32)
 
 
-def call(kernel, name, args, outs, scratch=(), limit=24):
-    def space(a):
+COST = {"start": 4000, "setup": 4000, "filter_ahead": 6000}
+
+
+def call(kernel, name, args, outs, scratch=(), limit=24, away=(), out_away=(), raw=()):
+    away, out_away, raw = list(away), list(out_away), list(raw)
+    hbm = pl.BlockSpec(memory_space=pltpu.HBM)
+
+    def space(i, a):
+        if i in away or i in raw:
+            return hbm
         small = a.dtype == jnp.int32
         return pl.BlockSpec(memory_space=pltpu.SMEM if small else pltpu.VMEM)
 
+    n_in, n_out, n_own = len(args), len(outs), len(scratch)
+    bufs = [pltpu.VMEM(args[i].shape, args[i].dtype) for i in away]
+    bufs += [pltpu.VMEM(outs[i].shape, outs[i].dtype) for i in out_away]
+    sems = [pltpu.SemaphoreType.DMA((len(bufs),))] if bufs else []
+
+    def body(*refs):
+        ins, results = list(refs[:n_in]), list(refs[n_in : n_in + n_out])
+        own, mine = refs[n_in + n_out : n_in + n_out + n_own], refs[n_in + n_out + n_own :]
+        copies = []
+        for k, i in enumerate(away):
+            copies.append(pltpu.make_async_copy(ins[i], mine[k], mine[-1].at[k]))
+            ins[i] = mine[k]
+        for copy in copies:
+            copy.start()
+        for copy in copies:
+            copy.wait()
+        copies = []
+        for k, i in enumerate(out_away, len(away)):
+            copies.append(pltpu.make_async_copy(mine[k], results[i], mine[-1].at[k]))
+            results[i] = mine[k]
+        kernel(*ins, *results, *own)
+        for copy in copies:
+            copy.start()
+        for copy in copies:
+            copy.wait()
+
     return pl.pallas_call(
-        kernel,
+        body,
         out_shape=outs,
-        in_specs=[space(a) for a in args],
-        out_specs=[pl.BlockSpec(memory_space=pltpu.VMEM) for _ in outs],
-        scratch_shapes=list(scratch),
+        in_specs=[space(i, a) for i, a in enumerate(args)],
+        out_specs=[hbm if i in out_away or (-1 - i) in raw else pl.BlockSpec(memory_space=pltpu.VMEM) for i in range(n_out)],
+        scratch_shapes=list(scratch) + bufs + sems,
         compiler_params=pltpu.CompilerParams(vmem_limit_bytes=limit * 2**20),
-        cost_estimate=pl.CostEstimate(flops=10**6, bytes_accessed=10**5, transcendentals=0),
+        cost_estimate=pl.CostEstimate(flops=COST.get(name, 1) * 10**6, bytes_accessed=10**5, transcendentals=0),
         name=name,
     )(*args)
 
@@ -964,16 +998,13 @@
     return real, exists
 
 
-def pack_io_kernel(in_ref, out_w_ref, out_ref):
+def start_kernel(x_ref, gain_ref, shift_ref, in_ref, out_w_ref, out_ref, io_ref):
     width = out_w_ref.shape[2]
     for p in range(3):
-        out_ref[:, p * width : (p + 1) * width] = in_ref[0, :, p, :]
-    out_ref[:, 3 * width :] = out_w_ref[0]
-
-
-def pack_ud_kernel(up_ref, down_ref, out_ref):
-    out_ref[0] = up_ref[0]
-    out_ref[1] = down_ref[0]
+        io_ref[:, p * width : (p + 1) * width] = in_ref[p]
+    io_ref[:, 3 * width :] = out_w_ref[0]
+    unit, _ = normed_of(x_ref[...].astype(F32))
+    out_ref[...] = (unit * gain_ref[...] + shift_ref[...]).astype(B16)
 
 
 def halves_kernel(left_ref, right_ref, a_ref, b_ref):
@@ -990,43 +1021,51 @@
     out_ref[meta_ref[OWNER + 7], half:] = b_ref[...]
 
 
-def norm_first_kernel(x_ref, gain_ref, shift_ref, out_ref):
-    unit, _ = normed_of(x_ref[...].astype(F32))
-    out_ref[...] = (unit * gain_ref[...] + shift_ref[...]).astype(B16)
-
-
 def own_mask(meta_ref, len_ref, rows):
     row = lax.broadcasted_iota(jnp.int32, (rows, 1), 0)
     return (meta_ref[AT] + meta_ref[REP] * rows + row < item_length(meta_ref, len_ref)).astype(F32)
 
 
-def top_kernel(meta_ref, len_ref, top_ref, out_ref):
-    mask = own_mask(meta_ref, len_ref, top_ref.shape[0])
-    out_ref[...] = (top_ref[...].astype(F32) * mask).astype(B16)
-
-
 def setup_kernel(
-    meta_ref, taps_ref, short_bias_ref, in_bias_ref, up_bias_ref, skip_ref, rate_ref, kern_w_ref, fb_ref, ib_ref, db_ref, sf_ref,
-    cols_ref, up_ref, chan_ref, columns_ref, small_col_ref, small_row_ref
+    meta_ref, len_ref, top_ref, up_ref, down_ref, taps_ref, short_bias_ref, in_bias_ref, up_bias_ref, skip_ref, rate_ref,
+    kern_w_ref, feat_ref, fb_ref, ib_ref, db_ref, sf_ref,
+    rows_ref, ud_ref, cols_ref, upb_ref, chan_ref, columns_ref, small_col_ref, small_row_ref, w1_ref, *rest
 ):
+    sems = rest[-1]
+    copies = [
+        pltpu.make_async_copy(up_ref, ud_ref.at[pl.ds(0, 1)], sems.at[0]),
+        pltpu.make_async_copy(down_ref, ud_ref.at[pl.ds(1, 1)], sems.at[1]),
+    ]
+    for copy in copies:
+        copy.start()
+    top, taps, short_bias, in_bias, up_bias, skip, rate, kern_w, feat, fb, ib, db, sf = (
+        top_ref, taps_ref, short_bias_ref, in_bias_ref, up_bias_ref, skip_ref, rate_ref, kern_w_ref, feat_ref,
+        fb_ref, ib_ref, db_ref, sf_ref,
+    )
+    mask = own_mask(meta_ref, len_ref, top.shape[0])
+    rows_ref[...] = (top[...].astype(F32) * mask).astype(B16)
     width = cols_ref.shape[0]
     chan = chan_ref.shape[0]
     rep, seq = meta_ref[REP], meta_ref[SEQ]
     lanes = pl.ds(pl.multiple_of(rep * width, width), width)
-    rows = [taps_ref[0, j, :, lanes] for j in range(3)] + [short_bias_ref[0, :, lanes], in_bias_ref[0, :, lanes]]
+    rows = [taps[j, p, :, lanes] for j in range(3) for p in range(3)]
+    rows += [short_bias[p, :, lanes] for p in range(3)] + [in_bias[p, :, lanes] for p in range(3)]
     stack = jnp.concatenate(rows + [jnp.zeros((LANE - 15, width), F32)], axis=0)
     cols_ref[...] = stack.T[:, :16]
-    up_ref[...] = up_bias_ref[:, pl.ds(pl.multiple_of(rep * up_ref.shape[1], LANE), up_ref.shape[1])]
+    upb_ref[...] = up_bias[:, pl.ds(pl.multiple_of(rep * upb_ref.shape[1], LANE), upb_ref.shape[1])]
     turn = width - seq * chan
-    stack = jnp.concatenate([skip_ref[:, lanes], rate_ref[:, lanes], jnp.zeros((LANE - 2, width), F32)], axis=0)
+    stack = jnp.concatenate([skip[:, lanes], rate[:, lanes], jnp.zeros((LANE - 2, width), F32)], axis=0)
     chan_ref[...] = pltpu.roll(stack, turn, 1)[:, :LANE].T[:chan, :2]
-    columns_ref[...] = pltpu.roll(kern_w_ref[0, :, lanes], turn, 1)[:, :chan]
+    columns_ref[...] = pltpu.roll(kern_w[0, :, lanes], turn, 1)[:, :chan]
     filt = small_row_ref.shape[1]
-    small = jnp.concatenate([fb_ref[...], ib_ref[...], db_ref[...], sf_ref[...]], axis=0)
+    small = jnp.concatenate([fb[...], ib[...], db[...], sf[...]], axis=0)
     small_row_ref[...] = small
     wide = jnp.concatenate([small, jnp.zeros((4, LANE - filt), F32)], axis=1)
     wide = jnp.concatenate([wide, jnp.zeros((LANE - 4, LANE), F32)], axis=0)
     small_col_ref[...] = wide.T[:filt, :4]
+    w1_ref[...] = jnp.concatenate([feat[i] for i in range(feat.shape[0])], axis=0)
+    for copy in copies:
+        copy.wait()
 
 
 def edges_kernel(meta_ref, x0, x1, x2, x3, last_ref, first_ref):
@@ -1062,8 +1101,11 @@
 
 
 def project_kernel(
-    meta_ref, len_ref, x0, x1, x2, x3, before_ref, after_ref, io_ref, cols_ref, proj_ref, halo_ref, gated_ref
+    meta_ref, len_ref, x0, x1, x2, x3, before_ref, after_ref, cols_ref,
+    p0, p1, p2, p3, p4, p5, p6, a_ref, b_ref, io_full_ref, proj_ref, halo_ref, gated_ref
 ):
+    assemble_kernel(meta_ref, p0, p1, p2, p3, p4, p5, p6, a_ref, b_ref, io_full_ref)
+    io_ref = io_full_ref.reshape(-1, io_full_ref.shape[2])
     rep = meta_ref[REP]
     width, group = gated_ref.shape
     weight = io_ref[:, : 3 * width]
@@ -1088,7 +1130,7 @@
 
 
 def out_project_kernel(
-    meta_ref, len_ref, proj_ref, halo_ref, cols_ref, mixed_ref, io_ref, y_ref, give3_ref, give1_ref, keep2_ref, keep0_ref
+    meta_ref, len_ref, proj_ref, halo_ref, cols_ref, io_ref, mixed_ref, y_ref, give3_ref, give1_ref, keep2_ref, keep0_ref
 ):
     rep = meta_ref[REP]
     width, group = mixed_ref.shape
@@ -1106,6 +1148,33 @@
         part = dot(left, io_ref[lo : lo + 256, 3 * width :], NT)
         for i, ref in enumerate(outs):
             ref[:, lo : lo + 256] = part[i * rows : (i + 1) * rows].astype(ref.dtype)
+
+
+def halves_far_kernel(left_ref, right_ref, a_ref, b_ref, sems):
+    half = a_ref.shape[0]
+    copies = [
+        pltpu.make_async_copy(left_ref.at[pl.ds(0, half)], a_ref, sems.at[0]),
+        pltpu.make_async_copy(right_ref.at[pl.ds(half, half)], b_ref, sems.at[1]),
+    ]
+    for copy in copies:
+        copy.start()
+    for copy in copies:
+        copy.wait()
+
+
+def assemble_far_kernel(meta_ref, p0, p1, p2, p3, p4, p5, p6, a_ref, b_ref, out_ref, sems):
+    half = a_ref.shape[0]
+    last = out_ref.at[meta_ref[OWNER + 7]]
+    copies = [
+        pltpu.make_async_copy(ref, out_ref.at[meta_ref[OWNER + k]], sems.at[k])
+        for k, ref in enumerate((p0, p1, p2, p3, p4, p5, p6))
+    ]
+    copies.append(pltpu.make_async_copy(a_ref, last.at[pl.ds(0, half)], sems.at[7]))
+    copies.append(pltpu.make_async_copy(b_ref, last.at[pl.ds(half, half)], sems.at[8]))
+    for copy in copies:
+        copy.start()
+    for copy in copies:
+        copy.wait()
 
 
 def norm_second_kernel(x_ref, keep_ref, near_ref, far_ref, bias_ref, gain_ref, shift_ref, middle_ref, out_ref):
@@ -1151,23 +1220,10 @@
             ref[:, k * owned : (k + 2) * owned] = part[i * rows : (i + 1) * rows].astype(ref.dtype)
 
 
-def mlp_grad_kernel(meta_ref, x0, x1, x2, x3, g0, g1, g2, g3, act_ref, gpre_ref, out_ref, left_ref, right_ref):
-    owners, _, owned, wide = out_ref.shape
-    for which, refs, right in ((0, (x0, x1, x2, x3), gpre_ref), (1, (g0, g1, g2, g3), act_ref)):
-        for k in range(0, owners, 2):
-            left = jnp.concatenate([r[:, k * owned : (k + 2) * owned] for r in refs], axis=0)
-            part = dot(left, right[...], TN).astype(B16)
-            out_ref[k, which] = part[:owned]
-            out_ref[k + 1, which] = part[owned:]
-    left_ref[...] = out_ref[meta_ref[LEFT + 1], 0]
-    right_ref[...] = out_ref[meta_ref[RIGHT + 1], 1]
-
-
-def ring_add_kernel(step, meta_ref, term_ref, left_in, right_in, left_ref, right_ref):
-    mine = term_ref[meta_ref[LEFT + step], 0].astype(F32)
-    left_ref[...] = (left_in[...].astype(F32) + mine).astype(left_ref.dtype)
-    mine = term_ref[meta_ref[RIGHT + step], 1].astype(F32)
-    right_ref[...] = (right_in[...].astype(F32) + mine).astype(right_ref.dtype)
+def mlp_grad_kernel(meta_ref, x0, x1, x2, x3, g0, g1, g2, g3, act_ref, gpre_ref, out_ref, a_ref, b_ref):
+    grad_pair((x0, x1, x2, x3), gpre_ref[...], out_ref, slice(None), 0)
+    grad_pair((g0, g1, g2, g3), act_ref[...], out_ref, slice(None), out_ref.shape[3] // 2)
+    give_first(meta_ref, out_ref, a_ref, b_ref)
 
 
 def norm_second_back_kernel(
@@ -1189,7 +1245,7 @@
 
 
 def grad_gate_kernel(
-    meta_ref, len_ref, x0, x1, x2, x3, io_ref, proj_ref, halo_ref, cols_ref, mixed_ref, gy_ref, gmix_ref, first_ref
+    meta_ref, len_ref, x0, x1, x2, x3, io_ref, proj_ref, halo_ref, cols_ref, mixed_ref, gy_ref, first_ref, gmix_ref
 ):
     rep = meta_ref[REP]
     width, group = mixed_ref.shape
@@ -1206,7 +1262,7 @@
 
 
 def conv_back_kernel(
-    g_ref, spec_ref, kern_ref, twist_ref, hi_ref, lo_ref, chan_ref, out_ref, grad_kern_ref, z_ref, p_ref
+    spec_ref, kern_ref, twist_ref, hi_ref, lo_ref, chan_ref, g_ref, out_ref, grad_kern_ref, z_ref, p_ref
 ):
     blocks, rows, length = twist_ref.shape[0], g_ref.shape[1], g_ref.shape[2]
     short_blocks = blocks // 4
@@ -1222,36 +1278,29 @@
     p_ref[2 * span :] = times(grad[:span], spec_ref[0:span], True) + times(grad[span:], spec_ref[span:], True)
     w = dot_split(p_ref[...], hi_ref[...], lo_ref[...], ((1,), (1,)))
     skip = chan_ref[:, 0:1]
-    zero = jnp.zeros((rows, LANE), B16)
     for b in range(blocks):
         acc = (back_rows(w, 0, rows, b, twist_ref, blocks) + skip * first[b]).astype(B16)
-        out_ref[b, :, :length] = acc
-        if b:
-            out_ref[b - 1, :, length:] = acc[:, :LANE]
+        out_ref[b] = acc
         if b < short_blocks:
             acc = (back_rows(w, span, rows, b, twist_ref, blocks) + skip * second[b]).astype(B16)
         else:
             acc = jnp.zeros((rows, length), B16)
-        out_ref[blocks + b, :, :length] = acc
-        if b:
-            out_ref[blocks + b - 1, :, length:] = acc[:, :LANE]
+        out_ref[blocks + b] = acc
         grad_kern_ref[b] = back_rows(w, 2 * span, rows, b, twist_ref, blocks)
-    out_ref[blocks - 1, :, length:] = zero
-    out_ref[2 * blocks - 1, :, length:] = zero
-
-
-def conv_ahead_kernel(x_ref, kern_ref, twist_ref, hi_ref, lo_ref, chan_ref, out_ref, spec_ref, z_ref):
+
+
+def conv_ahead_kernel(kern_ref, twist_ref, hi_ref, lo_ref, chan_ref, x_ref, out_ref, spec_ref, z_ref):
     conv_forward_kernel(
         twist_ref.shape[0] // 4, x_ref, kern_ref, twist_ref, hi_ref, lo_ref, chan_ref.at[:, 0:1], out_ref, spec_ref, z_ref
     )
 
 
 def filter_ahead_kernel(
-    grid_ref, ramp_ref, chan_ref, w1_ref, w2_ref, w3_ref, small_ref, columns_ref, twist_ref, hi_ref, lo_ref,
+    chan_ref, w1_ref, small_ref, columns_ref, grid_ref, ramp_ref, w2_ref, w3_ref, twist_ref, hi_ref, lo_ref,
     spec_ref, sin_ref, cos_ref, z_ref
 ):
     filter_forward_kernel(
-        grid_ref, ramp_ref, chan_ref.at[:, 1:2], w1_ref.at[0], w2_ref.at[0], w3_ref.at[0], small_ref, columns_ref,
+        grid_ref, ramp_ref, chan_ref.at[:, 1:2], w1_ref, w2_ref.at[0], w3_ref.at[0], small_ref, columns_ref,
         twist_ref, hi_ref, lo_ref, spec_ref, sin_ref, cos_ref, z_ref
     )
 
@@ -1274,16 +1323,16 @@
     ones = jnp.ones((8, gk.shape[1]), F32)
     gfreq = jnp.zeros((1, filt), F32)
     grads, biases = [None] * 3, [None] * 3
-    for i, w_ref in ((2, w3_ref), (1, w2_ref), (0, w1_ref)):
+    for i, weight in ((2, w3_ref[0]), (1, w2_ref[0]), (0, w1_ref[...])):
         turn = grad * cos_ref[i]
         below = sin_ref[i - 1] if i else grid_ref[...]
         raw = dot_high(below, turn, NT)
         total = dot_high(ones, turn, NT)[0:1]
         grads[i] = raw * freq_row
         biases[i] = total * freq_row
-        gfreq = gfreq + jnp.sum(raw * w_ref[0], axis=0, keepdims=True) + total * row_ref[i : i + 1, :]
+        gfreq = gfreq + jnp.sum(raw * weight, axis=0, keepdims=True) + total * row_ref[i : i + 1, :]
         if i:
-            grad = dot_high(w_ref[0], turn * freq, NN)
+            grad = dot_high(weight, turn * freq, NN)
     gap = jnp.zeros((filt - grads[0].shape[0], filt), F32)
     small = jnp.concatenate(biases + [gfreq, jnp.zeros((filt - 4, filt), F32)], axis=0)
     side_ref[...] = jnp.concatenate(
@@ -1291,10 +1340,33 @@
     )
 
 
-def grad_short_kernel(
-    meta_ref, len_ref, proj_ref, halo_ref, cols_ref, mixed_ref, gy_ref, ggated_ref, onext_ref, io_ref,
-    x0, x1, x2, x3, gain_ref, shift_ref,
-    tok_ref, sum_ref, norm_ref, give3_ref, give1_ref, keep2_ref, keep0_ref
+def summed(value):
+    total = value[:, :LANE]
+    for k in range(LANE, value.shape[1], LANE):
+        total = total + value[:, k : k + LANE]
+    return jnp.sum(total, axis=1, keepdims=True)
+
+
+def short_back(ext, cols, gshort, p, mid):
+    size = ext.shape[1]
+    mine = gshort[:, mid]
+    gproj = (
+        cols[:, 6 + p : 7 + p] * gshort
+        + cols[:, 3 + p : 4 + p] * pltpu.roll(gshort, size - 1, 1)
+        + cols[:, p : p + 1] * pltpu.roll(gshort, size - 2, 1)
+    )[:, mid].astype(B16).astype(F32)
+    sums = [
+        summed(mine),
+        summed(mine * ext[:, mid]),
+        summed(mine * pltpu.roll(ext, 1, 1)[:, mid]),
+        summed(mine * pltpu.roll(ext, 2, 1)[:, mid]),
+        summed(gproj),
+    ]
+    return gproj, sums
+
+
+def grad_first_kernel(
+    meta_ref, len_ref, proj_ref, halo_ref, cols_ref, mixed_ref, gy_ref, onext_ref, io_ref, tok_ref, sum_ref, part_ref
 ):
     rep = meta_ref[REP]
     width, group = mixed_ref.shape
@@ -1302,56 +1374,61 @@
     mask, exists = lane_masks(meta_ref, len_ref, size)
     mid = slice(LANE, size - LANE)
     next_on = exists[:, size - LANE :]
-    ones = jnp.ones((LANE, group), F32)
-    del ones
     columns = []
     for lo in range(0, width, PART):
         rows = slice(lo, lo + PART)
         cols = cols_ref[rows, :]
         gy = gy_ref[rows, :].astype(F32)
-        zero = jnp.zeros((PART, LANE), F32)
-        ext = [ext_of(proj_ref, halo_ref, exists, p, rows) for p in range(3)]
-        short = [short_from(ext[p], cols, p) for p in range(3)]
-        ggated = jnp.concatenate([zero, ggated_ref[rows, :].astype(F32)], axis=1) * (mask * exists)
         gout = gy * mixed_ref[rows, :].astype(F32)
-        gshort = [
-            jnp.concatenate([zero, gout, onext_ref[rows, :] * next_on], axis=1),
-            ggated * short[2],
-            ggated * short[1],
-        ]
-        gated = short[2][:, mid] * short[1][:, mid] * mask[:, mid]
-
-        def summed(value):
-            parts = [value[:, k : k + LANE] for k in range(0, group, LANE)]
-            total = parts[0]
-            for part in parts[1:]:
-                total = total + part
-            return jnp.sum(total, axis=1, keepdims=True)
-
-        sums = [summed(gy * short[0][:, mid] * gated)]
-        for p in range(3):
-            mine = gshort[p][:, mid]
-            sums.append(summed(mine))
-            sums.append(summed(mine * ext[p][:, mid]))
-            sums.append(summed(mine * pltpu.roll(ext[p], 1, 1)[:, mid]))
-            sums.append(summed(mine * pltpu.roll(ext[p], 2, 1)[:, mid]))
-            gproj = (
-                cols[:, 6 + p : 7 + p] * gshort[p]
-                + cols[:, 3 + p : 4 + p] * pltpu.roll(gshort[p], size - 1, 1)
-                + cols[:, p : p + 1] * pltpu.roll(gshort[p], size - 2, 1)
-            )[:, mid].astype(B16).astype(F32)
-            sums.append(summed(gproj))
-            at = slice(p * width + lo, p * width + lo + PART)
+        gshort = jnp.concatenate([jnp.zeros((PART, LANE), F32), gout, onext_ref[rows, :] * next_on], axis=1)
+        gproj, sums = short_back(ext_of(proj_ref, halo_ref, exists, 0, rows), cols, gshort, 0, mid)
+        for j in range(4):
+            tok_ref[rep ^ j, :, rows] = gproj[:, j * LANE : (j + 1) * LANE].T.astype(B16)
+        columns.append(jnp.concatenate(sums + [jnp.zeros((PART, LANE - 5), F32)], axis=1))
+    sum_ref[...] = jnp.concatenate(columns, axis=0).T[:8]
+    part_ref[...] = dot(tok_ref[...].reshape(-1, width), io_ref[:, :width], NT)
+
+
+def grad_short_kernel(
+    meta_ref, len_ref, proj_ref, halo_ref, cols_ref, gy_ref, io_ref, before_ref,
+    x0, x1, x2, x3, gain_ref, shift_ref, ggated_ref, gnext_ref,
+    tok_ref, sum_ref, norm_ref, give3_ref, give1_ref, keep2_ref, keep0_ref
+):
+    rep = meta_ref[REP]
+    width, group = gy_ref.shape
+    size = group + 2 * LANE
+    mask, exists = lane_masks(meta_ref, len_ref, size)
+    mid = slice(LANE, size - LANE)
+    columns = []
+    for lo in range(0, width, PART):
+        rows = slice(lo, lo + PART)
+        cols = cols_ref[rows, :]
+        ext = [ext_of(proj_ref, halo_ref, exists, p, rows) for p in (1, 2)]
+        short = [short_from(ext[p - 1], cols, p) for p in (1, 2)]
+        ggated = (
+            jnp.concatenate(
+                [jnp.zeros((PART, LANE), F32), ggated_ref[rows, :].astype(F32), gnext_ref[rows, :].astype(F32)], axis=1
+            )
+            * mask
+            * exists
+        )
+        gate_out = short_from(ext_of(proj_ref, halo_ref, exists, 0, rows), cols, 0)[:, mid]
+        gated = short[1][:, mid] * short[0][:, mid] * mask[:, mid]
+        sums = [summed(gy_ref[rows, :].astype(F32) * gate_out * gated)]
+        for p in (1, 2):
+            gproj, more = short_back(ext[p - 1], cols, ggated * short[2 - p], p, mid)
+            sums += more
+            at = slice((p - 1) * width + lo, (p - 1) * width + lo + PART)
             for j in range(4):
                 tok_ref[rep ^ j, :, at] = gproj[:, j * LANE : (j + 1) * LANE].T.astype(B16)
-        columns.append(jnp.concatenate(sums + [jnp.zeros((PART, LANE - 16), F32)], axis=1))
+        columns.append(jnp.concatenate(sums + [jnp.zeros((PART, LANE - 11), F32)], axis=1))
     sum_ref[...] = jnp.concatenate(columns, axis=0).T[:16]
     outs = (keep0_ref, give1_ref, keep2_ref, give3_ref)
-    left = tok_ref[...].reshape(-1, 3 * width)
+    left = tok_ref[...].reshape(-1, 2 * width)
     tall = tok_ref.shape[1]
     for lo in range(0, io_ref.shape[0], 256):
         cut = slice(lo, lo + 256)
-        part = dot(left, io_ref[cut, : 3 * width], NT)
+        part = dot(left, io_ref[cut, width : 3 * width], NT) + before_ref[:, cut]
         plain = jnp.sum(part, axis=0, keepdims=True)
         cross = None
         for i, (ref, x_ref) in enumerate(zip(outs, (x0, x1, x2, x3))):
@@ -1373,14 +1450,25 @@
             b_ref[i, j] = term_ref[i, 1 - s1, j, half:]
 
 
-def weight_grad_kernel(meta_ref, x0, x1, x2, x3, right_ref, out_ref, a_ref, b_ref):
-    owned, wide = out_ref.shape[3], out_ref.shape[4]
-    right = right_ref[...].reshape(-1, wide)
+def grad_pair(refs, right, out_ref, lanes, base=0):
+    owned = refs[0].shape[1] // 8
     for k in range(0, 8, 2):
-        left = jnp.concatenate([r[:, k * owned : (k + 2) * owned] for r in (x0, x1, x2, x3)], axis=0)
+        left = jnp.concatenate([r[:, k * owned : (k + 2) * owned] for r in refs], axis=0)
         part = dot(left, right, TN).astype(B16)
-        out_ref[k // 4, (k // 2) % 2, 0] = part[:owned]
-        out_ref[k // 4, (k // 2) % 2, 1] = part[owned:]
+        out_ref[k // 4, (k // 2) % 2, 0, base : base + owned, lanes] = part[:owned]
+        out_ref[k // 4, (k // 2) % 2, 1, base : base + owned, lanes] = part[owned:]
+
+
+def grad_early_kernel(meta_ref, g0, g1, g2, g3, y_ref, x0, x1, x2, x3, tok_ref, out_ref, a_ref, b_ref):
+    width = y_ref.shape[2]
+    grad_pair((g0, g1, g2, g3), y_ref[...].reshape(-1, width), out_ref, slice(0, width))
+    grad_pair((x0, x1, x2, x3), tok_ref[...].reshape(-1, width), out_ref, slice(width, 2 * width))
+    give_first(meta_ref, out_ref, a_ref, b_ref)
+
+
+def grad_late_kernel(meta_ref, x0, x1, x2, x3, tok_ref, out_ref, a_ref, b_ref):
+    width = tok_ref.shape[2]
+    grad_pair((x0, x1, x2, x3), tok_ref[...].reshape(-1, width), out_ref, slice(0, width))
     give_first(meta_ref, out_ref, a_ref, b_ref)
 
 
@@ -1403,17 +1491,25 @@
     give_b[...] = (keep_b_in[1 - s2] + b_in[1 - s2].astype(F32)).astype(B16)
 
 
-def halve_last_kernel(keep_a, keep_b, a_in, b_in, out_ref):
-    half = keep_a.shape[0]
-    if len(out_ref.shape) == 3:
-        out_ref[0, :half] = keep_a[...] + a_in[...].astype(F32)
-        out_ref[0, half:] = keep_b[...] + b_in[...].astype(F32)
-        return
-    width = out_ref.shape[3]
-    for p in range(3):
-        cut = slice(p * width, (p + 1) * width)
-        out_ref[0, :half, p, :] = keep_a[:, cut] + a_in[:, cut].astype(F32)
-        out_ref[0, half:, p, :] = keep_b[:, cut] + b_in[:, cut].astype(F32)
+def far_last_kernel(keep_a, keep_b, a_in, b_in, up_ref, down_ref):
+    up_ref[0] = keep_a[...] + a_in[...].astype(F32)
+    down_ref[0] = keep_b[...] + b_in[...].astype(F32)
+
+
+def early_last_kernel(keep_a, keep_b, a_in, b_in, out_ref, in_ref):
+    half, width = keep_a.shape[0], out_ref.shape[2]
+    for keep, came, rows in ((keep_a, a_in, slice(0, half)), (keep_b, b_in, slice(half, 2 * half))):
+        out_ref[0, rows] = keep[:, :width] + came[:, :width].astype(F32)
+        in_ref[rows] = keep[:, width:] + came[:, width:].astype(F32)
+
+
+def late_last_kernel(keep_a, keep_b, a_in, b_in, first_ref, out_ref):
+    half, width = keep_a.shape[0], out_ref.shape[3]
+    out_ref[0, 0] = first_ref[...]
+    for keep, came, rows in ((keep_a, a_in, slice(0, half)), (keep_b, b_in, slice(half, 2 * half))):
+        for p in range(2):
+            lanes = slice(p * width, (p + 1) * width)
+            out_ref[0, 1 + p, rows] = keep[:, lanes] + came[:, lanes].astype(F32)
 
 
 def norm_first_back_kernel(keep_ref, near_ref, far_ref, x_ref, middle_ref, gain_ref, out_ref):
@@ -1430,6 +1526,10 @@
     out_ref[...] = (middle_ref[...] + (part + bias_ref[...])).astype(B16)
 
 
+def heads_kernel(in_ref, out_ref):
+    out_ref[...] = in_ref[:, :LANE]
+
+
 def add_far_kernel(keep_ref, came_ref, out_ref):
     out_ref[...] = (keep_ref[...] + came_ref[...].astype(F32)).astype(B16)
 
@@ -1437,7 +1537,7 @@
 HALF = 88
 
 
-def pack_small_kernel(side_ref, wide_ref, col_ref, up_ref, one_ref, two_ref, out_ref):
+def pack_small_kernel(side_ref, wide_ref, col0_ref, col_ref, up_ref, one_ref, two_ref, out_ref):
     filt, width = side_ref.shape
     out_ref[:filt] = side_ref[...]
     at = filt
@@ -1446,7 +1546,9 @@
             for k in range(4):
                 out_ref[at : at + 1] = ref[r : r + 1, k * width : (k + 1) * width]
                 at += 1
-    out_ref[HALF : HALF + 16] = col_ref[...]
+    out_ref[HALF : HALF + 1] = col_ref[0:1]
+    out_ref[HALF + 1 : HALF + 6] = col0_ref[0:5]
+    out_ref[HALF + 6 : HALF + 16] = col_ref[1:11]
     for k in range(4):
         out_ref[HALF + 16 + k : HALF + 17 + k] = up_ref[:, k * width : (k + 1) * width]
     out_ref[HALF + 20 : HALF + 24] = jnp.zeros((4, width), F32)
@@ -1469,11 +1571,12 @@
     in_bias, taps, short_bias, fw, fb, iw, ib, dw, db, sf, kern_w, skip, out_b, n1g, n1s, n2g, n2s, up_b, down_b
 ):
     core = meta_ref[REP] & 1
-    filt, width = fw.shape[2], mine_ref.shape[1]
+    filt, width = iw.shape[2], mine_ref.shape[1]
     total = mine_ref[:HALF] + came_ref[:HALF]
     iw[0] = total[:filt, :filt]
     dw[0] = total[:filt, filt : 2 * filt]
-    fw[0] = total[: fw.shape[1], 2 * filt : 3 * filt]
+    for k in range(fw.shape[0]):
+        fw[k] = total[k : k + 1, 2 * filt : 3 * filt]
     for k, ref in enumerate((fb, ib, db, sf)):
         ref[...] = total[k : k + 1, 3 * filt :]
     at = filt
@@ -1490,10 +1593,10 @@
             skip[:, lanes] = block[0:1]
             for p in range(3):
                 row = 1 + 5 * p
-                short_bias[0, p : p + 1, lanes] = block[row : row + 1]
+                short_bias[p, :, lanes] = block[row : row + 1]
                 for j in range(3):
-                    taps[0, j, p : p + 1, lanes] = block[row + 3 - j : row + 4 - j]
-                in_bias[0, p : p + 1, lanes] = block[row + 4 : row + 5]
+                    taps[j, p, :, lanes] = block[row + 3 - j : row + 4 - j]
+                in_bias[p, :, lanes] = block[row + 4 : row + 5]
             for k in range(4):
                 lo_up = (2 * y + c) * 4 * width + k * width
                 up_b[:, lo_up : lo_up + width] = block[16 + k : 17 + k]
@@ -1505,8 +1608,8 @@
 
 
 class RingGather:
-    def __init__(self, name, meta, shard):
-        self.name, self.meta = name, meta
+    def __init__(self, name, meta, shard, far=False):
+        self.name, self.meta, self.far = name, meta, far
         self.pieces = [shard]
         self.send(shard, shard)
 
@@ -1519,7 +1622,13 @@
         count = len(self.pieces)
         if count == 7:
             half = shape((left.shape[0] // 2,) + left.shape[1:], B16)
-            left, right = call(halves_kernel, self.name + "_halves", [left, right], [half, half])
+            if self.far:
+                left, right = call(
+                    halves_far_kernel, self.name + "_halves", [left, right], [half, half],
+                    scratch=[pltpu.SemaphoreType.DMA((2,))], raw=[0, 1, -1, -2],
+                )
+            else:
+                left, right = call(halves_kernel, self.name + "_halves", [left, right], [half, half])
         if count < 9:
             self.send(left, right)
         return self.came
@@ -1527,12 +1636,13 @@
     def full(self, *others):
         left, right = tie(self.came, *others)
         pieces = self.pieces + [left, right]
-        return call(
-            assemble_kernel,
-            self.name + "_assemble",
-            [self.meta, *pieces],
-            [shape((8,) + self.pieces[0].shape, B16)],
-        )[0]
+        whole = [shape((8,) + self.pieces[0].shape, B16)]
+        if self.far:
+            return call(
+                assemble_far_kernel, self.name + "_assemble", [self.meta, *pieces], whole,
+                scratch=[pltpu.SemaphoreType.DMA((9,))], raw=range(1, 10),
+            )[0]
+        return call(assemble_kernel, self.name + "_assemble", [self.meta, *pieces], whole)[0]
 
 
 def gather_four(rows):
@@ -1550,33 +1660,32 @@
 
 
 class Halving:
-    def __init__(self, name, meta, term, give, out_dims):
-        self.name, self.meta, self.term, self.out_dims = name, meta, term, out_dims
-        self.stage = 0
+    def __init__(self, name, meta, term, give):
+        self.name, self.meta, self.term = name, meta, term
         self.came = (swap(give[0], "seq", 1), swap(give[1], "seq", 2))
 
-    def step(self, *others):
-        came = tie(self.came, *others)
-        self.stage += 1
+    def one(self, *others):
         rows, cols = self.term.shape[3] // 2, self.term.shape[4]
-        if self.stage == 1:
-            lead = (2, rows, cols)
-            ka, kb, ga, gb = call(
-                halve_one_kernel, self.name + "_one", [self.meta, self.term, *came],
-                [shape(lead, F32)] * 2 + [shape(lead, B16)] * 2,
-            )
-            self.came = (swap(ga, "seq", 2), swap(gb, "seq", 1))
-        elif self.stage == 2:
-            lead = (rows, cols)
-            ka, kb, ga, gb = call(
-                halve_two_kernel, self.name + "_two", [self.meta, *self.keep, *came],
-                [shape(lead, F32)] * 2 + [shape(lead, B16)] * 2,
-            )
-            self.came = (swap(ga, "seq", 4), swap(gb, "seq", 4))
-        else:
-            return call(halve_last_kernel, self.name + "_last", [*self.keep, *came], [shape(self.out_dims, F32)])[0]
-        self.keep = (ka, kb)
-        return self.keep
+        outs = [shape((2, rows, cols), F32)] * 2 + [shape((2, rows, cols), B16)] * 2
+        args = [self.meta, self.term, *tie(self.came, *others)]
+        *self.keep, ga, gb = call(halve_one_kernel, self.name + "_one", args, outs)
+        self.came = (swap(ga, "seq", 2), swap(gb, "seq", 1))
+        return ga
+
+    def two(self, *others):
+        rows, cols = self.term.shape[3] // 2, self.term.shape[4]
+        outs = [shape((rows, cols), F32)] * 2 + [shape((rows, cols), B16)] * 2
+        args = [self.meta, *self.keep, *tie(self.came, *others)]
+        *self.keep, ga, gb = call(halve_two_kernel, self.name + "_two", args, outs)
+        self.came = (swap(ga, "seq", 4), swap(gb, "seq", 4))
+        return ga
+
+    def last(self, *others):
+        return [*self.keep, *tie(self.came, *others)]
+
+
+def exchange(blocks):
+    return lax.all_to_all(blocks, "seq", 0, 0, tiled=True)
 
 
 def per_device_fast(
@@ -1622,77 +1731,91 @@
     sums_shapes = [row_b16, row_b16, row_f32, row_f32]
     flat_shape = shape((width, group), B16)
 
-    (io_shard,) = call(pack_io_kernel, "pack_io", [in_weight, out_weight], [shape((owned, 4 * width), B16)])
+    normed, io_shard = call(
+        start_kernel,
+        "start",
+        [tokens, norm1_gain, norm1_shift, in_weight[0].transpose(1, 0, 2), out_weight],
+        [row_b16, shape((owned, 4 * width), B16)],
+        away=range(5),
+    )
     io_ring = RingGather("io", meta, io_shard)
-    (normed,) = call(norm_first_kernel, "norm_first", [tokens, norm1_gain, norm1_shift], [row_b16])
     x_one = gather_four(normed)
     twist, table = transform_tables(blocks, group)
     hi, lo = split_table(table)
     grid, ramp = feature_table(seq_len, feat_weight.shape[1])
     twist, grid, ramp = jnp.asarray(twist), jnp.asarray(grid), jnp.asarray(ramp)
-    rates = jnp.asarray(decay_rates(model).T)
-    cols, up_block, chans, columns, small_col, small_row = call(
+    params = [
+        cotangent, up_weight, down_weight,
+        short_taps.transpose(1, 2, 0, 3), short_bias.transpose(1, 0, 2), in_bias.transpose(1, 0, 2), up_bias, skip_gain,
+        jnp.asarray(decay_rates(model).T), kernel_weight, feat_weight.transpose(1, 0, 2),
+        feat_bias, inner_bias, deep_bias, sine_freq,
+    ]
+    top_rows, ud_shard, cols, up_block, chans, columns, small_col, small_row, feat = call(
         setup_kernel,
         "setup",
+        [meta, lengths, *params],
         [
-            meta, short_taps, short_bias, in_bias, up_bias, skip_gain, rates, kernel_weight,
-            feat_bias, inner_bias, deep_bias, sine_freq,
+            row_b16, shape((2, owned, hidden), B16),
+            shape((width, 16), F32), shape((1, hidden), F32), shape((chan, 2), F32), shape((filt, chan), F32),
+            shape((filt, 4), F32), shape((4, filt), F32), shape(feat_weight.shape[1:], F32),
         ],
-        [
-            shape((width, 16), F32), shape((1, hidden), F32), shape((chan, 2), F32), shape((filt, chan), F32),
-            shape((filt, 4), F32), shape((4, filt), F32),
-        ],
-    )
-    (ud_shard,) = call(pack_ud_kernel, "pack_ud", [up_weight, down_weight], [shape((2, owned, hidden), B16)])
-    (top_rows,) = call(top_kernel, "top", [meta, lengths, cotangent], [row_b16])
-    io_ring.step(cols, ud_shard, top_rows)
-    nets = (feat_weight, inner_weight, deep_weight)
+        scratch=[pltpu.SemaphoreType.DMA((2,))],
+        away=[2] + list(range(5, 2 + len(params))),
+        raw=[3, 4, -2],
+    )
+    io_ring.step(x_one[1])
+    tables = [grid, ramp, inner_weight, deep_weight, twist, hi, lo]
     kern_spec, sines, cosines = call(
         filter_ahead_kernel,
         "filter_ahead",
-        [grid, ramp, chans, *nets, tie(small_col, io_ring.pieces[-1]), columns, twist, hi, lo],
+        [chans, feat, tie(small_col, io_ring.pieces[-1]), columns, *tables],
         [
             shape((blocks * chan, 2 * group), F32),
             shape((3, filt, seq_len), F32),
             shape((3, filt, seq_len), F32),
         ],
         scratch=[pltpu.VMEM((blocks * chan, 2 * group), F32)],
-    )
-    io_ring.step(kern_spec)
+        away=range(4, 4 + len(tables)),
+    )
+    io_ring.step(kern_spec, x_one[2])
 
     edge = shape((HALO, model), B16)
     last, first = call(edges_kernel, "edges", [meta, *x_one], [edge, edge])
     before = lax.ppermute(last, "seq", [(i, (i + 1) % 8) for i in range(8)])
     after = lax.ppermute(first, "seq", [(i, (i + 7) % 8) for i in range(8)])
     io_ring.step()
-    full_io = io_ring.full().reshape(model, 4 * width)
-    ud_ring = RingGather("ud", meta, tie(ud_shard, full_io))
+    io_pieces = io_ring.pieces + list(tie(io_ring.came, before, after))
+    ud_ring = RingGather("ud", meta, tie(ud_shard, io_pieces[-1]))
     g_top = gather_four(tie(top_rows, x_one[3]))
-    proj, halo, gated = call(
+    full_io, proj, halo, gated = call(
         project_kernel,
         "project",
-        [meta, lengths, *x_one, before, after, full_io, cols],
-        [shape((3, width, group), B16), shape((3, width, 2 * LANE), B16), flat_shape],
-    )
+        [meta, lengths, *x_one, before, after, cols, *io_pieces],
+        [
+            shape((8, owned, 4 * width), B16), shape((3, width, group), B16), shape((3, width, 2 * LANE), B16), flat_shape
+        ],
+    )
+    full_io = full_io.reshape(model, 4 * width)
     common = [proj, halo, cols]
 
-    received = lax.all_to_all(gated.reshape(8, chan, group), "seq", 0, 0, tiled=True)
+    spread = (8, chan, group)
+    received = exchange(gated.reshape(spread))
     ud_ring.step(received)
     spec_rows = 2 * blocks * chan
-    mixed_chan, kept_spec = call(
+    mixed, kept_spec = call(
         conv_ahead_kernel,
         "conv_ahead",
-        [received, kern_spec, twist, hi, lo, chans],
-        [shape(received.shape, B16), shape((spec_rows, 2 * group), F32)],
+        [kern_spec, twist, hi, lo, chans, received],
+        [shape(spread, B16), shape((spec_rows, 2 * group), F32)],
         scratch=[pltpu.VMEM((spec_rows, 2 * group), F32)],
     )
-    mixed = lax.all_to_all(mixed_chan, "seq", 0, 0, tiled=True).reshape(width, group)
+    mixed = exchange(mixed).reshape(width, group)
     ud_ring.step(mixed)
 
     y_tok, give3, give1, keep2, keep0 = call(
         out_project_kernel,
         "out_project",
-        [meta, lengths, *common, mixed, full_io],
+        [meta, lengths, *common, full_io, mixed],
         [shape((4, tok_rows, width), B16)] + sums_shapes,
     )
     near, far, _ = pass_far(give3, give1, keep2)
@@ -1708,88 +1831,80 @@
 
     tall = shape((group, hidden), B16)
     act, gpre, gup = call(
-        mlp_kernel, "mlp", [*x_two, *g_top, full_ud, up_block], [tall, tall, shape((1, hidden), F32)]
+        mlp_kernel, "mlp", [*x_two, *g_top, full_ud, up_block], [tall, tall, shape((1, hidden), F32)],
     )
     give3, give1, keep2, keep0 = call(partial(rows_kernel, 0), "grad_two", [gpre, full_ud], sums_shapes)
     near, far, passed = pass_far(give3, give1, keep2)
-    one_way = shape((owned, hidden), B16)
-    mlp_terms, left, right = call(
+    give = shape((2, 2, owned, hidden), B16)
+    mlp_terms, ga, gb = call(
         mlp_grad_kernel,
         "mlp_grad",
         [meta, *x_two, *g_top, act, tie(gpre, passed)],
-        [shape((8, 2, owned, hidden), B16), one_way, one_way],
-    )
-
-    def ring_send(left, right):
-        return lax.ppermute(left, "seq", AHEAD), lax.ppermute(right, "seq", BACK)
-
-    def ring_add(step, came, *others):
-        left, right = tie(came, *others)
-        out = shape((owned, hidden), F32 if step == 8 else B16)
-        return call(
-            partial(ring_add_kernel, step), "ring_add_%d" % step, [meta, mlp_terms, left, right], [out, out]
-        )
-
-    ring = ring_send(left, right)
+        [shape((2, 2, 2, 2 * owned, hidden), B16), give, give],
+    )
+    wide_back = Halving("far", meta, mlp_terms, (ga, gb))
     grad_middle, gx, norm_sums = call(
         norm_second_back_kernel,
         "norm_second_back",
-        [meta, lengths, keep0, near, tie(far, left), middle, cotangent, norm2_gain],
+        [meta, lengths, keep0, near, tie(far, ga), middle, cotangent, norm2_gain],
         [row_f32, row_b16, shape((8, model), F32)],
     )
     g_mid = gather_four(gx)
     m3, m1, m2, m0 = call(partial(rows_kernel, 1), "mlp_rows", [tie(act, gx), full_ud], sums_shapes)
-    ring = ring_send(*ring_add(2, ring, g_mid[2], m3))
-    gy, gmix, gate_first = call(
+    gy, gate_first, gmix = call(
         grad_gate_kernel,
         "grad_gate",
         [meta, lengths, *tie(tuple(g_mid), m3), full_io, *common, mixed],
-        [flat_shape, flat_shape, shape((width, LANE), F32)],
-    )
-
-    grads_chan = lax.all_to_all(gmix.reshape(8, chan, group), "seq", 0, 0, tiled=True)
-    gate_next = lax.ppermute(gate_first, "seq", [(i, (i + 7) % 8) for i in range(8)])
-    m_near, m_far, _ = pass_far(tie(m3, gmix), m1, m2)
-    ring = ring_send(*ring_add(3, ring, grads_chan))
-    ggated_chan, grad_kernel = call(
+        [flat_shape, shape((width, LANE), F32), flat_shape],
+    )
+
+    received = exchange(gmix.reshape(spread))
+    given = wide_back.one(received)
+    gate_next = lax.ppermute(tie(gate_first, received), "seq", [(i, (i + 7) % 8) for i in range(8)])
+    ggated, grad_kernel = call(
         conv_back_kernel,
         "conv_back",
-        [grads_chan, kept_spec, kern_spec, twist, hi, lo, chans],
-        [shape((8, chan, group + LANE), B16), shape((blocks, chan, group), F32)],
+        [kept_spec, kern_spec, twist, hi, lo, chans, tie(received, given)],
+        [shape(spread, B16), shape((blocks, chan, group), F32)],
         scratch=[pltpu.VMEM((spec_rows, 2 * group), F32), pltpu.VMEM((3 * spec_rows // 2, 2 * group), F32)],
     )
-    out_cube = (2, 2, 2, owned, width)
-    give = shape((2, 2, owned // 2, width), B16)
-    out_terms, ga, gb = call(
-        weight_grad_kernel,
-        "grad_out",
-        [meta, *tie(tuple(g_mid), grads_chan), y_tok],
-        [shape(out_cube, B16), give, give],
-    )
-    ring = ring_send(*ring_add(4, ring, ggated_chan))
-    ggated = lax.all_to_all(ggated_chan, "seq", 0, 0, tiled=True).reshape(width, group + LANE)
-    out_back = Halving("grad_out", meta, out_terms, (ga, gb), (1, owned, width))
-    ring = ring_send(*ring_add(5, ring, ggated))
-    gproj_tok, col_sums, norm_one, give3, give1, keep2, keep0 = call(
+    ggated = exchange(tie(ggated, gate_next)).reshape(width, group)
+    given = wide_back.two(ggated)
+    (heads,) = call(heads_kernel, "heads", [tie(ggated, given)], [shape((width, LANE), B16)])
+    ggated_next = lax.ppermute(heads, "seq", [(i, (i + 7) % 8) for i in range(8)])
+    tok_first, sum_first, part_first = call(
+        grad_first_kernel,
+        "grad_first",
+        [meta, lengths, *common, mixed, gy, tie(gate_next, heads), full_io],
+        [shape((4, tok_rows, width), B16), shape((8, width), F32), shape((group, model), F32)],
+    )
+    cube = shape((2, 2, 2, owned, 2 * width), B16)
+    give = shape((2, 2, owned // 2, 2 * width), B16)
+    early_terms, ga, gb = call(
+        grad_early_kernel,
+        "grad_early",
+        [meta, *g_mid, y_tok, *x_one, tok_first],
+        [cube, give, give],
+    )
+    early = Halving("early", meta, early_terms, (ga, gb))
+    tok_rest, col_sums, norm_one, give3, give1, keep2, keep0 = call(
         grad_short_kernel,
         "grad_short",
-        [meta, lengths, *common, mixed, gy, ggated, gate_next, full_io, *x_one, norm1_gain, norm1_shift],
-        [shape((4, tok_rows, 3 * width), B16), shape((16, width), F32), shape((2, model), F32)] + sums_shapes,
+        [meta, lengths, *common, gy, full_io, part_first, *x_one, norm1_gain, norm1_shift, tie(ggated, ga), ggated_next],
+        [shape((4, tok_rows, 2 * width), B16), shape((16, width), F32), shape((2, model), F32)] + sums_shapes,
     )
     near, far, passed = pass_far(give3, give1, keep2)
-    give = shape((2, 2, owned // 2, 3 * width), B16)
-    in_terms, ga, gb = call(
-        weight_grad_kernel,
-        "grad_in",
-        [meta, *x_one, gproj_tok],
-        [shape((2, 2, 2, owned, 3 * width), B16), give, give],
-    )
-    in_back = Halving("grad_in", meta, in_terms, (ga, gb), (1, owned, 3, width))
+    late_terms, ga, gb = call(
+        grad_late_kernel, "grad_late", [meta, *tie(tuple(x_one), passed), tok_rest], [cube, give, give]
+    )
+    late = Halving("late", meta, late_terms, (ga, gb))
+    given = early.one(ga)
     side, wide = call(
         filter_back_kernel,
         "filter_back",
         [
-            meta, tie(grad_kernel, ga), grid, ramp, chans, *nets, small_col, small_row, columns, sines, cosines
+            meta, tie(grad_kernel, given), grid, ramp, chans, feat, inner_weight, deep_weight, small_col, small_row, columns,
+            sines, cosines
         ],
         [shape((filt, 4 * filt), F32), shape((filt, width), F32)],
     )
@@ -1797,42 +1912,48 @@
     (small,) = call(
         pack_small_kernel,
         "pack_small",
-        [side, wide, col_sums, gup, norm_one, norm_sums],
+        [side, wide, sum_first, col_sums, gup, norm_one, norm_sums],
         [shape((2 * HALF, width), F32)],
     )
     came = swap(small, "seq", 1)
+    m_near, m_far, m_passed = pass_far(tie(m3, small), m1, m2)
     (grad_tokens,) = call(
-        norm_first_back_kernel, "norm_first_back", [keep0, near, tie(far, small), tokens, grad_middle, norm1_gain], [row_f32]
-    )
+        norm_first_back_kernel,
+        "norm_first_back",
+        [keep0, near, tie(far, small), tokens, grad_middle, norm1_gain],
+        [row_f32],
+    )
+    given = late.one(grad_tokens, m_passed)
+    (small,) = call(add_small_kernel, "add_small", [small, tie(came, given)], [small])
+    came = swap(small, "seq", 2)
+    given = early.two(small)
+    result = shape((1, owned, hidden), F32)
+    grad_up, grad_down = call(far_last_kernel, "far_last", wide_back.last(given), [result, result])
+    given = late.two(grad_up)
+    (small,) = call(add_small_kernel, "add_small", [small, tie(came, given)], [small])
+    came = swap(small, "seq", 4)
     (layer_out,) = call(layer_out_kernel, "layer_out", [m0, m_near, tie(m_far, small), middle, down_bias], [row_b16])
-    ring = ring_send(*ring_add(6, ring, small))
-    out_back.step(small)
-    (small,) = call(add_small_kernel, "add_small", [small, came], [small])
-    came = swap(small, "seq", 2)
-    in_back.step(small)
-    ring = ring_send(*ring_add(7, ring, small))
-    (small,) = call(add_small_kernel, "add_small", [small, came], [small])
-    came = swap(small, "seq", 4)
-    out_back.step(small)
-    (small,) = call(add_small_kernel, "add_small", [small, came], [small])
+    grad_out, first_in = call(
+        early_last_kernel, "early_last", early.last(layer_out), [shape((1, owned, width), F32), shape((owned, width), F32)]
+    )
+    (small,) = call(add_small_kernel, "add_small", [small, tie(came, grad_out)], [small])
     came = swap(small, "rep", 2)
-    in_back.step(small)
-    grad_up, grad_down = ring_add(8, ring, small)
     (small,) = call(
         list_small_kernel, "list_small", [meta, small, came], [shape((3 * HALF, width), F32)]
     )
     came = swap(small, "rep", 1)
-    grad_out = out_back.step(small)
-    grad_in = in_back.step(small)
+    (grad_in,) = call(
+        late_last_kernel, "late_last", [*late.last(small), first_in], [shape((1, 3, owned, width), F32)]
+    )
     vector = shape((1, model), F32)
     square, short = shape((1, filt, filt), F32), shape((1, filt), F32)
-    triple = shape((1, 3, model), F32)
+    triple = shape((3, 1, model), F32)
     outs = call(
         unpack_small_kernel,
         "unpack_small",
         [meta, small, came],
         [
-            triple, shape((1, 3, 3, model), F32), triple, shape(feat_weight.shape, F32), short, square, short, square,
+            triple, shape((3, 3, 1, model), F32), triple, shape(params[10].shape, F32), short, square, short, square,
             short, short, shape(kernel_weight.shape, F32), vector, vector, vector, vector, vector, vector,
             shape(up_bias.shape, F32), vector,
         ],
@@ -1840,13 +1961,17 @@
     return (
         layer_out,
         grad_tokens,
-        grad_in,
-        *outs[:12],
+        grad_in.transpose(0, 2, 1, 3),
+        outs[0].transpose(1, 0, 2),
+        outs[1].transpose(2, 0, 1, 3),
+        outs[2].transpose(1, 0, 2),
+        outs[3].transpose(1, 0, 2),
+        *outs[4:12],
         grad_out,
         *outs[12:17],
-        grad_up[None],
+        grad_up,
         outs[17],
-        grad_down[None],
+        grad_down,
         outs[18],
     )
 

time: 327 us -> 294 us (0.90)
  local copies, waits for them, and re-layouts: 52.2 us -> 16.7 us
  blocking collectives: 24.3 us -> 46.5 us
  starting transfers between devices: 93.2 us -> 77.4 us
  Pallas kernels: 72.2 us -> 64.7 us
  waiting for transfers between devices: 79.2 us -> 84.2 us
    unnamed x242 -> x212, local copies, waits for them, and re-layouts: 51.5 us -> 16 us
    all_to_all x2 -> x3, blocking collectives: 24.3 us -> 46.5 us  [exchange(): return lax.all_to_all(blocks, 'seq', 0, 0, tiled=True)]
    ppermute x15 -> x2, starting transfers between devices: 32.9 us -> 14.5 us  [the longest x1 12.8 us: per_device_fast(): lax.ppermute(tie(gate_first, received), 'seq', [(i, (i + 7) % 8) for i in...]
    ppermute x41 -> x47, waiting for transfers between devices: 46.9 us -> 64.8 us  [swap(): return lax.ppermute(values, axis_name, [(i, i ^ bit) for i in range(size)])]
    ppermute x15 -> x2, waiting for transfers between devices: 15 us -> 0.01 us  [the longest x1 0.01 us: per_device_fast(): lax.ppermute(heads, 'seq', [(i, (i + 7) % 8) for i in range(8)])]
    ppermute x41 -> x47, starting transfers between devices: 27.6 us -> 36.1 us  [swap(): return lax.ppermute(values, axis_name, [(i, i ^ bit) for i in range(size)])]
    all_to_all x2 -> x1, waiting for transfers between devices: 0.01 us -> 8.25 us  [exchange(): return lax.all_to_all(blocks, 'seq', 0, 0, tiled=True)]
    pallas_call x51 -> x45, Pallas kernels: 72.2 us -> 64.7 us  [call(): pl.pallas_call(body, out_shape=outs, in_specs=[space(i, a) for i, a in en...]
  transfers between devices with their start and end apart: 76 -> 68, of which waited for: 30 -> 28; matrix products, arithmetic and copies ran while one was open for 1% -> 0% of each run, Pallas kernels for 20% -> 17%
where the time goes in v4:
time: 294 us; the launch traced here: 292 us
  waiting for transfers between devices  84.2 us (29%)
  starting transfers between devices  77.4 us (26%)
  Pallas kernels  64.7 us (22%)
  blocking collectives  46.5 us (16%)
  local copies, waits for them, and re-layouts  16.7 us (6%)
    ppermute x47, waiting for transfers between devices, swap(): return lax.ppermute(values, axis_name, [(i, i ^ bit) for i in range(size)])  64.8 us
    pallas_call x45, Pallas kernels, call(): pl.pallas_call(body, out_shape=outs, in_specs=[space(i, a) for i, a in en...  64.7 us
    all_to_all x3, blocking collectives, exchange(): return lax.all_to_all(blocks, 'seq', 0, 0, tiled=True)  46.5 us
    ppermute x47, starting transfers between devices, swap(): return lax.ppermute(values, axis_name, [(i, i ^ bit) for i in range(size)])  36.1 us
    unnamed x212, local copies, waits for them, and re-layouts  16 us
    ppermute x8, starting transfers between devices, send(): lax.ppermute(right, 'seq', BACK)  13.3 us
    ppermute x1, starting transfers between devices, per_device_fast(): lax.ppermute(tie(gate_first, received), 'seq', [(i, (i + 7) % 8) for i in...  12.8 us
    all_to_all x1, waiting for transfers between devices, exchange(): return lax.all_to_all(blocks, 'seq', 0, 0, tiled=True)  8.25 us
  transfers between devices with their start and end apart: 68, of which 28 were waited for; matrix products, arithmetic and copies ran while one was open for 0% of the time, Pallas kernels for 17%

profile of v4, /device:TPU:0, one launch (start us, length us, event | category | flops | bytes accessed | tf_op | source)
XLA Modules:
  0.0 291.8 jit_solution(10569426224255952913)
XLA Ops:
  5.6 3.0 %collective-permute-start.6 = (bf16[128,1024]{1,0:T(8,128)(2,1)S(1)}, bf16[128,1024]{1,0:T(8,128)(2,1)S(1)}, u32[]{:S(2)}, u32[]{:S(2)}) collective-permute-start(bf16[128,1024]{1,0:T(8,128)(2,1)S(1)} %get-tuple-element.210.refs_9_), channel_id=1, source_target_pairs={{8,0},{16,8},{24,16},{28,24},{20,28},{12,20},{4,12},{0,4},{9,1},{1... | collective-permute-start | bytes 786440 | tf_op jit(solution)/shard_map/ppermute | solution.py:1617
  18.5 5.0 %filter_ahead.1 = (f32[128,1024]{1,0:T(8,128)S(1)}, f32[3,64,2048]{2,1,0:T(8,128)S(1)}, f32[3,64,2048]{2,1,0:T(8,128)S(1)}) custom-call(f32[32,2]{1,0:T(8,128)S(1)} %get-tuple-element.213.refs_0_.refs_4_.refs_5_, f32[33,64]{1,0:T(8,128)S(1)} %get-tuple-element.214.refs_1_.refs_5_, f32[64,4]{1,0:T(8,128)S(1)} %get-tuple-element.216.refs_2_.refs_8_, ...), custom_call_target="tpu_custom_call" | custom-call | flops 6000000000 | bytes 100000 | tf_op jit(solution)/shard_map/filter_ahead/pallas_call | solution.py:959
  26.8 4.3 %collective-permute-done.9.refs_0_.refs_14_ = bf16[128,1024]{1,0:T(8,128)(2,1)S(1)} collective-permute-done((bf16[128,1024]{1,0:T(8,128)(2,1)S(1)}, bf16[128,1024]{1,0:T(8,128)(2,1)S(1)}, u32[]{:S(2)}, u32[]{:S(2)}) %collective-permute-start.9) | collective-permute-done | bytes 262176 | tf_op jit(solution)/shard_map/ppermute | solution.py:1617
  36.0 3.3 %collective-permute-start.4 = (bf16[16,1024]{1,0:T(8,128)(2,1)S(1)}, bf16[16,1024]{1,0:T(8,128)(2,1)S(1)}, u32[]{:S(2)}, u32[]{:S(2)}) collective-permute-start(bf16[16,1024]{1,0:T(8,128)(2,1)S(1)} %get-tuple-element.208), channel_id=1, source_target_pairs={{0,28},{4,0},{8,4},{12,8},{16,12},{20,16},{24,20},{28,24},{1,29},{... | collective-permute-start | bytes 98312 | tf_op jit(solution)/shard_map/ppermute | solution.py:1785
  46.1 3.4 %project.1 = (bf16[8,128,1024]{2,1,0:T(8,128)(2,1)S(1)}, bf16[3,256,512]{2,1,0:T(8,128)(2,1)S(1)}, bf16[3,256,256]{2,1,0:T(8,128)(2,1)S(1)}, bf16[256,512]{1,0:T(8,128)(2,1)S(1)}) custom-call(s32[34]{0:T(128)S(1)} %dynamic-slice_bitcast_fusion.refs_0_, s32[2]{0:T(128)S(1)} %copy-done.72, ...), custom_call_target="tpu_custom_call" | custom-call | flops 1000000 | bytes 100000 | tf_op jit(solution)/shard_map/project/pallas_call | solution.py:959
  49.5 16.2 %all_to_all.20.refs_5_ = bf16[8,32,512]{2,1,0:T(8,128)(2,1)S(1)} all-to-all(bf16[8,32,512]{2,1,0:T(8,128)(2,1)S(1)} %bitcast.26), channel_id=1, replica_groups=mesh['seq'=8,'rep'=4] {'seq'}, dimensions={0} | all-to-all | bytes 524288 | tf_op jit(solution)/shard_map/all_to_all | solution.py:1688
  68.0 4.0 %conv_ahead.1 = (bf16[8,32,512]{2,1,0:T(8,128)(2,1)S(1)}, f32[256,1024]{1,0:T(8,128)S(1)}) custom-call(f32[128,1024]{1,0:T(8,128)S(1)} %get-tuple-element.218.refs_0_.refs_1_, f32[4,4,2,512]{3,2,1,0:T(2,128)S(1)} %copy-done.42, bf16[1024,1024]{1,0:T(8,128)(2,1)S(1)} %copy-done.1, bf16[1024,1024]{1,0:T(8,128)(2,1)S(1)} %copy-done, ...), custom_call_target="tpu_custom_call" | custom-call | flops 1000000 | bytes 100000 | tf_op jit(solution)/shard_map/conv_ahead/pallas_call | solution.py:959
  71.9 10.6 %all_to_all.21 = bf16[8,32,512]{2,1,0:T(8,128)(2,1)S(1)} all-to-all(bf16[8,32,512]{2,1,0:T(8,128)(2,1)S(1)} %get-tuple-element.231), channel_id=1, replica_groups=mesh['seq'=8,'rep'=4] {'seq'}, dimensions={0} | all-to-all | bytes 524288 | tf_op jit(solution)/shard_map/all_to_all | solution.py:1688
  84.4 2.0 collective-permute-start.27
  88.5 7.1 %collective-permute-done.15.refs_3_ = bf16[128,1024]{1,0:T(8,128)(2,1)S(1)} collective-permute-done((bf16[128,1024]{1,0:T(8,128)(2,1)S(1)}, bf16[128,1024]{1,0:T(8,128)(2,1)S(1)}, u32[]{:S(2)}, u32[]{:S(2)}) %collective-permute-start.15) | collective-permute-done | bytes 262176 | tf_op jit(solution)/shard_map/ppermute | solution.py:23
  101.3 5.1 %collective-permute-done.17.refs_2_.refs_3_ = bf16[128,1024]{1,0:T(8,128)(2,1)S(1)} collective-permute-done((bf16[128,1024]{1,0:T(8,128)(2,1)S(1)}, bf16[128,1024]{1,0:T(8,128)(2,1)S(1)}, u32[]{:S(2)}, u32[]{:S(2)}) %collective-permute-start.17) | collective-permute-done | bytes 262176 | tf_op jit(solution)/shard_map/ppermute | solution.py:23
  108.4 3.1 %mlp.1 = (bf16[512,1024]{1,0:T(8,128)(2,1)S(1)}, bf16[512,1024]{1,0:T(8,128)(2,1)S(1)}, f32[1,1024]{1,0:T(1,128)S(1)}) custom-call(bf16[128,1024]{1,0:T(8,128)(2,1)S(1)} %get-tuple-element.236.refs_0_.refs_1_, bf16[128,1024]{1,0:T(8,128)(2,1)S(1)} %collective-permute-done.16.refs_1_.refs_2_, bf16[128,1024]{1,0:T(8,128)(2,1)S(1)} %collective-permute-done.17.refs_2_.refs_3_, ...), custom_call_target="tpu_custom_call" | custom-call | flops 1000000 | bytes 100000 | tf_op jit(solution)/shard_map/mlp/pallas_call | solution.py:959
  116.0 3.4 %mlp_grad.1 = (bf16[2,2,2,256,1024]{4,3,2,1,0:T(8,128)(2,1)S(1)}, bf16[2,2,128,1024]{3,2,1,0:T(8,128)(2,1)S(1)}, bf16[2,2,128,1024]{3,2,1,0:T(8,128)(2,1)S(1)}) custom-call(s32[34]{0:T(128)S(1)} %dynamic-slice_bitcast_fusion.refs_0_, bf16[128,1024]{1,0:T(8,128)(2,1)S(1)} %get-tuple-element.236.refs_0_.refs_1_, ...), custom_call_target="tpu_custom_call" | custom-call | flops 1000000 | bytes 100000 | tf_op jit(solution)/shard_map/mlp_grad/pallas_call | solution.py:959
  119.4 3.4 %collective-permute-done.32.refs_4_ = bf16[128,1024]{1,0:T(8,128)(2,1)S(1)} collective-permute-done((bf16[128,1024]{1,0:T(8,128)(2,1)S(1)}, bf16[128,1024]{1,0:T(8,128)(2,1)S(1)}, u32[]{:S(2)}, u32[]{:S(2)}) %collective-permute-start.32) | collective-permute-done | bytes 262176 | tf_op jit(solution)/shard_map/ppermute | solution.py:23
  128.4 3.8 %collective-permute-done.35.refs_4_.refs_3_ = bf16[128,1024]{1,0:T(8,128)(2,1)S(1)} collective-permute-done((bf16[128,1024]{1,0:T(8,128)(2,1)S(1)}, bf16[128,1024]{1,0:T(8,128)(2,1)S(1)}, u32[]{:S(2)}, u32[]{:S(2)}) %collective-permute-start.35) | collective-permute-done | bytes 262176 | tf_op jit(solution)/shard_map/ppermute | solution.py:23
  135.5 19.7 %all_to_all.22.refs_6_ = bf16[8,32,512]{2,1,0:T(8,128)(2,1)S(1)} all-to-all(bf16[8,32,512]{2,1,0:T(8,128)(2,1)S(1)} %bitcast.27), channel_id=1, replica_groups=mesh['seq'=8,'rep'=4] {'seq'}, dimensions={0} | all-to-all | bytes 524288 | tf_op jit(solution)/shard_map/all_to_all | solution.py:1688
  155.2 12.8 %collective-permute-start.39 = (f32[256,128]{1,0:T(8,128)S(1)}, f32[256,128]{1,0:T(8,128)S(1)}, u32[]{:S(2)}, u32[]{:S(2)}) collective-permute-start(f32[256,128]{1,0:T(8,128)S(1)} %get-tuple-element.284), channel_id=1, source_target_pairs={{0,28},{4,0},{8,4},{12,8},{16,12},{20,16},{24,20},{28,24},{1,29},{... | collective-permute-start | bytes 393224 | tf_op jit(solution)/shard_map/ppermute | solution.py:1863
  172.1 4.9 %conv_back.1 = (bf16[8,32,512]{2,1,0:T(8,128)(2,1)S(1)}, f32[4,32,512]{2,1,0:T(8,128)S(1)}) custom-call(f32[256,1024]{1,0:T(8,128)S(1)} %get-tuple-element.268.refs_0_, f32[128,1024]{1,0:T(8,128)S(1)} %get-tuple-element.218.refs_0_.refs_1_, f32[4,4,2,512]{3,2,1,0:T(2,128)S(1)} %copy-done.42, bf16[1024,1024]{1,0:T(8,128)(2,1)S(1)} %copy-done.1, ...), custom_call_target="tpu_custom_call" | custom-call | flops 1000000 | bytes 100000 | tf_op jit(solution)/shard_map/conv_back/pallas_call | solution.py:959
  179.1 4.0 %all-to-all-start.3 = ((bf16[8,32,512]{2,1,0:T(8,128)(2,1)}), bf16[8,32,512]{2,1,0:T(8,128)(2,1)}, u32[]{:S(2)}, u32[]{:S(2)}) async-start(bf16[8,32,512]{2,1,0:T(8,128)(2,1)} %copy-done.53), calls=%async_computation.3 | async-start | bytes 524288 | tf_op jit(solution)/shard_map/all_to_all | solution.py:1688
  183.2 8.3 %all-to-all-done.3 = bf16[8,32,512]{2,1,0:T(8,128)(2,1)} async-done(((bf16[8,32,512]{2,1,0:T(8,128)(2,1)}), bf16[8,32,512]{2,1,0:T(8,128)(2,1)}, u32[]{:S(2)}, u32[]{:S(2)}) %all-to-all-start.3) | async-done | bytes 262176 | tf_op jit(solution)/shard_map/all_to_all | solution.py:1688
  198.1 2.7 grad_first.1
  202.5 5.6 %grad_short.1 = (bf16[4,128,512]{2,1,0:T(8,128)(2,1)S(1)}, f32[16,256]{1,0:T(8,128)S(1)}, f32[2,1024]{1,0:T(2,128)S(1)}, bf16[128,1024]{1,0:T(8,128)(2,1)S(1)}, ...) custom-call(s32[34]{0:T(128)S(1)} %dynamic-slice_bitcast_fusion.refs_0_, ...), custom_call_target="tpu_custom_call" | custom-call | flops 1000000 | bytes 100000 | tf_op jit(solution)/shard_map/grad_short/pallas_call | solution.py:959
  213.9 3.4 %collective-permute-done.43.refs_3_ = bf16[2,2,64,512]{3,2,1,0:T(8,128)(2,1)S(1)} collective-permute-done((bf16[2,2,64,512]{3,2,1,0:T(8,128)(2,1)S(1)}, bf16[2,2,64,512]{3,2,1,0:T(8,128)(2,1)S(1)}, u32[]{:S(2)}, u32[]{:S(2)}) %collective-permute-start.43) | collective-permute-done | bytes 262176 | tf_op jit(solution)/shard_map/ppermute | solution.py:23
  218.7 6.1 %filter_back.1 = (f32[64,256]{1,0:T(8,128)S(1)}, f32[64,256]{1,0:T(8,128)S(1)}) custom-call(s32[34]{0:T(128)S(1)} %dynamic-slice_bitcast_fusion.refs_0_, f32[4,32,512]{2,1,0:T(8,128)S(1)} %copy-done.50, f32[33,2048]{1,0:T(8,128)S(1)} %copy-done.41, f32[1,2048]{1,0:T(1,128)S(1)} %copy-done.76, f32[32,2]{1,0:T(8,128)S(1)} %copy-done.57, ...), custom_call_target="tpu_custom_call" | custom-call | flops 1000000 | bytes 100000 | tf_op jit(solution)/shard_map/filter_back/pallas_call | solution.py:959
  237.1 9.3 %collective-permute-done.57.refs_3_ = bf16[128,1024]{1,0:T(8,128)(2,1)S(1)} collective-permute-done((bf16[128,1024]{1,0:T(8,128)(2,1)S(1)}, bf16[128,1024]{1,0:T(8,128)(2,1)S(1)}, u32[]{:S(2)}, u32[]{:S(2)}) %collective-permute-start.57) | collective-permute-done | bytes 262176 | tf_op jit(solution)/shard_map/ppermute | solution.py:23
  246.7 4.8 %collective-permute-done.56.refs_2_ = bf16[128,1024]{1,0:T(8,128)(2,1)S(1)} collective-permute-done((bf16[128,1024]{1,0:T(8,128)(2,1)S(1)}, bf16[128,1024]{1,0:T(8,128)(2,1)S(1)}, u32[]{:S(2)}, u32[]{:S(2)}) %collective-permute-start.56) | collective-permute-done | bytes 262176 | tf_op jit(solution)/shard_map/ppermute | solution.py:23
  257.9 2.2 collective-permute-start.64
  261.7 10.4 %collective-permute-done.64.refs_3_ = bf16[64,512]{1,0:T(8,128)(2,1)S(1)} collective-permute-done((bf16[64,512]{1,0:T(8,128)(2,1)S(1)}, bf16[64,512]{1,0:T(8,128)(2,1)S(1)}, u32[]{:S(2)}, u32[]{:S(2)}) %collective-permute-start.64) | collective-permute-done | bytes 65568 | tf_op jit(solution)/shard_map/ppermute | solution.py:23
  273.5 2.3 collective-permute-start.65
  275.8 4.7 %collective-permute-done.65.refs_2_ = f32[176,256]{1,0:T(8,128)S(1)} collective-permute-done((f32[176,256]{1,0:T(8,128)S(1)}, f32[176,256]{1,0:T(8,128)S(1)}, u32[]{:S(2)}, u32[]{:S(2)}) %collective-permute-start.65) | collective-permute-done | bytes 180256 | tf_op jit(solution)/shard_map/ppermute | solution.py:23
  281.2 2.9 collective-permute-start.60
  284.1 4.3 %collective-permute-done.61.refs_3_ = bf16[64,512]{1,0:T(8,128)(2,1)S(1)} collective-permute-done((bf16[64,512]{1,0:T(8,128)(2,1)S(1)}, bf16[64,512]{1,0:T(8,128)(2,1)S(1)}, u32[]{:S(2)}, u32[]{:S(2)}) %collective-permute-start.61) | collective-permute-done | bytes 65568 | tf_op jit(solution)/shard_map/ppermute | solution.py:23
  (365 shorter events, 103.5 us)
Async XLA Ops:
  5.6 9.4 %collective-permute-start.6 = (bf16[128,1024]{1,0:T(8,128)(2,1)S(1)}, bf16[128,1024]{1,0:T(8,128)(2,1)S(1)}, u32[]{:S(2)}, u32[]{:S(2)}) collective-permute-start(bf16[128,1024]{1,0:T(8,128)(2,1)S(1)} %get-tuple-element.210.refs_9_), channel_id=1, source_target_pairs={{8,0},{16,8},{24,16},{28,24},{20,28},{12,20},{4,12},{0,4},{9,1},{1... | collective-permute-start | bytes 786440 | tf_op jit(solution)/shard_map/ppermute | solution.py:1617
  8.8 16.0 %collective-permute-start.1 = (bf16[128,1024]{1,0:T(8,128)(2,1)S(1)}, bf16[128,1024]{1,0:T(8,128)(2,1)S(1)}, u32[]{:S(2)}, u32[]{:S(2)}) collective-permute-start(bf16[128,1024]{1,0:T(8,128)(2,1)S(1)} %get-tuple-element.303.refs_1_.refs_2_.refs_6_.refs_8_), channel_id=1, source_target_pairs={{0,2},{1,3},{2,0},{3,1},{4,6},{5,7},{6,4},{7,5},{8,10},{9,11},{10,... | collective-permute-start | bytes 786440 | tf_op jit(solution)/shard_map/ppermute | solution.py:23
  31.7 9.5 %collective-permute-start.11 = (bf16[64,1024]{1,0:T(8,128)(2,1)S(1)}, bf16[64,1024]{1,0:T(8,128)(2,1)S(1)}, u32[]{:S(2)}, u32[]{:S(2)}) collective-permute-start(bf16[64,1024]{1,0:T(8,128)(2,1)S(1)} %get-tuple-element.223), channel_id=1, source_target_pairs={{0,8},{8,16},{16,24},{24,28},{28,20},{20,12},{12,4},{4,0},{1,9},{9... | collective-permute-start | bytes 393224 | tf_op jit(solution)/shard_map/ppermute | solution.py:1617
  41.2 24.5 %collective-permute-start.23 = (bf16[2,128,1024]{2,1,0:T(8,128)(2,1)S(1)}, bf16[2,128,1024]{2,1,0:T(8,128)(2,1)S(1)}, u32[]{:S(2)}, u32[]{:S(2)}) collective-permute-start(bf16[2,128,1024]{2,1,0:T(8,128)(2,1)S(1)} %get-tuple-element.240.refs_1_), channel_id=1, source_target_pairs={{8,0},{16,8},{24,16},{28,24},{20,28},{12,20},{4,12},{0,4},{9,1},{1... | collective-permute-start | bytes 1572872 | tf_op jit(solution)/shard_map/ppermute | solution.py:1617
  42.7 23.0 %collective-permute-start.22 = (bf16[2,128,1024]{2,1,0:T(8,128)(2,1)S(1)}, bf16[2,128,1024]{2,1,0:T(8,128)(2,1)S(1)}, u32[]{:S(2)}, u32[]{:S(2)}) collective-permute-start(bf16[2,128,1024]{2,1,0:T(8,128)(2,1)S(1)} %get-tuple-element.240.refs_1_), channel_id=1, source_target_pairs={{0,8},{8,16},{16,24},{24,28},{28,20},{20,12},{12,4},{4,0},{1,9},{9... | collective-permute-start | bytes 1572872 | tf_op jit(solution)/shard_map/ppermute | solution.py:1617
  65.7 18.6 %collective-permute-start.24 = (bf16[2,128,1024]{2,1,0:T(8,128)(2,1)S(1)}, bf16[2,128,1024]{2,1,0:T(8,128)(2,1)S(1)}, u32[]{:S(2)}, u32[]{:S(2)}) collective-permute-start(bf16[2,128,1024]{2,1,0:T(8,128)(2,1)S(1)} %collective-permute-done.22.refs_2_), channel_id=1, source_target_pairs={{0,8},{8,16},{16,24},{24,28},{28,20},{20,12},{12,4},{4,0},{1,9},{9... | collective-permute-start | bytes 1572872 | tf_op jit(solution)/shard_map/ppermute | solution.py:1617
  66.0 18.3 %collective-permute-start.25 = (bf16[2,128,1024]{2,1,0:T(8,128)(2,1)S(1)}, bf16[2,128,1024]{2,1,0:T(8,128)(2,1)S(1)}, u32[]{:S(2)}, u32[]{:S(2)}) collective-permute-start(bf16[2,128,1024]{2,1,0:T(8,128)(2,1)S(1)} %collective-permute-done.23.refs_3_), channel_id=1, source_target_pairs={{8,0},{16,8},{24,16},{28,24},{20,28},{12,20},{4,12},{0,4},{9,1},{1... | collective-permute-start | bytes 1572872 | tf_op jit(solution)/shard_map/ppermute | solution.py:1617
  84.3 14.3 %collective-permute-start.26 = (bf16[2,128,1024]{2,1,0:T(8,128)(2,1)S(1)}, bf16[2,128,1024]{2,1,0:T(8,128)(2,1)S(1)}, u32[]{:S(2)}, u32[]{:S(2)}) collective-permute-start(bf16[2,128,1024]{2,1,0:T(8,128)(2,1)S(1)} %collective-permute-done.24.refs_4_), channel_id=1, source_target_pairs={{0,8},{8,16},{16,24},{24,28},{28,20},{20,12},{12,4},{4,0},{1,9},{9... | collective-permute-start | bytes 1572872 | tf_op jit(solution)/shard_map/ppermute | solution.py:1617
  84.4 14.3 %collective-permute-start.27 = (bf16[2,128,1024]{2,1,0:T(8,128)(2,1)S(1)}, bf16[2,128,1024]{2,1,0:T(8,128)(2,1)S(1)}, u32[]{:S(2)}, u32[]{:S(2)}) collective-permute-start(bf16[2,128,1024]{2,1,0:T(8,128)(2,1)S(1)} %collective-permute-done.25.refs_5_), channel_id=1, source_target_pairs={{8,0},{16,8},{24,16},{28,24},{20,28},{12,20},{4,12},{0,4},{9,1},{1... | collective-permute-start | bytes 1572872 | tf_op jit(solution)/shard_map/ppermute | solution.py:1617
  88.0 13.2 %collective-permute-start.20 = (bf16[128,1024]{1,0:T(8,128)(2,1)S(1)}, bf16[128,1024]{1,0:T(8,128)(2,1)S(1)}, u32[]{:S(2)}, u32[]{:S(2)}) collective-permute-start(bf16[128,1024]{1,0:T(8,128)(2,1)S(1)} %get-tuple-element.238.refs_4_.refs_5_), channel_id=1, source_target_pairs={{0,2},{1,3},{2,0},{3,1},{4,6},{5,7},{6,4},{7,5},{8,10},{9,11},{10,... | collective-permute-start | bytes 786440 | tf_op jit(solution)/shard_map/ppermute | solution.py:23
  96.0 10.5 %collective-permute-start.17 = (bf16[128,1024]{1,0:T(8,128)(2,1)S(1)}, bf16[128,1024]{1,0:T(8,128)(2,1)S(1)}, u32[]{:S(2)}, u32[]{:S(2)}) collective-permute-start(bf16[128,1024]{1,0:T(8,128)(2,1)S(1)} %get-tuple-element.236.refs_0_.refs_1_), channel_id=1, source_target_pairs={{0,2},{1,3},{2,0},{3,1},{4,6},{5,7},{6,4},{7,5},{8,10},{9,11},{10,... | collective-permute-start | bytes 786440 | tf_op jit(solution)/shard_map/ppermute | solution.py:23
  126.1 41.9 %collective-permute-start.38 = (bf16[2,2,128,1024]{3,2,1,0:T(8,128)(2,1)S(1)}, bf16[2,2,128,1024]{3,2,1,0:T(8,128)(2,1)S(1)}, u32[]{:S(2)}, u32[]{:S(2)}) collective-permute-start(bf16[2,2,128,1024]{3,2,1,0:T(8,128)(2,1)S(1)} %get-tuple-element.275), channel_id=1, source_target_pairs={{0,8},{4,12},{8,0},{12,4},{16,24},{20,28},{24,16},{28,20},{1,9},{5... | collective-permute-start | bytes 3145736 | tf_op jit(solution)/shard_map/ppermute | solution.py:23
  126.4 41.7 %collective-permute-start.37 = (bf16[2,2,128,1024]{3,2,1,0:T(8,128)(2,1)S(1)}, bf16[2,2,128,1024]{3,2,1,0:T(8,128)(2,1)S(1)}, u32[]{:S(2)}, u32[]{:S(2)}) collective-permute-start(bf16[2,2,128,1024]{3,2,1,0:T(8,128)(2,1)S(1)} %get-tuple-element.259), channel_id=1, source_target_pairs={{0,4},{4,0},{8,12},{12,8},{16,20},{20,16},{24,28},{28,24},{1,5},{5... | collective-permute-start | bytes 3145736 | tf_op jit(solution)/shard_map/ppermute | solution.py:23
  155.2 23.3 %collective-permute-start.39 = (f32[256,128]{1,0:T(8,128)S(1)}, f32[256,128]{1,0:T(8,128)S(1)}, u32[]{:S(2)}, u32[]{:S(2)}) collective-permute-start(f32[256,128]{1,0:T(8,128)S(1)} %get-tuple-element.284), channel_id=1, source_target_pairs={{0,28},{4,0},{8,4},{12,8},{16,12},{20,16},{24,20},{28,24},{1,29},{... | collective-permute-start | bytes 393224 | tf_op jit(solution)/shard_map/ppermute | solution.py:1863
  170.8 12.4 %collective-permute-start.41 = (bf16[2,128,1024]{2,1,0:T(8,128)(2,1)}, bf16[2,128,1024]{2,1,0:T(8,128)(2,1)}, u32[]{:S(2)}, u32[]{:S(2)}) collective-permute-start(bf16[2,128,1024]{2,1,0:T(8,128)(2,1)} %get-tuple-element.289), channel_id=1, source_target_pairs={{0,4},{4,0},{8,12},{12,8},{16,20},{20,16},{24,28},{28,24},{1,5},{5... | collective-permute-start | bytes 1572872 | tf_op jit(solution)/shard_map/ppermute | solution.py:23
  171.5 11.6 %collective-permute-start.40 = (bf16[2,128,1024]{2,1,0:T(8,128)(2,1)}, bf16[2,128,1024]{2,1,0:T(8,128)(2,1)}, u32[]{:S(2)}, u32[]{:S(2)}) collective-permute-start(bf16[2,128,1024]{2,1,0:T(8,128)(2,1)} %get-tuple-element.278), channel_id=1, source_target_pairs={{0,8},{4,12},{8,0},{12,4},{16,24},{20,28},{24,16},{28,20},{1,9},{5... | collective-permute-start | bytes 1572872 | tf_op jit(solution)/shard_map/ppermute | solution.py:23
  179.1 12.3 %all-to-all-start.3 = ((bf16[8,32,512]{2,1,0:T(8,128)(2,1)}), bf16[8,32,512]{2,1,0:T(8,128)(2,1)}, u32[]{:S(2)}, u32[]{:S(2)}) async-start(bf16[8,32,512]{2,1,0:T(8,128)(2,1)} %copy-done.53), calls=%async_computation.3 | async-start | bytes 524288 | tf_op jit(solution)/shard_map/all_to_all | solution.py:1688
  208.2 9.2 %collective-permute-start.43 = (bf16[2,2,64,512]{3,2,1,0:T(8,128)(2,1)S(1)}, bf16[2,2,64,512]{3,2,1,0:T(8,128)(2,1)S(1)}, u32[]{:S(2)}, u32[]{:S(2)}) collective-permute-start(bf16[2,2,64,512]{3,2,1,0:T(8,128)(2,1)S(1)} %get-tuple-element.298), channel_id=1, source_target_pairs={{0,8},{4,12},{8,0},{12,4},{16,24},{20,28},{24,16},{28,20},{1,9},{5... | collective-permute-start | bytes 786440 | tf_op jit(solution)/shard_map/ppermute | solution.py:23
  208.2 9.6 %collective-permute-start.42 = (bf16[2,2,64,512]{3,2,1,0:T(8,128)(2,1)S(1)}, bf16[2,2,64,512]{3,2,1,0:T(8,128)(2,1)S(1)}, u32[]{:S(2)}, u32[]{:S(2)}) collective-permute-start(bf16[2,2,64,512]{3,2,1,0:T(8,128)(2,1)S(1)} %get-tuple-element.297), channel_id=1, source_target_pairs={{0,4},{4,0},{8,12},{12,8},{16,20},{20,16},{24,28},{28,24},{1,5},{5... | collective-permute-start | bytes 786440 | tf_op jit(solution)/shard_map/ppermute | solution.py:23
  208.9 16.1 %collective-permute-start.51 = (bf16[128,1024]{1,0:T(8,128)(2,1)S(1)}, bf16[128,1024]{1,0:T(8,128)(2,1)S(1)}, u32[]{:S(2)}, u32[]{:S(2)}) collective-permute-start(bf16[128,1024]{1,0:T(8,128)(2,1)S(1)} %get-tuple-element.327), channel_id=1, source_target_pairs={{0,1},{1,0},{2,3},{3,2},{4,5},{5,4},{6,7},{7,6},{8,9},{9,8},{10,11... | collective-permute-start | bytes 786440 | tf_op jit(solution)/shard_map/ppermute | solution.py:23
  211.2 15.0 %collective-permute-start.50 = (bf16[2,2,64,512]{3,2,1,0:T(8,128)(2,1)S(1)}, bf16[2,2,64,512]{3,2,1,0:T(8,128)(2,1)S(1)}, u32[]{:S(2)}, u32[]{:S(2)}) collective-permute-start(bf16[2,2,64,512]{3,2,1,0:T(8,128)(2,1)S(1)} %get-tuple-element.325), channel_id=1, source_target_pairs={{0,8},{4,12},{8,0},{12,4},{16,24},{20,28},{24,16},{28,20},{1,9},{5... | collective-permute-start | bytes 786440 | tf_op jit(solution)/shard_map/ppermute | solution.py:23
  212.3 15.7 %collective-permute-start.49 = (bf16[2,2,64,512]{3,2,1,0:T(8,128)(2,1)S(1)}, bf16[2,2,64,512]{3,2,1,0:T(8,128)(2,1)S(1)}, u32[]{:S(2)}, u32[]{:S(2)}) collective-permute-start(bf16[2,2,64,512]{3,2,1,0:T(8,128)(2,1)S(1)} %get-tuple-element.308), channel_id=1, source_target_pairs={{0,4},{4,0},{8,12},{12,8},{16,20},{20,16},{24,28},{28,24},{1,5},{5... | collective-permute-start | bytes 786440 | tf_op jit(solution)/shard_map/ppermute | solution.py:23
  217.3 11.1 %collective-permute-start.52 = (bf16[128,1024]{1,0:T(8,128)(2,1)S(1)}, bf16[128,1024]{1,0:T(8,128)(2,1)S(1)}, u32[]{:S(2)}, u32[]{:S(2)}) collective-permute-start(bf16[128,1024]{1,0:T(8,128)(2,1)S(1)} %add_far.6), channel_id=1, source_target_pairs={{0,2},{1,3},{2,0},{3,1},{4,6},{5,7},{6,4},{7,5},{8,10},{9,11},{10,... | collective-permute-start | bytes 786440 | tf_op jit(solution)/shard_map/ppermute | solution.py:23
  225.0 21.3 %collective-permute-start.57 = (bf16[128,1024]{1,0:T(8,128)(2,1)S(1)}, bf16[128,1024]{1,0:T(8,128)(2,1)S(1)}, u32[]{:S(2)}, u32[]{:S(2)}) collective-permute-start(bf16[128,1024]{1,0:T(8,128)(2,1)S(1)} %get-tuple-element.339), channel_id=1, source_target_pairs={{0,16},{4,20},{8,24},{12,28},{16,0},{20,4},{24,8},{28,12},{1,17},{... | collective-permute-start | bytes 786440 | tf_op jit(solution)/shard_map/ppermute | solution.py:23
  226.2 25.3 %collective-permute-start.56 = (bf16[128,1024]{1,0:T(8,128)(2,1)S(1)}, bf16[128,1024]{1,0:T(8,128)(2,1)S(1)}, u32[]{:S(2)}, u32[]{:S(2)}) collective-permute-start(bf16[128,1024]{1,0:T(8,128)(2,1)S(1)} %get-tuple-element.292), channel_id=1, source_target_pairs={{0,16},{4,20},{8,24},{12,28},{16,0},{20,4},{24,8},{28,12},{1,17},{... | collective-permute-start | bytes 786440 | tf_op jit(solution)/shard_map/ppermute | solution.py:23
  228.4 23.1 %collective-permute-start.59 = (bf16[2,64,512]{2,1,0:T(8,128)(2,1)S(1)}, bf16[2,64,512]{2,1,0:T(8,128)(2,1)S(1)}, u32[]{:S(2)}, u32[]{:S(2)}) collective-permute-start(bf16[2,64,512]{2,1,0:T(8,128)(2,1)S(1)} %get-tuple-element.342), channel_id=1, source_target_pairs={{0,4},{4,0},{8,12},{12,8},{16,20},{20,16},{24,28},{28,24},{1,5},{5... | collective-permute-start | bytes 393224 | tf_op jit(solution)/shard_map/ppermute | solution.py:23
  230.0 23.0 %collective-permute-start.58 = (bf16[2,64,512]{2,1,0:T(8,128)(2,1)S(1)}, bf16[2,64,512]{2,1,0:T(8,128)(2,1)S(1)}, u32[]{:S(2)}, u32[]{:S(2)}) collective-permute-start(bf16[2,64,512]{2,1,0:T(8,128)(2,1)S(1)} %get-tuple-element.311), channel_id=1, source_target_pairs={{0,8},{4,12},{8,0},{12,4},{16,24},{20,28},{24,16},{28,20},{1,9},{5... | collective-permute-start | bytes 393224 | tf_op jit(solution)/shard_map/ppermute | solution.py:23
  235.5 21.7 %collective-permute-start.53 = (f32[176,256]{1,0:T(8,128)S(1)}, f32[176,256]{1,0:T(8,128)S(1)}, u32[]{:S(2)}, u32[]{:S(2)}) collective-permute-start(f32[176,256]{1,0:T(8,128)S(1)} %add_small.3.refs_0_), channel_id=1, source_target_pairs={{0,8},{4,12},{8,0},{12,4},{16,24},{20,28},{24,16},{28,20},{1,9},{5... | collective-permute-start | bytes 540680 | tf_op jit(solution)/shard_map/ppermute | solution.py:23
  251.5 9.4 %collective-permute-start.47 = (bf16[128,1024]{1,0:T(8,128)(2,1)S(1)}, bf16[128,1024]{1,0:T(8,128)(2,1)S(1)}, u32[]{:S(2)}, u32[]{:S(2)}) collective-permute-start(bf16[128,1024]{1,0:T(8,128)(2,1)S(1)} %add_far.7), channel_id=1, source_target_pairs={{0,2},{1,3},{2,0},{3,1},{4,6},{5,7},{6,4},{7,5},{8,10},{9,11},{10,... | collective-permute-start | bytes 786440 | tf_op jit(solution)/shard_map/ppermute | solution.py:23
  257.2 16.3 %collective-permute-start.62 = (f32[176,256]{1,0:T(8,128)S(1)}, f32[176,256]{1,0:T(8,128)S(1)}, u32[]{:S(2)}, u32[]{:S(2)}) collective-permute-start(f32[176,256]{1,0:T(8,128)S(1)} %add_small.4.refs_0_), channel_id=1, source_target_pairs={{0,16},{4,20},{8,24},{12,28},{16,0},{20,4},{24,8},{28,12},{1,17},{... | collective-permute-start | bytes 540680 | tf_op jit(solution)/shard_map/ppermute | solution.py:23
  257.9 14.2 %collective-permute-start.64 = (bf16[64,512]{1,0:T(8,128)(2,1)S(1)}, bf16[64,512]{1,0:T(8,128)(2,1)S(1)}, u32[]{:S(2)}, u32[]{:S(2)}) collective-permute-start(bf16[64,512]{1,0:T(8,128)(2,1)S(1)} %get-tuple-element.359), channel_id=1, source_target_pairs={{0,16},{4,20},{8,24},{12,28},{16,0},{20,4},{24,8},{28,12},{1,17},{... | collective-permute-start | bytes 196616 | tf_op jit(solution)/shard_map/ppermute | solution.py:23
  260.2 12.7 %collective-permute-start.63 = (bf16[64,512]{1,0:T(8,128)(2,1)S(1)}, bf16[64,512]{1,0:T(8,128)(2,1)S(1)}, u32[]{:S(2)}, u32[]{:S(2)}) collective-permute-start(bf16[64,512]{1,0:T(8,128)(2,1)S(1)} %get-tuple-element.345), channel_id=1, source_target_pairs={{0,16},{4,20},{8,24},{12,28},{16,0},{20,4},{24,8},{28,12},{1,17},{... | collective-permute-start | bytes 196616 | tf_op jit(solution)/shard_map/ppermute | solution.py:23
  (142 other events, 1285.5 us)
